TPU v7x, 256 devices: a whole 4x4x8 slice. The times are simulated.
256 devices in a mesh: dp: 2 (over core), expert: 16 (over x, y), tensor: 8 (over z).
Axes of the slice: x: 4, y: 4, z: 8, core: 2. Of those that a mesh axis runs over, the one named last changes fastest.
Arguments:
- tokens: bfloat16 [32768, 1536], P(('dp', 'expert', 'tensor')), may hold values from -6 to 6
- segments: int32 [32, 1024], P(('dp', 'expert')), may hold values from 0 to 18, as said below
- routes: int32 [32768, 8], P(('dp', 'expert', 'tensor')), may hold values from 0 to 31, all different within a row; in each aligned block of 128 rows (0 to 127, 128 to 255, ...) at most 64 rows name the same one
- norm1_gain: float32 [1536], replicated, may hold values from 0.1 to 1.9
- w_query: bfloat16 [1536, 1536], P(None, 'tensor'), may hold values from -0.21875 to 0.21875
- w_key: bfloat16 [1536, 512], P(None, 'tensor'), may hold values from -0.15625 to 0.15625
- w_value: bfloat16 [1536, 512], P(None, 'tensor'), may hold values from -0.15625 to 0.15625
- w_out: bfloat16 [1536, 1536], P('tensor'), may hold values from -0.75 to 0.75
- norm2_gain: float32 [1536], replicated, may hold values from 0.1 to 1.9
- w_router: bfloat16 [1536, 32], replicated, may hold values from -0.078125 to 0.078125
- w_gate: bfloat16 [32, 1536, 512], P('expert', ('dp', 'tensor')), may hold values from -0.15625 to 0.15625
- w_up: bfloat16 [32, 1536, 512], P('expert', ('dp', 'tensor')), may hold values from -0.15625 to 0.15625
- w_down: bfloat16 [32, 512, 1536], P('expert', ('dp', 'tensor')), may hold values from -1 to 1
- cotangent: bfloat16 [32768, 1536], P(('dp', 'expert', 'tensor')), may hold values from -6 to 6
Outputs:
- output: bfloat16 [32768, 1536], P(('dp', 'expert', 'tensor'))
- input_grad: float32 [32768, 1536], P(('dp', 'expert', 'tensor'))
- norm1_gain_grad: float32 [1536], replicated
- w_query_grad: float32 [1536, 1536], P(None, 'tensor')
- w_key_grad: float32 [1536, 512], P(None, 'tensor')
- w_value_grad: float32 [1536, 512], P(None, 'tensor')
- w_out_grad: float32 [1536, 1536], P('tensor')
- norm2_gain_grad: float32 [1536], replicated
- w_router_grad: float32 [1536, 32], replicated
- w_gate_grad: float32 [32, 1536, 512], P('expert', ('dp', 'tensor'))
- w_up_grad: float32 [32, 1536, 512], P('expert', ('dp', 'tensor'))
- w_down_grad: float32 [32, 512, 1536], P('expert', ('dp', 'tensor'))
Inputs may be any that keep to these rules, and one draw needn't show every extreme that they name: `segments`: along a sequence the numbers never fall; 0 marks trailing padding and nothing else, and every sequence ends in at least one padding position; documents are numbered 1, 2, ... in order. Every document but the last of a sequence has 60 to 800 positions; the last may be cut shorter by the padding. In every draw some sequence reaches the largest document number. `routes`: each row names 8 different experts. Within the rows of one device no expert is named by more than 64 rows, and in every draw some device names some expert exactly 64 times.
All inputs are finite; a program needn't handle non-finite values.
Results may differ from a plain program's by a relative error of at most 0.023.
Values may be sent and summed in bfloat16 or wider, within the bound.
No kernel may reach another device: no remote copies, remote signals or barrier semaphores. Data moves between devices by JAX's collectives and lax.ppermute only.
A program may use at most 192 MiB of HBM per device.

v0:
```python
import jax
import jax.numpy as jnp
from jax import lax
from jax.sharding import PartitionSpec as P

HEAD_DIM = 64
TOP = 8


epsilon_norm = 1e-06
rope_theta = 10000.0
masked_score = -1e30
block_limit = 512


def rms_forward(values, norm_gain):
    inverse = lax.rsqrt(jnp.mean(values * values, axis=-1, keepdims=True) + epsilon_norm)
    return (values * inverse * norm_gain, inverse)


def rms_backward(values, inverse, norm_gain, grad_out):
    scaled = grad_out * norm_gain
    grad_in = inverse * scaled - values * (inverse * inverse * inverse) * jnp.mean(
        scaled * values, axis=-1, keepdims=True
    )
    return (grad_in, jnp.sum(grad_out * values * inverse, axis=0))


def rope_tables(seq_len, head_width):
    half_dim = head_width // 2
    frequency = rope_theta ** (-2.0 * jnp.arange(half_dim, dtype=jnp.float32) / head_width)
    angles = jnp.arange(seq_len, dtype=jnp.float32)[:, None] * frequency[None, :]
    angles = jnp.concatenate([angles, angles], axis=1)
    return (jnp.cos(angles), jnp.sin(angles))


def rotate_half(values):
    half_dim = values.shape[-1] // 2
    return jnp.concatenate([-values[..., half_dim:], values[..., :half_dim]], axis=-1)


def rotate_back(values):
    half_dim = values.shape[-1] // 2
    return jnp.concatenate([values[..., half_dim:], -values[..., :half_dim]], axis=-1)


def apply_rope(values, cosine_table, sine_table):
    return values * cosine_table + rotate_half(values) * sine_table


def undo_rope(grads_in, cosine_table, sine_table):
    return grads_in * cosine_table + rotate_back(grads_in * sine_table)


def allowed_mask(query_pos, query_seg, key_pos, key_seg):
    same_doc = query_seg[:, None] == key_seg[None, :]
    causal = key_pos[None, :] <= query_pos[:, None]
    diagonal = key_pos[None, :] == query_pos[:, None]
    return causal & same_doc & ((query_seg[:, None] != 0) | diagonal)


def local(
    tokens,
    segments,
    routes,
    norm1_gain,
    w_query,
    w_key,
    w_value,
    w_out,
    norm2_gain,
    w_router,
    w_gate,
    w_up,
    w_down,
    cotangent,
):
    tok_rows, model_width = tokens.shape
    seq_len = segments.shape[1]
    query_width = w_query.shape[1]
    kv_width = w_key.shape[1]
    query_heads = query_width // HEAD_DIM
    kv_count = kv_width // HEAD_DIM
    group_size = query_heads // kv_count
    local_experts = w_gate.shape[0]
    expert_count = w_router.shape[1]
    owner_count = lax.axis_size("expert")
    capacity = min(tok_rows, max(4, 8 * (tok_rows * TOP // (4 * expert_count))))
    pair_count = tok_rows * TOP
    score_scale = HEAD_DIM ** (-0.5)
    block_rows = min(block_limit, seq_len)
    block_count = seq_len // block_rows
    token_f32 = tokens.astype(jnp.float32)
    normed_one, inverse_one = rms_forward(token_f32, norm1_gain)
    normed_low = normed_one.astype(jnp.bfloat16)
    joined_weights = jnp.concatenate([w_query, w_key, w_value], axis=1)
    joined = jnp.dot(
        lax.all_gather(normed_low, "tensor", axis=0, tiled=True),
        joined_weights,
        preferred_element_type=jnp.float32,
    )
    cosine_table, sine_table = rope_tables(seq_len, HEAD_DIM)
    query_raw = joined[:, :query_width].reshape(seq_len, kv_count, group_size, HEAD_DIM)
    key_raw = joined[:, query_width : query_width + kv_width].reshape(seq_len, kv_count, HEAD_DIM)
    value_raw = joined[:, query_width + kv_width :].reshape(seq_len, kv_count, HEAD_DIM)
    query_low = apply_rope(
        query_raw, cosine_table[:, None, None, :], sine_table[:, None, None, :]
    ).astype(jnp.bfloat16)
    key_low = apply_rope(key_raw, cosine_table[:, None, :], sine_table[:, None, :]).astype(
        jnp.bfloat16
    )
    value_low = value_raw.astype(jnp.bfloat16)
    key_pos = jnp.arange(seq_len, dtype=jnp.int32)
    key_seg = segments[0]
    query_blocks = query_low.reshape(block_count, block_rows, kv_count, group_size, HEAD_DIM)
    pos_blocks = key_pos.reshape(block_count, block_rows)
    seg_blocks = key_seg.reshape(block_count, block_rows)

    def block_scores(query_block, query_pos, query_seg):
        scores = (
            jnp.einsum("qgrd,kgd->grqk", query_block, key_low, preferred_element_type=jnp.float32)
            * score_scale
        )
        return jnp.where(allowed_mask(query_pos, query_seg, key_pos, key_seg), scores, masked_score)

    def attend_block(block_in):
        query_block, query_pos, query_seg = block_in
        masked = block_scores(query_block, query_pos, query_seg)
        top_score = jnp.max(masked, axis=-1, keepdims=True)
        exp_scores = jnp.exp(masked - top_score)
        exp_total = jnp.sum(exp_scores, axis=-1, keepdims=True)
        attn_probs = (exp_scores / exp_total).astype(jnp.bfloat16)
        context = jnp.einsum(
            "grqk,kgd->qgrd", attn_probs, value_low, preferred_element_type=jnp.float32
        )
        return (context, (top_score + jnp.log(exp_total))[..., 0])

    context_blocks, lse_blocks = lax.map(attend_block, (query_blocks, pos_blocks, seg_blocks))
    context_low = context_blocks.reshape(seq_len, query_width).astype(jnp.bfloat16)
    picked = context_low
    attention = lax.psum_scatter(
        jnp.dot(picked, w_out, preferred_element_type=jnp.float32),
        "tensor",
        scatter_dimension=0,
        tiled=True,
    )
    residual_mid = token_f32 + attention
    normed_two, inverse_two = rms_forward(residual_mid, norm2_gain)
    normed_two_low = normed_two.astype(jnp.bfloat16)
    logits = jnp.dot(normed_two_low, w_router, preferred_element_type=jnp.float32)
    expert_ids = jnp.arange(expert_count, dtype=jnp.int32)
    onehot = (routes[:, :, None] == expert_ids[None, None, :]).astype(jnp.float32)
    chosen = jnp.sum(onehot * logits[:, None, :], axis=2)
    chosen_exp = jnp.exp(chosen - jnp.max(chosen, axis=1, keepdims=True))
    gate_probs = chosen_exp / jnp.sum(chosen_exp, axis=1, keepdims=True)
    flat_routes = routes.reshape(pair_count)
    pair_hot = (flat_routes[:, None] == expert_ids[None, :]).astype(jnp.int32)
    pair_rank = jnp.sum(pair_hot * (jnp.cumsum(pair_hot, axis=0) - 1), axis=1)
    pair_slot = flat_routes * capacity + pair_rank
    slot_pair = (
        jnp.full((expert_count * capacity,), pair_count, jnp.int32)
        .at[pair_slot]
        .set(jnp.arange(pair_count, dtype=jnp.int32))
    )
    row_pad = jnp.zeros((1, model_width), jnp.bfloat16)
    send_rows = jnp.concatenate([normed_two_low, row_pad], axis=0)[slot_pair // TOP]
    send_rows = send_rows.reshape(owner_count, local_experts, capacity, model_width)
    full_gate, full_up, full_down = (
        lax.all_gather(w_gate, ("dp", "tensor"), axis=1, tiled=True),
        lax.all_gather(w_up, ("dp", "tensor"), axis=1, tiled=True),
        lax.all_gather(w_down, ("dp", "tensor"), axis=1, tiled=True),
    )

    def expert_apply(arrived):
        gate_pre = jnp.einsum(
            "sxcd,xdf->sxcf", arrived, full_gate, preferred_element_type=jnp.float32
        )
        up_pre = jnp.einsum("sxcd,xdf->sxcf", arrived, full_up, preferred_element_type=jnp.float32)
        gate_sig = jax.nn.sigmoid(gate_pre)
        hidden = (gate_pre * gate_sig * up_pre).astype(jnp.bfloat16)
        return (gate_pre, up_pre, gate_sig, hidden)

    arrived = lax.all_to_all(send_rows, "expert", split_axis=0, concat_axis=0, tiled=True)
    gate_pre, up_pre, gate_sig, hidden = expert_apply(arrived)
    result = jnp.einsum(
        "sxcf,xfd->sxcd", hidden, full_down, preferred_element_type=jnp.float32
    ).astype(jnp.bfloat16)
    returned = lax.all_to_all(result, "expert", split_axis=0, concat_axis=0, tiled=True)
    returned, kept_rows = (returned, arrived)
    returned_flat = returned.reshape(expert_count * capacity, model_width)
    pair_results = returned_flat[pair_slot].reshape(tok_rows, TOP, model_width)
    mixture = jnp.sum(gate_probs[:, :, None] * pair_results, axis=1)
    output = (residual_mid + mixture).astype(jnp.bfloat16)
    cot_f32 = cotangent.astype(jnp.float32)
    gate_grad = jnp.einsum(
        "tkd,td->tk", pair_results, cotangent, preferred_element_type=jnp.float32
    )
    chosen_grad = gate_probs * (gate_grad - jnp.sum(gate_probs * gate_grad, axis=1, keepdims=True))
    logit_grad = jnp.sum(onehot * chosen_grad[:, :, None], axis=1).astype(jnp.bfloat16)
    router_grad = jnp.einsum(
        "td,te->de", normed_two_low, logit_grad, preferred_element_type=jnp.float32
    )
    normed_two_grad = jnp.einsum(
        "te,de->td", logit_grad, w_router, preferred_element_type=jnp.float32
    )
    pair_grads = (
        (gate_probs[:, :, None] * cot_f32[:, None, :])
        .astype(jnp.bfloat16)
        .reshape(pair_count, model_width)
    )
    send_grads = jnp.concatenate([pair_grads, row_pad], axis=0)[slot_pair]
    send_grads = send_grads.reshape(owner_count, local_experts, capacity, model_width)
    grads_in = lax.all_to_all(send_grads, "expert", split_axis=0, concat_axis=0, tiled=True)
    rows_in = lax.all_to_all(send_rows, "expert", split_axis=0, concat_axis=0, tiled=True)
    gate_pre, up_pre, gate_sig, hidden = expert_apply(rows_in)
    hidden_grad = jnp.einsum(
        "sxcd,xfd->sxcf", grads_in, full_down, preferred_element_type=jnp.float32
    )
    gate_pre_grad = (
        hidden_grad * up_pre * (gate_sig + gate_pre * gate_sig * (1.0 - gate_sig))
    ).astype(jnp.bfloat16)
    up_pre_grad = (hidden_grad * gate_pre * gate_sig).astype(jnp.bfloat16)
    row_grads = jnp.einsum(
        "sxcf,xdf->sxcd", gate_pre_grad, full_gate, preferred_element_type=jnp.float32
    )
    row_grads = row_grads + jnp.einsum(
        "sxcf,xdf->sxcd", up_pre_grad, full_up, preferred_element_type=jnp.float32
    )
    row_grads, gate_pre_grad, up_pre_grad, hidden, rows_in, grads_in = (
        row_grads.astype(jnp.bfloat16),
        gate_pre_grad,
        up_pre_grad,
        hidden,
        rows_in,
        grads_in,
    )
    gate_w_part = jnp.einsum(
        "sxcd,sxcf->xdf", rows_in, gate_pre_grad, preferred_element_type=jnp.float32
    )
    up_w_part = jnp.einsum(
        "sxcd,sxcf->xdf", rows_in, up_pre_grad, preferred_element_type=jnp.float32
    )
    down_w_part = jnp.einsum("sxcf,sxcd->xfd", hidden, grads_in, preferred_element_type=jnp.float32)
    w_gate_grad, w_up_grad, w_down_grad = (
        lax.psum_scatter(
            gate_w_part.astype(jnp.bfloat16), ("dp", "tensor"), scatter_dimension=1, tiled=True
        ).astype(jnp.float32),
        lax.psum_scatter(
            up_w_part.astype(jnp.bfloat16), ("dp", "tensor"), scatter_dimension=1, tiled=True
        ).astype(jnp.float32),
        lax.psum_scatter(
            down_w_part.astype(jnp.bfloat16), ("dp", "tensor"), scatter_dimension=1, tiled=True
        ).astype(jnp.float32),
    )
    back_rows = lax.all_to_all(row_grads, "expert", split_axis=0, concat_axis=0, tiled=True)
    pair_back = back_rows.reshape(expert_count * capacity, model_width)[pair_slot].reshape(
        tok_rows, TOP, model_width
    )
    normed_two_grad = normed_two_grad + jnp.sum(pair_back, axis=1, dtype=jnp.float32)
    mid_part, norm2_gain_part = rms_backward(residual_mid, inverse_two, norm2_gain, normed_two_grad)
    mid_grad = cot_f32 + mid_part
    attention_low = mid_grad.astype(jnp.bfloat16)
    shard_rows = lax.all_gather(attention_low, "tensor", axis=0, tiled=True)
    picked = context_low
    out_grad = jnp.einsum("tq,td->qd", picked, shard_rows, preferred_element_type=jnp.float32)
    grad_rows = jnp.einsum(
        "td,qd->tq", shard_rows, w_out, preferred_element_type=jnp.float32
    ).astype(jnp.bfloat16)
    context_grad = grad_rows
    context_grad_blocks = context_grad.reshape(
        block_count, block_rows, kv_count, group_size, HEAD_DIM
    )

    def attend_back(running, block_in):
        key_grad, value_grad = running
        query_block, grad_block, lse_block, query_pos, query_seg = block_in
        masked = block_scores(query_block, query_pos, query_seg)
        attn_probs = jnp.exp(masked - lse_block[..., None])
        probs_grad = jnp.einsum(
            "qgrd,kgd->grqk", grad_block, value_low, preferred_element_type=jnp.float32
        )
        row_dot = jnp.sum(attn_probs * probs_grad, axis=-1, keepdims=True)
        score_grad = (attn_probs * (probs_grad - row_dot)).astype(jnp.bfloat16)
        query_grad = (
            jnp.einsum("grqk,kgd->qgrd", score_grad, key_low, preferred_element_type=jnp.float32)
            * score_scale
        )
        key_grad = (
            key_grad
            + jnp.einsum(
                "grqk,qgrd->kgd", score_grad, query_block, preferred_element_type=jnp.float32
            )
            * score_scale
        )
        value_grad = value_grad + jnp.einsum(
            "grqk,qgrd->kgd",
            attn_probs.astype(jnp.bfloat16),
            grad_block,
            preferred_element_type=jnp.float32,
        )
        return ((key_grad, value_grad), query_grad)

    zero_kv = jnp.zeros((seq_len, kv_count, HEAD_DIM), jnp.float32)
    (key_grad, value_grad), query_grad = lax.scan(
        attend_back,
        (zero_kv, zero_kv),
        (query_blocks, context_grad_blocks, lse_blocks, pos_blocks, seg_blocks),
    )
    query_grad = undo_rope(
        query_grad.reshape(seq_len, kv_count, group_size, HEAD_DIM),
        cosine_table[:, None, None, :],
        sine_table[:, None, None, :],
    )
    key_grad = undo_rope(key_grad, cosine_table[:, None, :], sine_table[:, None, :])
    joined_grad = jnp.concatenate(
        [
            query_grad.reshape(seq_len, query_width),
            key_grad.reshape(seq_len, kv_width),
            value_grad.reshape(seq_len, kv_width),
        ],
        axis=1,
    ).astype(jnp.bfloat16)
    grad_rows = joined_grad
    joined_w_part = jnp.einsum(
        "td,tq->dq",
        lax.all_gather(normed_low, "tensor", axis=0, tiled=True),
        grad_rows,
        preferred_element_type=jnp.float32,
    )
    grad_rows = joined_grad
    normed_one_grad = lax.psum_scatter(
        jnp.einsum(
            "tq,dq->td", grad_rows, joined_weights, preferred_element_type=jnp.float32
        ).astype(jnp.bfloat16),
        "tensor",
        scatter_dimension=0,
        tiled=True,
    ).astype(jnp.float32)
    input_part, norm1_gain_part = rms_backward(token_f32, inverse_one, norm1_gain, normed_one_grad)
    input_grad = mid_grad + input_part
    attn_sums = (
        lax.psum(joined_w_part[:, :query_width].astype(jnp.bfloat16), ("dp", "expert")).astype(
            jnp.float32
        ),
        lax.psum(
            joined_w_part[:, query_width : query_width + kv_width].astype(jnp.bfloat16),
            ("dp", "expert"),
        ).astype(jnp.float32),
        lax.psum(
            joined_w_part[:, query_width + kv_width :].astype(jnp.bfloat16), ("dp", "expert")
        ).astype(jnp.float32),
        lax.psum(out_grad.astype(jnp.bfloat16), ("dp", "expert")).astype(jnp.float32),
    )
    shared_sums = lax.psum(
        (norm1_gain_part, norm2_gain_part, router_grad), ("dp", "expert", "tensor")
    )
    return (
        output,
        input_grad,
        shared_sums[0],
        attn_sums[0],
        attn_sums[1],
        attn_sums[2],
        attn_sums[3],
        shared_sums[1],
        shared_sums[2],
        w_gate_grad,
        w_up_grad,
        w_down_grad,
    )


def solution(mesh):
    placed = (
        P(("dp", "expert", "tensor"), None),
        P(("dp", "expert"), None),
        P(("dp", "expert", "tensor"), None),
        P(),
        P(None, "tensor"),
        P(None, "tensor"),
        P(None, "tensor"),
        P("tensor", None),
        P(),
        P(),
        P("expert", ("dp", "tensor"), None),
        P("expert", ("dp", "tensor"), None),
        P("expert", ("dp", "tensor"), None),
        P(("dp", "expert", "tensor"), None),
    )
    return jax.shard_map(
        local,
        mesh=mesh,
        in_specs=placed,
        out_specs=(
            P(("dp", "expert", "tensor"), None),
            P(("dp", "expert", "tensor"), None),
            P(),
            P(None, "tensor"),
            P(None, "tensor"),
            P(None, "tensor"),
            P("tensor", None),
            P(),
            P(),
            P("expert", ("dp", "tensor"), None),
            P("expert", ("dp", "tensor"), None),
            P("expert", ("dp", "tensor"), None),
        ),
        check_vma=False,
    )
```

profile of v0, /device:TPU:1, one launch (start us, length us, event | category | flops | bytes accessed | tf_op | source)
XLA Modules:
  0.0 1174.5 jit_solution(15634468208141323851)
XLA Ops:
  21.7 39.4 %all-gather.6.cloned.1.call-done = bf16[1024,1536]{1,0:T(8,128)(2,1)} async-done(((bf16[128,1536]{1,0:T(8,128)(2,1)}), bf16[1024,1536]{1,0:T(8,128)(2,1)}) %all-gather.6.cloned.1.call-update) | async-done | bytes 3145744 | tf_op jit(solution)/shard_map/all_gather | solution.py:98
  71.7 14.0 %while.30 = (s32[]{:T(128)}, bf16[2,512,1,3,64]{1,4,3,2,0:T(8,128)(2,1)}, f32[2,1,3,512]{3,2,1,0:T(4,128)S(1)}, s32[2,512]{1,0:T(2,128)S(1)}, s32[2,512]{1,0:T(2...) while((s32[]{:T(128)}, ...), condition=%wide.region_4.5_spmd.clone.clone, body=%wide.region_1.4_spmd.clone.clone.sunk | while | flops 424672256 | bytes 25048244 | solution.py:138
  93.7 9.0 reduce-window.6
  107.5 71.8 %reduce-scatter.6.cloned.1.call-done = f32[128,1536]{1,0:T(8,128)} async-done(((f32[1024,1536]{1,0:T(8,128)}), f32[128,1536]{1,0:T(8,128)}) %reduce-scatter.6.cloned.1.call-update) | async-done | bytes 786448 | tf_op jit(solution)/shard_map/reduce_scatter | solution.py:141
  180.9 10.1 gather_fusion
  191.0 6.5 all-to-all-start
  198.1 97.8 %all-to-all-done = bf16[16,2,64,1536]{3,2,1,0:T(8,128)(2,1)} async-done(((bf16[16,2,64,1536]{3,2,1,0:T(8,128)(2,1)}), bf16[16,2,64,1536]{3,2,1,0:T(8,128)(2,1)}, u32[]{:S(2)}, u32[]{:S(2)}) %all-to-all-start) | async-done | bytes 6291488 | tf_op jit(solution)/shard_map/all_to_all | solution.py:183
  295.9 9.1 fusion.76
  305.0 11.3 fusion.82
  316.3 5.9 convert_bitcast_fusion
  325.6 10.3 all-to-all-start.1
  336.4 74.1 %all-to-all-done.1 = bf16[16,2,64,1536]{3,2,1,0:T(8,128)(2,1)} async-done(((bf16[16,2,64,1536]{3,2,1,0:T(8,128)(2,1)}), bf16[16,2,64,1536]{3,2,1,0:T(8,128)(2,1)}, u32[]{:S(2)}, u32[]{:S(2)}) %all-to-all-start.1) | async-done | bytes 6291488 | tf_op jit(solution)/shard_map/all_to_all | solution.py:188
  410.4 10.9 gather_fusion.1
  427.6 15.6 %gather_fusion.2 = bf16[2048,1536]{1,0:T(8,128)(2,1)} fusion(bf16[1025,1536]{1,0:T(8,128)(2,1)} %concatenate.92, s32[2048]{0:T(1024)S(1)} %get-tuple-element.419), kind=kCustom, calls=%fused_computation.2 | custom fusion | bytes 12591104 | tf_op jit(solution)/shard_map/gather | solution.py:211
  443.2 76.6 %all_to_all.21 = bf16[16,2,64,1536]{3,2,1,0:T(8,128)(2,1)S(1)} all-to-all(bf16[16,2,64,1536]{3,2,1,0:T(8,128)(2,1)} %bitcast.421), channel_id=1, replica_groups=mesh['dp'=2,'expert'=16,'tensor'=8] {'expert'}, dimensions={0} | all-to-all | bytes 12582912 | tf_op jit(solution)/shard_map/all_to_all | solution.py:213
  519.8 11.5 fusion.81
  531.4 10.5 fusion.90
  541.8 9.6 fusion.68
  564.9 70.3 %all-to-all-done.3 = bf16[16,2,64,1536]{3,2,1,0:T(8,128)(2,1)} async-done(((bf16[16,2,64,1536]{3,2,1,0:T(8,128)(2,1)}), bf16[16,2,64,1536]{3,2,1,0:T(8,128)(2,1)}, u32[]{:S(2)}, u32[]{:S(2)}) %all-to-all-start.3) | async-done | bytes 6291488 | tf_op jit(solution)/shard_map/all_to_all | solution.py:255
  635.2 10.9 gather_fusion.3
  652.0 8.6 bitcast_convert_fusion
  660.9 8.5 bitcast_convert_fusion.1
  669.5 8.5 bitcast_convert_fusion.2
  678.2 53.9 %all-gather.14.cloned.1.call-done = bf16[1024,1536]{1,0:T(8,128)(2,1)} async-done(((bf16[128,1536]{1,0:T(8,128)(2,1)}), bf16[1024,1536]{1,0:T(8,128)(2,1)}) %all-gather.14.cloned.1.call-update) | async-done | bytes 3145744 | tf_op jit(solution)/shard_map/all_gather | solution.py:263
  735.5 38.9 %while.31 = (s32[]{:T(128)}, f32[1024,1,64]{0,2,1:T(8,128)S(1)}, f32[1024,1,64]{0,2,1:T(8,128)}, f32[2,512,1,3,64]{1,0,4,3,2:T(2,128)}, bf16[2,512,1,3,64]{1,4,3...) while((s32[]{:T(128)}, f32[1024,1,64]{0,2,1:T(8,128)S(1)}, ...), condition=%wide.region_21.22_spmd.clone.clone, body=%wide.region_19.21_spmd.clone.clone.sunk | while | flops 1033796608 | bytes 53544112 | solution.py:304
  746.6 8.1 dynamic_update_slice.24
  766.4 8.1 dynamic_update_slice.24
  793.4 45.6 %reduce-scatter.12.cloned.1.call-done = bf16[2,96,512]{2,1,0:T(8,128)(2,1)} async-done(((bf16[2,1536,512]{2,1,0:T(8,128)(2,1)}), bf16[2,96,512]{2,1,0:T(8,128)(2,1)}) %reduce-scatter.12.cloned.1.call-update) | async-done | bytes 196624 | tf_op jit(solution)/shard_map/reduce_scatter | solution.py:248
  840.7 69.9 %reduce-scatter.10.cloned.1.call-done = bf16[2,96,512]{2,1,0:T(8,128)(2,1)} async-done(((bf16[2,1536,512]{2,1,0:T(8,128)(2,1)}), bf16[2,96,512]{2,1,0:T(8,128)(2,1)}) %reduce-scatter.10.cloned.1.call-update) | async-done | bytes 196624 | tf_op jit(solution)/shard_map/reduce_scatter | solution.py:245
  920.2 37.4 %reduce-scatter.8.cloned.1.call-done = bf16[128,1536]{1,0:T(8,128)(2,1)} async-done(((bf16[1024,1536]{1,0:T(8,128)(2,1)}), bf16[128,1536]{1,0:T(8,128)(2,1)}) %reduce-scatter.8.cloned.1.call-update) | async-done | bytes 393232 | tf_op jit(solution)/shard_map/reduce_scatter | solution.py:331
  961.1 77.1 %all-reduce.2 = (f32[1536]{0:T(1024)}, f32[1536]{0:T(1024)}) all-reduce(f32[1536]{0:T(1024)S(1)} %get-tuple-element.337, f32[1536]{0:T(1024)S(1)} %get-tuple-element.335), channel_id=1, replica_groups=mesh['dp'=2,'expert'=16,'tensor'=8] {'dp','expert','tensor'}, use_global_device_ids=true, to_apply=%region_25.26 | all-reduce | flops 3072 | bytes 24576 | tf_op jit(solution)/shard_map/psum | solution.py:354
  1038.2 127.1 %all-reduce.7.cloned.1.call-done = f32[1536,32]{0,1:T(8,128)} async-done(((f32[1536,32]{0,1:T(8,128)}), f32[1536,32]{0,1:T(8,128)}) %all-reduce.7.cloned.1.call-update) | async-done | bytes 196624 | tf_op jit(solution)/shard_map/psum | solution.py:354
  (258 shorter events, 143.4 us)
Async XLA Ops:
  8.0 80.2 %copy-start = (bf16[192,1536]{1,0:T(8,128)(2,1)S(1)}, bf16[192,1536]{1,0:T(8,128)(2,1)}, u32[]{:S(2)}) copy-start(bf16[192,1536]{1,0:T(8,128)(2,1)} %param.25) | copy-start | bytes 1769476
  8.0 13.6 %copy-start.26 = (bf16[1536,64]{0,1:T(8,128)(2,1)S(1)}, bf16[1536,64]{0,1:T(8,128)(2,1)}, u32[]{:S(2)}) copy-start(bf16[1536,64]{0,1:T(8,128)(2,1)} %param.24) | copy-start | bytes 589828
  8.0 53.1 %all-gather.6.cloned.1.call-start = ((), (), s32[]{:S(2)}) async-start(), calls=%async_computation.9 | async-start | bytes 3538944 | tf_op jit(solution)/shard_map/all_gather | solution.py:98
  12.4 166.9 %reduce-scatter.6.cloned.1.call-start = ((), (), s32[]{:S(2)}) async-start(), calls=%async_computation.10 | async-start | bytes 7077888 | tf_op jit(solution)/shard_map/reduce_scatter | solution.py:141
  21.7 39.4 %copy-start.25 = (bf16[1536,320]{0,1:T(8,128)(2,1)}, bf16[1536,320]{0,1:T(8,128)(2,1)S(1)}, u32[]{:S(2)}) copy-start(bf16[1536,320]{0,1:T(8,128)(2,1)S(1)} %constant_dynamic-update-slice_fusion) | copy-start | bytes 2949124
  91.9 87.4 %copy-start.5 = (bf16[128,1536]{1,0:T(8,128)(2,1)S(1)}, bf16[128,1536]{1,0:T(8,128)(2,1)}, u32[]{:S(2)}) copy-start(bf16[128,1536]{1,0:T(8,128)(2,1)} %param.18) | copy-start | bytes 1179652
  91.9 88.8 %copy-start.33 = (f32[1536]{0:T(1024)S(1)}, f32[1536]{0:T(1024)}, u32[]{:S(2)}) copy-start(f32[1536]{0:T(1024)} %param.26) | copy-start | bytes 18436
  92.0 106.1 %all-gather.8.cloned.1.call-start = ((), (), s32[]{:S(2)}) async-start(), calls=%async_computation.11 | async-start | bytes 3342336 | tf_op jit(solution)/shard_map/all_gather | solution.py:169
  92.5 212.5 %all-gather.10.cloned.1.call-start = ((), (), s32[]{:S(2)}) async-start(), calls=%async_computation.12 | async-start | bytes 3342336 | tf_op jit(solution)/shard_map/all_gather | solution.py:170
  180.8 155.2 %copy-start.8 = (bf16[128,1536]{1,0:T(8,128)(2,1)}, bf16[128,1536]{1,0:T(8,128)(2,1)S(1)}, u32[]{:S(2)}) copy-start(bf16[128,1536]{1,0:T(8,128)(2,1)S(1)} %multiply_convert_fusion) | copy-start | bytes 1179652
  191.0 105.0 %all-to-all-start = ((bf16[16,2,64,1536]{3,2,1,0:T(8,128)(2,1)}), bf16[16,2,64,1536]{3,2,1,0:T(8,128)(2,1)}, u32[]{:S(2)}, u32[]{:S(2)}) async-start(bf16[16,2,64,1536]{3,2,1,0:T(8,128)(2,1)} %bitcast.420), calls=%async_computation.1 | async-start | bytes 12582912 | tf_op jit(solution)/shard_map/all_to_all | solution.py:183
  197.5 118.8 %all-gather.12.cloned.1.call-start = ((), (), s32[]{:S(2)}) async-start(), calls=%async_computation.13 | async-start | bytes 3342336 | tf_op jit(solution)/shard_map/all_gather | solution.py:171
  325.6 84.8 %all-to-all-start.1 = ((bf16[16,2,64,1536]{3,2,1,0:T(8,128)(2,1)}), bf16[16,2,64,1536]{3,2,1,0:T(8,128)(2,1)}, u32[]{:S(2)}, u32[]{:S(2)}) async-start(bf16[16,2,64,1536]{3,2,1,0:T(8,128)(2,1)} %copy.82), calls=%async_computation.2 | async-start | bytes 12582912 | tf_op jit(solution)/shard_map/all_to_all | solution.py:188
  554.4 80.7 %all-to-all-start.3 = ((bf16[16,2,64,1536]{3,2,1,0:T(8,128)(2,1)}), bf16[16,2,64,1536]{3,2,1,0:T(8,128)(2,1)}, u32[]{:S(2)}, u32[]{:S(2)}) async-start(bf16[16,2,64,1536]{3,2,1,0:T(8,128)(2,1)} %copy.85), calls=%async_computation.4 | async-start | bytes 12582912 | tf_op jit(solution)/shard_map/all_to_all | solution.py:255
  559.1 173.0 %all-gather.14.cloned.1.call-start = ((), (), s32[]{:S(2)}) async-start(), calls=%async_computation.14 | async-start | bytes 3538944 | tf_op jit(solution)/shard_map/all_gather | solution.py:263
  651.9 139.8 %reduce-scatter.14.cloned.1.call-start = ((), (), s32[]{:S(2)}) async-start(), calls=%async_computation.19 | async-start | bytes 3342336 | tf_op jit(solution)/shard_map/reduce_scatter | solution.py:251
  660.6 178.4 %reduce-scatter.12.cloned.1.call-start = ((), (), s32[]{:S(2)}) async-start(), calls=%async_computation.18 | async-start | bytes 3342336 | tf_op jit(solution)/shard_map/reduce_scatter | solution.py:248
  669.4 241.3 %reduce-scatter.10.cloned.1.call-start = ((), (), s32[]{:S(2)}) async-start(), calls=%async_computation.17 | async-start | bytes 3342336 | tf_op jit(solution)/shard_map/reduce_scatter | solution.py:245
  678.0 57.4 %copy-start.2 = (bf16[1024,1,64]{0,2,1:T(8,128)(2,1)S(1)}, bf16[1024,1,64]{0,2,1:T(8,128)(2,1)}, u32[]{:S(2)}) copy-start(bf16[1024,1,64]{0,2,1:T(8,128)(2,1)} %copy-done.1) | copy-start | bytes 393220
  678.1 57.4 %copy-start.4 = (bf16[2,512,1,3,64]{1,4,3,2,0:T(8,128)(2,1)S(1)}, bf16[2,512,1,3,64]{1,4,3,2,0:T(8,128)(2,1)}, u32[]{:S(2)}) copy-start(bf16[2,512,1,3,64]{1,4,3,2,0:T(8,128)(2,1)} %copy-done.3) | copy-start | bytes 1179652
  678.1 57.4 %copy-start.13 = (bf16[1024,1,64]{0,2,1:T(8,128)(2,1)S(1)}, bf16[1024,1,64]{0,2,1:T(8,128)(2,1)}, u32[]{:S(2)}) copy-start(bf16[1024,1,64]{0,2,1:T(8,128)(2,1)} %copy-done.12) | copy-start | bytes 393220
  678.1 57.4 %copy-start.21 = (s32[1,1024]{1,0:T(1,128)S(1)}, s32[1,1024]{1,0:T(1,128)}, u32[]{:S(2)}) copy-start(s32[1,1024]{1,0:T(1,128)} %param.19) | copy-start | bytes 12292
  678.1 57.4 %copy-start.28 = (s32[2,512]{1,0:T(2,128)S(1)}, s32[2,512]{1,0:T(2,128)}, u32[]{:S(2)}) copy-start(s32[2,512]{1,0:T(2,128)} %copy-done.27) | copy-start | bytes 12292
  678.1 57.4 %copy-start.30 = (s32[2,512]{1,0:T(2,128)S(1)}, s32[2,512]{1,0:T(2,128)}, u32[]{:S(2)}) copy-start(s32[2,512]{1,0:T(2,128)} %copy-done.29) | copy-start | bytes 12292
  678.1 57.4 %copy-start.32 = (f32[2,1,3,512]{3,2,1,0:T(4,128)S(1)}, f32[2,1,3,512]{3,2,1,0:T(4,128)}, u32[]{:S(2)}) copy-start(f32[2,1,3,512]{3,2,1,0:T(4,128)} %copy-done.31) | copy-start | bytes 36868
  678.1 234.3 %all-reduce.9.cloned.1.call-start = ((), (), s32[]{:S(2)}) async-start(), calls=%async_computation.20 | async-start | bytes 3145728 | tf_op jit(solution)/shard_map/psum | solution.py:342
  785.6 172.0 %reduce-scatter.8.cloned.1.call-start = ((), (), s32[]{:S(2)}) async-start(), calls=%async_computation.15 | async-start | bytes 3538944 | tf_op jit(solution)/shard_map/reduce_scatter | solution.py:331
  790.7 166.9 %copy-start.6 = (bf16[128,1536]{1,0:T(8,128)(2,1)S(1)}, bf16[128,1536]{1,0:T(8,128)(2,1)}, u32[]{:S(2)}) copy-start(bf16[128,1536]{1,0:T(8,128)(2,1)} %param.18) | copy-start | bytes 1179652
  790.7 166.9 %copy-start.34 = (f32[1536]{0:T(1024)S(1)}, f32[1536]{0:T(1024)}, u32[]{:S(2)}) copy-start(f32[1536]{0:T(1024)} %param.21) | copy-start | bytes 18436
  790.7 166.9 %copy-start.37 = (f32[128]{0:T(128)S(1)}, f32[128]{0:T(128)}, u32[]{:S(2)}) copy-start(f32[128]{0:T(128)} %copy-done.36) | copy-start | bytes 1540
  790.7 168.2 %copy-start.38 = (f32[128]{0:T(128)S(1)}, f32[128]{0:T(128)}, u32[]{:S(2)}) copy-start(f32[128]{0:T(128)} %get-tuple-element.421) | copy-start | bytes 1540
  790.7 374.6 %all-reduce.7.cloned.1.call-start = ((), (), s32[]{:S(2)}) async-start(), calls=%async_computation.16 | async-start | bytes 393216 | tf_op jit(solution)/shard_map/psum | solution.py:354
  (25 other events, 106.5 us)
Sparse Core Ops, SparseCore 0:
  12.5 48.5 all-gather.5
  92.1 87.2 reduce-scatter.5
  652.1 79.9 all-gather.13
  785.7 116.9 all-reduce.8
  908.9 256.3 all-reduce.6
Sparse Core Ops, SparseCore 1:
  94.3 87.3 all-gather.7
  183.4 39.5 all-gather.9
  224.7 39.7 all-gather.11
  660.7 107.2 reduce-scatter.13
  770.6 68.4 reduce-scatter.11
  841.6 69.0 reduce-scatter.9
  913.1 44.5 reduce-scatter.7
where the time goes:
time: 1180 us; the launch traced here: 1170 us
  waiting for transfers between devices  689 us (58%)
  blocking collectives  154 us (13%)
  matrix products  130 us (11%)
  local copies, waits for them, and re-layouts  94.6 us (8%)
  other arithmetic  67.9 us (6%)
  starting transfers between devices  22.8 us (2%)
  between operations  16.7 us (1%)
    psum x1, waiting for transfers between devices, local(): lax.psum((norm1_gain_part, norm2_gain_part, router_grad), ('dp', 'expert'...  127 us
    all_to_all x1, waiting for transfers between devices, local(): lax.all_to_all(send_rows, 'expert', split_axis=0, concat_axis=0, tiled=True)  97.8 us
    psum x1, blocking collectives, local(): lax.psum((norm1_gain_part, norm2_gain_part, router_grad), ('dp', 'expert'...  77.1 us
    all_to_all x1, blocking collectives, local(): lax.all_to_all(send_grads, 'expert', split_axis=0, concat_axis=0, tiled=T...  76.6 us
    all_to_all x1, waiting for transfers between devices, local(): lax.all_to_all(result, 'expert', split_axis=0, concat_axis=0, tiled=True)  74.1 us
    reduce_scatter x1, waiting for transfers between devices, local(): lax.psum_scatter(jnp.dot(picked, w_out, preferred_element_type=jnp.float3...  71.8 us
    all_to_all x1, waiting for transfers between devices, local(): lax.all_to_all(row_grads, 'expert', split_axis=0, concat_axis=0, tiled=True)  70.3 us
    reduce_scatter x1, waiting for transfers between devices, local(): lax.psum_scatter(gate_w_part.astype(jnp.bfloat16), ('dp', 'tensor'), scat...  69.9 us
  transfers between devices with their start and end apart: 15, of which 10 were waited for; matrix products, arithmetic and copies ran while one was open for 14% of the time, Pallas kernels for 0%

commit v1 on v0

v1 whole, which is shorter than its diff:
```python
import jax
import jax.numpy as jnp
from jax import lax
from jax.sharding import PartitionSpec as P

HEAD_DIM = 64
HALF = HEAD_DIM // 2
TOP = 8
CAP = 64
LANES = 128

epsilon_norm = 1e-06
rope_theta = 10000.0
masked_score = -1e30
block_limit = 512
f32 = jnp.float32
bf16 = jnp.bfloat16


def rms_inverse(values):
    return lax.rsqrt(jnp.mean(values * values, axis=-1, keepdims=True) + epsilon_norm)


def rms_backward(values, inverse, norm_gain, grad_out):
    scaled = grad_out * norm_gain
    grad_in = inverse * scaled - values * (inverse * inverse * inverse) * jnp.mean(
        scaled * values, axis=-1, keepdims=True
    )
    return (grad_in, jnp.sum(grad_out * values * inverse, axis=0))


def rope_tables(seq_len, head_width):
    half_dim = head_width // 2
    frequency = rope_theta ** (-2.0 * jnp.arange(half_dim, dtype=f32) / head_width)
    angles = jnp.arange(seq_len, dtype=f32)[:, None] * frequency[None, :]
    angles = jnp.concatenate([angles, angles], axis=1)
    return (jnp.cos(angles), jnp.sin(angles))


def rotate_half(values):
    return jnp.concatenate([-values[..., HALF:], values[..., :HALF]], axis=-1)


def rotate_back(values):
    return jnp.concatenate([values[..., HALF:], -values[..., :HALF]], axis=-1)


def dot32(left, right):
    return jnp.dot(left, right, preferred_element_type=f32)


def allowed_mask(query_pos, query_seg, key_pos, key_seg):
    same_doc = query_seg[:, None] == key_seg[None, :]
    causal = key_pos[None, :] <= query_pos[:, None]
    diagonal = key_pos[None, :] == query_pos[:, None]
    return causal & same_doc & ((query_seg[:, None] != 0) | diagonal)


def attention_forward(normed_all, joined_weights, key_seg, tables):
    seq_len = normed_all.shape[0]
    kv_width = HEAD_DIM
    query_width = joined_weights.shape[1] - 2 * kv_width
    heads = query_width // HEAD_DIM
    joined = dot32(normed_all, joined_weights)
    cosine, sine = tables
    query = joined[:, :query_width].reshape(seq_len, heads, HEAD_DIM)
    key = joined[:, query_width : query_width + kv_width]
    value_low = joined[:, query_width + kv_width :].astype(bf16)
    query_low = (query * cosine[:, None, :] + rotate_half(query) * sine[:, None, :]).astype(bf16)
    key_low = (key * cosine + rotate_half(key) * sine).astype(bf16)
    pos = jnp.arange(seq_len, dtype=jnp.int32)
    scores = jnp.einsum("qrd,kd->rqk", query_low, key_low, preferred_element_type=f32)
    masked = jnp.where(
        allowed_mask(pos, key_seg, pos, key_seg), scores * HEAD_DIM ** (-0.5), masked_score
    )
    top_score = jnp.max(masked, axis=-1, keepdims=True)
    exp_scores = jnp.exp(masked - top_score)
    exp_total = jnp.sum(exp_scores, axis=-1, keepdims=True)
    probs = (exp_scores / exp_total).astype(bf16)
    context = jnp.einsum("rqk,kd->qrd", probs, value_low, preferred_element_type=f32)
    lse = (top_score + jnp.log(exp_total))[..., 0]
    return context.reshape(seq_len, query_width).astype(bf16), (
        query_low,
        key_low,
        value_low,
        lse,
    )


def attention_backward(saved, context_grad, key_seg, tables):
    query_low, key_low, value_low, lse = saved
    seq_len, heads, _ = query_low.shape
    cosine, sine = tables
    grad = context_grad.reshape(seq_len, heads, HEAD_DIM)
    pos = jnp.arange(seq_len, dtype=jnp.int32)
    scale = HEAD_DIM ** (-0.5)
    scores = jnp.einsum("qrd,kd->rqk", query_low, key_low, preferred_element_type=f32) * scale
    masked = jnp.where(allowed_mask(pos, key_seg, pos, key_seg), scores, masked_score)
    probs = jnp.exp(masked - lse[..., None])
    probs_grad = jnp.einsum("qrd,kd->rqk", grad, value_low, preferred_element_type=f32)
    row_dot = jnp.sum(probs * probs_grad, axis=-1, keepdims=True)
    score_grad = (probs * (probs_grad - row_dot)).astype(bf16)
    query_grad = jnp.einsum("rqk,kd->qrd", score_grad, key_low, preferred_element_type=f32)
    key_grad = jnp.einsum("rqk,qrd->kd", score_grad, query_low, preferred_element_type=f32)
    value_grad = jnp.einsum("rqk,qrd->kd", probs.astype(bf16), grad, preferred_element_type=f32)
    query_grad = query_grad * scale
    key_grad = key_grad * scale
    query_grad = query_grad * cosine[:, None, :] + rotate_back(query_grad * sine[:, None, :])
    key_grad = key_grad * cosine + rotate_back(key_grad * sine)
    return jnp.concatenate(
        [query_grad.reshape(seq_len, heads * HEAD_DIM), key_grad, value_grad], axis=1
    ).astype(bf16)


def split_two(values):
    high = values.astype(bf16)
    return high, (values - high.astype(f32)).astype(bf16)


SIDE = 4
STEPS = (0, 1, -1, 2)


def owner_of(place, me):
    return jnp.asarray([0, 2, 3, 1])[(place - me) % SIDE]


def along(axis, step):
    pairs = []
    for a in range(SIDE):
        for b in range(SIDE):
            to = ((a + step) % SIDE, b) if axis == 0 else (a, (b + step) % SIDE)
            pairs.append((a * SIDE + b, to[0] * SIDE + to[1]))
    return pairs


def move(values, axis, step):
    return lax.ppermute(values, "expert", along(axis, step))


def together(*values):
    return lax.optimization_barrier(values)


def swap_cores(values):
    return lax.ppermute(values, "dp", [(0, 1), (1, 0)])


def line_gather(values, axis):
    return [values] + [move(values, axis, step) for step in STEPS[1:]]


def gather_plane(values):
    half = values.shape[0] // 2
    first = line_gather(jnp.stack(line_gather(values[:half], 1)), 0)
    second = line_gather(jnp.stack(line_gather(values[half:], 0)), 1)
    return first, second


def line_scatter(parts, axis):
    total = parts[0].astype(f32)
    for part, step in zip(parts[1:], STEPS[1:]):
        total = total + move(part, axis, -step).astype(f32)
    return total.astype(bf16)


def scatter_plane(first, second):
    first = line_scatter(first, 0)
    second = line_scatter(second, 1)
    first = line_scatter([first[i] for i in range(SIDE)], 1)
    second = line_scatter([second[i] for i in range(SIDE)], 0)
    return jnp.concatenate([first, second], axis=0)


def local(
    tokens,
    segments,
    routes,
    norm1_gain,
    w_query,
    w_key,
    w_value,
    w_out,
    norm2_gain,
    w_router,
    w_gate,
    w_up,
    w_down,
    cotangent,
):
    tok_rows, width = tokens.shape
    seq_len = segments.shape[1]
    query_width = w_query.shape[1]
    kv_width = w_key.shape[1]
    joined_width = query_width + 2 * kv_width
    local_experts = w_gate.shape[0]
    experts = w_router.shape[1]
    owners = lax.axis_size("expert")
    planes = lax.axis_size("tensor")
    owner = lax.axis_index("expert")
    first_expert = owner * local_experts
    key_seg = segments[0]
    hidden_width = w_gate.shape[2]

    token_f32 = tokens.astype(f32)
    inverse_one = rms_inverse(token_f32)
    normed_low = (token_f32 * inverse_one * norm1_gain).astype(bf16)
    joined_weights = jnp.concatenate([w_query, w_key, w_value], axis=1)
    normed_all = lax.all_gather(normed_low, "tensor", axis=0, tiled=True)
    core = lax.axis_index("dp")

    expert_ids = jnp.arange(experts, dtype=jnp.int32)
    onehot = (routes[:, :, None] == expert_ids[None, None, :]).astype(f32)
    member = jnp.sum(onehot, axis=1)
    lower = (jnp.arange(tok_rows)[:, None] <= jnp.arange(tok_rows)[None, :]).astype(bf16)
    rank = jnp.einsum("te,tu->eu", member.astype(bf16), lower, preferred_element_type=f32)
    rank = jnp.where(member.T > 0, rank - 1.0, -1.0).astype(bf16)
    extra = jnp.pad(rank, ((0, tok_rows - experts), (0, LANES - tok_rows)))
    cot_payload = jnp.concatenate([cotangent, extra], axis=1)

    cot_halves = gather_plane(cot_payload)

    def half_gather(shard):
        count = shard.shape[0] // 2
        half = lax.dynamic_slice_in_dim(shard, core * count, count, 0)
        return lax.all_gather(half, "tensor", axis=0)

    normed_all, cot_halves, w_out = together(normed_all, cot_halves, w_out)
    half_out = half_gather(w_out)
    weights = jnp.concatenate(
        [w_gate, w_up, w_down.reshape(local_experts, -1, hidden_width)], axis=1
    )
    half_out, weights = together(half_out, weights)
    weights_all = lax.all_gather(weights, ("dp", "tensor"), axis=0)
    weights_all, joined_rows = together(weights_all, joined_weights.T)
    half_joined = half_gather(joined_rows)

    tables = rope_tables(seq_len, HEAD_DIM)
    context, saved = attention_forward(normed_all, joined_weights, key_seg, tables)
    context_home = lax.all_to_all(
        context.reshape(planes, tok_rows, query_width), "tensor", split_axis=0, concat_axis=0
    )
    other_out = swap_cores(half_out)

    def both_halves(blocks, mine, other):
        count = blocks.shape[2] // 2
        first = lax.dynamic_slice_in_dim(blocks, core * count, count, 2)
        second = lax.dynamic_slice_in_dim(blocks, (1 - core) * count, count, 2)
        return jnp.einsum("jtq,jqd->td", first, mine, preferred_element_type=f32) + jnp.einsum(
            "jtq,jqd->td", second, other, preferred_element_type=f32
        )

    mid = token_f32 + both_halves(context_home, half_out, other_out)
    inverse_two = rms_inverse(mid)
    normed_two = (mid * inverse_two * norm2_gain).astype(bf16)
    logits = dot32(normed_two, w_router)
    logits = jnp.where(member > 0, logits, masked_score)
    chosen_exp = jnp.where(
        member > 0, jnp.exp(logits - jnp.max(logits, axis=1, keepdims=True)), 0.0
    )
    gates = chosen_exp / jnp.sum(chosen_exp, axis=1, keepdims=True)
    gate_high, gate_low = split_two(gates)
    payload = jnp.concatenate(
        [normed_two, gate_high, gate_low, jnp.zeros((tok_rows, LANES - 2 * experts), bf16)],
        axis=1,
    )
    rows_halves = gather_plane(payload)

    def whole(halves):
        first, second = halves
        first = jnp.stack(first)
        second = jnp.stack(second).transpose(1, 0, 2, 3)
        return jnp.concatenate([first, second], axis=2).reshape(owners, tok_rows, width + LANES)

    cot_all = whole(cot_halves)
    rows_all = whole(rows_halves)
    ranks = lax.dynamic_slice_in_dim(
        cot_all[:, :experts, width : width + tok_rows], first_expert, local_experts, 1
    )
    slots = jnp.arange(CAP, dtype=f32)
    pick = (ranks[:, :, None, :].astype(f32) == slots[:, None]).astype(bf16)
    rows = jnp.einsum("sect,std->secd", pick, rows_all, preferred_element_type=f32).astype(bf16)
    cots = jnp.einsum(
        "sect,std->secd", pick, cot_all[:, :, :width], preferred_element_type=f32
    ).astype(bf16)
    lane = jnp.arange(LANES, dtype=jnp.int32)
    mine = first_expert + jnp.arange(local_experts, dtype=jnp.int32)[:, None]
    mine_mask = ((lane == mine) | (lane == mine + experts)).astype(f32)
    gate_col = jnp.sum(
        rows[..., width:].astype(f32) * mine_mask[:, None, :], axis=-1, keepdims=True
    )
    rows = rows[..., :width]

    group = weights_all.shape[0]
    part_rows = w_gate.shape[1]
    down_rows = w_down.shape[1]
    full_gate = weights_all[:, :, :part_rows].transpose(1, 0, 2, 3).reshape(
        local_experts, group * part_rows, hidden_width
    )
    full_up = weights_all[:, :, part_rows : 2 * part_rows].transpose(1, 0, 2, 3).reshape(
        local_experts, group * part_rows, hidden_width
    )
    full_down = (
        weights_all[:, :, 2 * part_rows :]
        .transpose(1, 0, 2, 3)
        .reshape(local_experts, group * down_rows, width)
    )
    gate_pre = jnp.einsum("secd,edf->secf", rows, full_gate, preferred_element_type=f32)
    up_pre = jnp.einsum("secd,edf->secf", rows, full_up, preferred_element_type=f32)
    gate_sig = jax.nn.sigmoid(gate_pre)
    silu = gate_pre * gate_sig
    hidden = (silu * up_pre).astype(bf16)
    back = jnp.einsum("secd,efd->secf", cots, full_down, preferred_element_type=f32)
    gate_grad = jnp.sum(back * hidden.astype(f32), axis=-1, keepdims=True)
    hidden_grad = gate_col * back
    gate_pre_grad = (hidden_grad * up_pre * (gate_sig + silu * (1.0 - gate_sig))).astype(bf16)
    up_pre_grad = (hidden_grad * silu).astype(bf16)
    row_grads = jnp.einsum("secf,edf->secd", gate_pre_grad, full_gate, preferred_element_type=f32)
    row_grads = row_grads + jnp.einsum(
        "secf,edf->secd", up_pre_grad, full_up, preferred_element_type=f32
    )
    grad_high, grad_low = split_two(gate_grad)
    high_mask = (lane == mine)[:, None, :]
    low_mask = (lane == mine + experts)[:, None, :]
    tail = jnp.where(high_mask, grad_high, jnp.where(low_mask, grad_low, jnp.zeros((), bf16)))
    row_grads = jnp.concatenate([row_grads.astype(bf16), tail], axis=-1)
    back_part = jnp.einsum("sect,secd->std", pick, row_grads, preferred_element_type=f32)
    back_part = back_part.astype(bf16).reshape(SIDE, SIDE, tok_rows, width + LANES)
    half = tok_rows // 2
    back_home = scatter_plane(
        [back_part[i, :, :half] for i in range(SIDE)],
        [back_part[:, i, half:] for i in range(SIDE)],
    )

    expert_out = jnp.einsum("secf,efd->secd", hidden, full_down, preferred_element_type=f32)
    mixture_part = jnp.einsum(
        "sect,secd->std", pick, (gate_col * expert_out).astype(bf16), preferred_element_type=f32
    )
    place = (owner_of(jnp.arange(SIDE), owner // SIDE)[:, None] * SIDE) + owner_of(
        jnp.arange(SIDE), owner % SIDE
    )
    gate_w = jnp.einsum("secd,secf->edf", rows, gate_pre_grad, preferred_element_type=f32)
    up_w = jnp.einsum("secd,secf->edf", rows, up_pre_grad, preferred_element_type=f32)
    scaled_hidden = (gate_col * hidden.astype(f32)).astype(bf16)
    down_w = jnp.einsum("secf,secd->efd", scaled_hidden, cots, preferred_element_type=f32)

    def by_holder(part):
        return part.astype(bf16).reshape(local_experts, group, -1, hidden_width)

    weight_part = jnp.concatenate([by_holder(gate_w), by_holder(up_w), by_holder(down_w)], axis=2)
    weight_part = weight_part.transpose(1, 0, 2, 3)
    kept = lax.dynamic_slice_in_dim(weight_part, core * planes, planes, 0)
    given = lax.dynamic_slice_in_dim(weight_part, (1 - core) * planes, planes, 0)
    kept = (kept.astype(f32) + swap_cores(given).astype(f32)).astype(bf16)
    back_home, mixture_part, kept, half_joined = together(
        back_home, mixture_part.astype(bf16)[place.reshape(-1)], kept, half_joined
    )
    cot_f32 = cotangent.astype(f32)
    grad_tail = back_home[:, width:].astype(f32)
    gate_grad = grad_tail[:, :experts] + grad_tail[:, experts : 2 * experts]
    chosen_grad = gates * (gate_grad - jnp.sum(gates * gate_grad, axis=1, keepdims=True))
    logit_grad = chosen_grad.astype(bf16)
    router_part = jnp.einsum("td,te->de", normed_two, logit_grad, preferred_element_type=f32)
    normed_two_grad = back_home[:, :width].astype(f32) + jnp.einsum(
        "te,de->td", logit_grad, w_router, preferred_element_type=f32
    )
    mid_part, norm2_part = rms_backward(mid, inverse_two, norm2_gain, normed_two_grad)
    mid_grad = cot_f32 + mid_part
    attention_low = mid_grad.astype(bf16)
    def both_back(rows, mine, other):
        first = jnp.einsum("td,jqd->jtq", rows, mine, preferred_element_type=f32)
        second = jnp.einsum("td,jqd->jtq", rows, other, preferred_element_type=f32)
        low = jnp.where(core == 0, first, second)
        high = jnp.where(core == 0, second, first)
        return jnp.concatenate([low, high], axis=2).astype(bf16)

    context_grad = both_back(attention_low, half_out, other_out)
    context_grad = lax.all_to_all(context_grad, "tensor", split_axis=0, concat_axis=0)
    weight_sum = lax.psum_scatter(kept, "tensor", scatter_dimension=0, tiled=True)[0].astype(f32)
    mixture_part, weight_sum = together(mixture_part, weight_sum)
    mixture = lax.psum_scatter(
        mixture_part.reshape(owners * tok_rows, width), "expert", scatter_dimension=0, tiled=True
    )
    output = (mid + mixture.astype(f32)).astype(bf16)
    w_gate_grad = weight_sum[:, :part_rows]
    w_up_grad = weight_sum[:, part_rows : 2 * part_rows]
    w_down_grad = weight_sum[:, 2 * part_rows :].reshape(local_experts, down_rows, width)

    joined_grad = attention_backward(
        saved, context_grad.reshape(seq_len, query_width), key_seg, tables
    )
    joined_grad, weight_sum = together(joined_grad, weight_sum)
    joined_home = lax.all_to_all(
        joined_grad.reshape(planes, tok_rows, joined_width), "tensor", split_axis=0, concat_axis=0
    )
    attention_all = lax.all_gather(attention_low, "tensor", axis=0, tiled=True)
    out_part = jnp.einsum("tq,td->qd", context, attention_all, preferred_element_type=f32)
    joined_part = jnp.einsum("td,tq->dq", normed_all, joined_grad, preferred_element_type=f32)
    normed_one_grad = both_halves(joined_home, half_joined, swap_cores(half_joined))
    input_part, norm1_part = rms_backward(token_f32, inverse_one, norm1_gain, normed_one_grad)
    input_grad = mid_grad + input_part

    sharers = lax.axis_size("dp") * owners
    shared_part = jnp.concatenate([router_part.reshape(-1), norm2_part, norm1_part])
    flat_part = jnp.concatenate(
        [
            part.astype(bf16).reshape(-1, LANES)
            for part in (joined_part, out_part, shared_part)
        ],
        axis=0,
    )
    flat_rows = flat_part.shape[0]
    block = -(-flat_rows // (16 * sharers)) * 16
    flat_part = jnp.pad(flat_part, ((0, sharers * block - flat_rows), (0, 0)))
    arrived = lax.all_to_all(
        flat_part.reshape(sharers, block, LANES), ("dp", "expert"), split_axis=0, concat_axis=0
    )
    total = jnp.sum(arrived.astype(f32), axis=0).astype(bf16)
    flat_sum = lax.all_to_all(
        jnp.broadcast_to(total[None], arrived.shape), ("dp", "expert"), split_axis=0, concat_axis=0
    ).reshape(sharers * block, LANES)
    cut = width * joined_width // LANES
    end = cut + query_width * width // LANES
    joined_sum = flat_sum[:cut].reshape(width, joined_width).astype(f32)
    out_sum = flat_sum[cut:end].reshape(query_width, width).astype(f32)
    shared = flat_sum[end:flat_rows]
    shared = lax.all_to_all(
        jnp.broadcast_to(shared[None], (planes,) + shared.shape),
        "tensor",
        split_axis=0,
        concat_axis=0,
    )
    shared = jnp.sum(shared.astype(f32), axis=0).reshape(-1)
    router_size = width * experts
    return (
        output,
        input_grad,
        shared[router_size + width : router_size + 2 * width],
        joined_sum[:, :query_width],
        joined_sum[:, query_width : query_width + kv_width],
        joined_sum[:, query_width + kv_width :],
        out_sum,
        shared[router_size : router_size + width],
        shared[:router_size].reshape(width, experts),
        w_gate_grad,
        w_up_grad,
        w_down_grad,
    )


def solution(mesh):
    rows = P(("dp", "expert", "tensor"), None)
    columns = P(None, "tensor")
    experts = P("expert", ("dp", "tensor"), None)
    return jax.shard_map(
        local,
        mesh=mesh,
        in_specs=(
            rows,
            P(("dp", "expert"), None),
            rows,
            P(),
            columns,
            columns,
            columns,
            P("tensor", None),
            P(),
            P(),
            experts,
            experts,
            experts,
            rows,
        ),
        out_specs=(
            rows,
            rows,
            P(),
            columns,
            columns,
            columns,
            P("tensor", None),
            P(),
            P(),
            experts,
            experts,
            experts,
        ),
        check_vma=False,
    )
```

time: 1180 us -> 829 us (0.70)
  waiting for transfers between devices: 689 us -> 317 us
  blocking collectives: 154 us -> 41.7 us
  starting transfers between devices: 22.8 us -> 86.4 us
  local copies, waits for them, and re-layouts: 94.6 us -> 148 us
  other arithmetic: 67.9 us -> 82.5 us
    reduce_scatter x5 -> x1, waiting for transfers between devices: 225 us -> 23.9 us  [local(): lax.psum_scatter(kept, 'tensor', scatter_dimension=0, tiled=True)[0]]
    all_to_all x3 -> x5, waiting for transfers between devices: 242 us -> 64.6 us  [the longest x1 25 us: local(): lax.all_to_all(jnp.broadcast_to(total[None], arrived.shape), ('dp', 'expe...]
    psum x2 -> x0, waiting for transfers between devices: 127 us -> none  [the longest x1 127 us: local(): lax.psum((norm1_gain_part, norm2_gain_part, router_grad), ('dp', 'expert'...]
    ppermute x0 -> x39, waiting for transfers between devices: none -> 127 us  [the longest x36 127 us: move(): return lax.ppermute(values, 'expert', along(axis, step))]
    psum x1 -> x0, blocking collectives: 77.1 us -> none  [local(): lax.psum((norm1_gain_part, norm2_gain_part, router_grad), ('dp', 'expert'...]
    ppermute x0 -> x39, starting transfers between devices: none -> 63.5 us  [the longest x36 40.6 us: move(): return lax.ppermute(values, 'expert', along(axis, step))]
    gather x4 -> x3, local copies, waits for them, and re-layouts: 47.4 us -> 7.78 us  [the longest x1 6.5 us: local(): mixture_part.astype(bf16)[place.reshape(-1)]]
    all_to_all x1, blocking collectives: 76.6 us -> 41.7 us  [local(): lax.all_to_all(flat_part.reshape(sharers, block, LANES), ('dp', 'expert')...]
  transfers between devices with their start and end apart: 15 -> 51, of which waited for: 10 -> 24; matrix products, arithmetic and copies ran while one was open for 14% -> 31% of each run, Pallas kernels for 0% -> 0%
where the time goes in v1:
time: 829 us; the launch traced here: 820 us
  waiting for transfers between devices  317 us (38%)
  local copies, waits for them, and re-layouts  148 us (18%)
  matrix products  129 us (16%)
  starting transfers between devices  86.4 us (10%)
  other arithmetic  82.5 us (10%)
  blocking collectives  41.7 us (5%)
  between operations  15.8 us (2%)
    ppermute x36, waiting for transfers between devices, move(): return lax.ppermute(values, 'expert', along(axis, step))  127 us
    all_gather x2, waiting for transfers between devices, half_gather(): return lax.all_gather(half, 'tensor', axis=0)  64 us
    all_to_all x1, blocking collectives, local(): lax.all_to_all(flat_part.reshape(sharers, block, LANES), ('dp', 'expert')...  41.7 us
    ppermute x36, starting transfers between devices, move(): return lax.ppermute(values, 'expert', along(axis, step))  40.6 us
    all_gather x1, waiting for transfers between devices, local(): attention_all = lax.all_gather(attention_low, 'tensor', axis=0, tiled=True)  37.4 us
    unnamed x183, local copies, waits for them, and re-layouts  35.9 us
    ppermute x12, local copies, waits for them, and re-layouts, move(): return lax.ppermute(values, 'expert', along(axis, step))  31 us
    all_to_all x1, waiting for transfers between devices, local(): lax.all_to_all(jnp.broadcast_to(total[None], arrived.shape), ('dp', 'expe...  25 us
  transfers between devices with their start and end apart: 51, of which 24 were waited for; matrix products, arithmetic and copies ran while one was open for 31% of the time, Pallas kernels for 0%

profile of v1, /device:TPU:1, one launch (start us, length us, event | category | flops | bytes accessed | tf_op | source)
XLA Modules:
  0.0 820.1 jit_solution(17604763860556234135)
XLA Ops:
  21.1 6.2 collective-permute-done.8
  36.2 16.4 %collective-permute-done.1 = bf16[64,1664]{1,0:T(8,128)(2,1)S(1)} collective-permute-done((bf16[64,1664]{1,0:T(8,128)(2,1)S(1)}, bf16[64,1664]{1,0:T(8,128)(2,1)S(1)}, u32[]{:S(2)}, u32[]{:S(2)}) %collective-permute-start.1) | collective-permute-done | bytes 213024 | tf_op jit(solution)/shard_map/ppermute | solution.py:138
  58.3 16.4 %collective-permute-done.9 = bf16[4,64,1664]{2,1,0:T(8,128)(2,1)} collective-permute-done((bf16[4,64,1664]{2,1,0:T(8,128)(2,1)S(1)}, bf16[4,64,1664]{2,1,0:T(8,128)(2,1)}, u32[]{:S(2)}, u32[]{:S(2)}) %collective-permute-start.9) | collective-permute-done | bytes 852000 | tf_op jit(solution)/shard_map/ppermute | solution.py:138
  78.8 64.0 %all-gather.13.cloned.1.call-done = bf16[768,1536]{1,0:T(8,128)(2,1)} async-done(((bf16[96,1536]{1,0:T(8,128)(2,1)}), bf16[768,1536]{1,0:T(8,128)(2,1)}) %all-gather.13.cloned.1.call-update) | async-done | bytes 2359312 | tf_op jit(solution)/shard_map/all_gather | solution.py:226
  172.1 16.5 %all-to-all-done = bf16[8,128,192]{1,2,0:T(8,128)(2,1)S(1)} async-done(((bf16[8,128,192]{1,2,0:T(8,128)(2,1)}), bf16[8,128,192]{1,2,0:T(8,128)(2,1)S(1)}, u32[]{:S(2)}, u32[]{:S(2)}) %all-to-all-start) | async-done | bytes 393248 | tf_op jit(solution)/shard_map/all_to_all | solution.py:240
  205.9 10.0 %collective-permute-done.15 = bf16[64,1664]{0,1:T(8,128)(2,1)S(1)} collective-permute-done((bf16[64,1664]{0,1:T(8,128)(2,1)S(1)}, bf16[64,1664]{0,1:T(8,128)(2,1)S(1)}, u32[]{:S(2)}, u32[]{:S(2)}) %collective-permute-start.15) | collective-permute-done | bytes 213024 | tf_op jit(solution)/shard_map/ppermute | solution.py:138
  229.8 18.1 %collective-permute-done.19 = bf16[64,1664]{0,1:T(8,128)(2,1)S(1)} collective-permute-done((bf16[64,1664]{0,1:T(8,128)(2,1)}, bf16[64,1664]{0,1:T(8,128)(2,1)S(1)}, u32[]{:S(2)}, u32[]{:S(2)}) %collective-permute-start.19) | collective-permute-done | bytes 213024 | tf_op jit(solution)/shard_map/ppermute | solution.py:138
  249.5 8.5 %collective-permute-done.21 = bf16[64,1664]{0,1:T(8,128)(2,1)S(1)} collective-permute-done((bf16[64,1664]{0,1:T(8,128)(2,1)}, bf16[64,1664]{0,1:T(8,128)(2,1)S(1)}, u32[]{:S(2)}, u32[]{:S(2)}) %collective-permute-start.21) | collective-permute-done | bytes 213024 | tf_op jit(solution)/shard_map/ppermute | solution.py:138
  287.0 6.1 collective-permute-done.24
  306.1 9.8 %copy.215 = bf16[4,4,128,1664]{3,2,1,0:T(8,128)(2,1)} copy(bf16[4,4,128,1664]{2,3,0,1:T(8,128)(2,1)} %pad_maximum_fusion.2) | data formatting | bytes 13631488 | tf_op jit(solution)/shard_map/concatenate | solution.py:273
  347.2 11.1 %fusion.28 = (f32[16,2,64]{2,0,1:T(8,128)S(1)}, bf16[16,2,64,512]{3,2,0,1:T(8,128)(2,1)}, bf16[16,2,64,512]{3,2,0,1:T(8,128)(2,1)}, bf16[16,2,64,512]{3,2,0,1:T(8,128)(2,1)S(1)}) fusion(f32[2,512,16,64]{1,3,2,0:T(8,128)} %fusion.18, f32[2,512,16,64]{1,3,2,0:T(8,128)} %fusion.16, f32[16,2,64]{2,0,1:T(8,128)S(1)} %copy.216, ...), kind=kOutput, calls=%fused_computation.51 | convolution fusion | flops 3240097792 | bytes 24133632 | tf_op jit(solution)/shard_map/secd,efd->secf/dot_general | solution.py:313
  358.3 7.3 bitcast_convert_fusion.4
  370.5 7.1 bitcast_convert_fusion.2
  383.4 7.5 pad_maximum_fusion
  390.9 6.7 constant_dynamic-slice_fusion.2
  400.4 15.9 %collective-permute-start.37 = (bf16[8,2,288,512]{3,2,1,0:T(8,128)(2,1)}, bf16[8,2,288,512]{3,2,1,0:T(8,128)(2,1)}, u32[]{:S(2)}, u32[]{:S(2)}) collective-permute-start(bf16[8,2,288,512]{3,2,1,0:T(8,128)(2,1)} %bitcast.321), channel_id=1, source_target_pairs={{0,128},{128,0},{1,129},{129,1},{2,130},{130,2},{3,131},{131,3},{4... | collective-permute-start | bytes 14155784 | tf_op jit(solution)/shard_map/ppermute | solution.py:146
  416.3 6.4 fusion.61
  423.7 9.6 %fusion.27 = bf16[16,2,64,1536]{3,2,1,0:T(8,128)(2,1)} fusion(f32[2,1536,16,64]{1,3,0,2:T(8,128)} %fusion.61, bf16[2,1536,512,1]{2,1,0,3:T(8,128)(2,1)} %bitcast.357, bf16[16,2,64,512]{3,2,0,1:T(8,128)(2,1)S(1)} %copy-done.73), kind=kOutput, calls=%fused_computation.50 | convolution fusion | flops 3227516928 | bytes 24117248 | tf_op jit(solution)/shard_map/secf,edf->secd/dot_general | solution.py:319
  452.7 10.2 %bitcast_convert_fusion.1 = bf16[16,128,1536]{2,1,0:T(8,128)(2,1)} fusion(bf16[2,512,1536,1]{2,1,0,3:T(8,128)(2,1)} %reshape.478, f32[16,2,64]{2,1,0:T(2,128)S(1)} %multiply_reduce_fusion, bf16[16,2,64,512]{3,2,0,1:T(8,128)(2,1)} %get-tuple-element.109, f32[16,2,128]{2,1,0:T(2,128)S(1)} %dynamic-slice_convert_fusion), kind=kOutput, calls=%fused_computation.9 | convolution fusion | flops 4036231168 | bytes 11558912 | tf_op jit(solution)/shard_map/sect,secd->std/dot_general | solution.py:336
  462.9 6.5 gather_fusion.2
  496.0 9.8 %collective-permute-done.33 = bf16[4,64,1664]{2,1,0:T(8,128)(2,1)} collective-permute-done((bf16[4,64,1664]{2,1,0:T(8,128)(2,1)}, bf16[4,64,1664]{2,1,0:T(8,128)(2,1)}, u32[]{:S(2)}, u32[]{:S(2)}) %collective-permute-start.33) | collective-permute-done | bytes 852000 | tf_op jit(solution)/shard_map/ppermute | solution.py:138
  514.3 12.8 %collective-permute-done.29 = bf16[64,1664]{0,1:T(8,128)(2,1)} collective-permute-done((bf16[64,1664]{0,1:T(8,128)(2,1)S(1)}, bf16[64,1664]{0,1:T(8,128)(2,1)}, u32[]{:S(2)}, u32[]{:S(2)}) %collective-permute-start.29) | collective-permute-done | bytes 213024 | tf_op jit(solution)/shard_map/ppermute | solution.py:138
  531.1 7.2 collective-permute-done.36
  538.8 6.1 fusion.6
  562.0 14.4 %all-to-all-done.1 = bf16[8,128,192]{1,2,0:T(8,128)(2,1)S(1)} async-done(((bf16[8,128,192]{1,2,0:T(8,128)(2,1)}), bf16[8,128,192]{1,2,0:T(8,128)(2,1)S(1)}, u32[]{:S(2)}, u32[]{:S(2)}) %all-to-all-start.1) | async-done | bytes 393248 | tf_op jit(solution)/shard_map/all_to_all | solution.py:378
  576.9 9.0 %fusion = (f32[3,1024]{1,0:T(4,128)S(1)}, f32[1024,1024,3]{1,0,2:T(8,128)}) fusion(f32[3,1024,1024]{1,2,0:T(8,128)} %copy-done.3, f32[3,1024]{1,0:T(4,128)S(1)} %log_add_fusion, bf16[1024,3,64]{0,2,1:T(8,128)(2,1)S(1)} %reshape_reshape.3, f32[1024,320]{0,1:T(8,128)} %copy-done.34), kind=kOutput, calls=%fused_computation.6 | convolution fusion | flops 412087296 | bytes 25714688 | tf_op jit(solution)/shard_map/qrd,kd->rqk/dot_general | solution.py:100
  585.9 23.9 %reduce-scatter.5.cloned.1.call-done = bf16[1,2,288,512]{3,2,1,0:T(8,128)(2,1)} async-done(((bf16[8,2,288,512]{3,2,1,0:T(8,128)(2,1)}), bf16[1,2,288,512]{3,2,1,0:T(8,128)(2,1)}) %reduce-scatter.5.cloned.1.call-update) | async-done | bytes 589840 | tf_op jit(solution)/shard_map/reduce_scatter | solution.py:379
  612.1 10.5 %fusion.2 = bf16[3,1024,1024]{1,2,0:T(8,128)(2,1)S(1)} fusion(f32[1024,1024,3]{1,0,2:T(8,128)} %get-tuple-element.185, f32[3,1024,1024]{1,2,0:T(8,128)} %copy-done.3, f32[3,1024]{1,0:T(4,128)S(1)} %get-tuple-element.184, f32[3,1024]{1,0:T(4,128)S(1)} %log_add_fusion), kind=kLoop, calls=%fused_computation.8 | loop fusion | flops 12582912 | bytes 31481856 | tf_op jit(solution)/shard_map/convert_element_type | solution.py:102
  635.7 37.4 %all-gather.11.cloned.1.call-done = bf16[1024,1536]{0,1:T(8,128)(2,1)} async-done(((bf16[128,1536]{0,1:T(8,128)(2,1)}), bf16[1024,1536]{0,1:T(8,128)(2,1)}) %all-gather.11.cloned.1.call-update) | async-done | bytes 3145744 | tf_op jit(solution)/shard_map/all_gather | solution.py:396
  692.5 41.7 %all_to_all.30 = bf16[32,208,128]{2,1,0:T(8,128)(2,1)S(1)} all-to-all(bf16[32,208,128]{2,1,0:T(8,128)(2,1)S(1)} %bitcast.346), channel_id=1, replica_groups=mesh['dp'=2,'expert'=16,'tensor'=8] {'dp','expert'}, dimensions={0} | all-to-all | bytes 3407872 | tf_op jit(solution)/shard_map/all_to_all | solution.py:415
  744.3 25.0 %all-to-all-done.4 = bf16[32,208,128]{2,1,0:T(8,128)(2,1)S(1)} async-done(((bf16[32,208,128]{2,1,0:T(8,128)(2,1)}), bf16[32,208,128]{2,1,0:T(8,128)(2,1)S(1)}, u32[]{:S(2)}, u32[]{:S(2)}) %all-to-all-start.4) | async-done | bytes 1703968 | tf_op jit(solution)/shard_map/all_to_all | solution.py:419
  791.1 8.7 %all-to-all-done.5 = bf16[8,408,128]{2,1,0:T(8,128)(2,1)} async-done(((bf16[8,408,128]{2,1,0:T(8,128)(2,1)}), bf16[8,408,128]{2,1,0:T(8,128)(2,1)}, u32[]{:S(2)}, u32[]{:S(2)}) %all-to-all-start.5) | async-done | bytes 835616 | tf_op jit(solution)/shard_map/all_to_all | solution.py:427
  (428 shorter events, 337.6 us)
Async XLA Ops:
  7.2 67.6 %all-gather.9.cloned.1.call-start = ((), (), s32[]{:S(2)}) async-start(), calls=%async_computation.8 | async-start | bytes 3538944 | tf_op jit(solution)/shard_map/all_gather | solution.py:209
  11.5 131.2 %all-gather.13.cloned.1.call-start = ((), (), s32[]{:S(2)}) async-start(), calls=%async_computation.11 | async-start | bytes 2654208 | tf_op jit(solution)/shard_map/all_gather | solution.py:226
  27.5 28.0 %collective-permute-start.10 = (bf16[4,64,1664]{2,1,0:T(8,128)(2,1)S(1)}, bf16[4,64,1664]{2,1,0:T(8,128)(2,1)S(1)}, u32[]{:S(2)}, u32[]{:S(2)}) collective-permute-start(bf16[4,64,1664]{2,1,0:T(8,128)(2,1)S(1)} %pad_maximum_fusion.6), channel_id=1, source_target_pairs={{0,24},{8,0},{16,8},{24,16},{32,56},{40,32},{48,40},{56,48},{64,88... | collective-permute-start | bytes 2555912 | tf_op jit(solution)/shard_map/ppermute | solution.py:138
  33.0 25.3 %collective-permute-start.11 = (bf16[4,64,1664]{2,1,0:T(8,128)(2,1)S(1)}, bf16[4,64,1664]{2,1,0:T(8,128)(2,1)S(1)}, u32[]{:S(2)}, u32[]{:S(2)}) collective-permute-start(bf16[4,64,1664]{2,1,0:T(8,128)(2,1)S(1)} %pad_maximum_fusion.6), channel_id=1, source_target_pairs={{0,16},{8,24},{16,0},{24,8},{32,48},{40,56},{48,32},{56,40},{64,80... | collective-permute-start | bytes 2555912 | tf_op jit(solution)/shard_map/ppermute | solution.py:138
  36.2 38.5 %collective-permute-start.9 = (bf16[4,64,1664]{2,1,0:T(8,128)(2,1)S(1)}, bf16[4,64,1664]{2,1,0:T(8,128)(2,1)}, u32[]{:S(2)}, u32[]{:S(2)}) collective-permute-start(bf16[4,64,1664]{2,1,0:T(8,128)(2,1)S(1)} %pad_maximum_fusion.6), channel_id=1, source_target_pairs={{0,8},{8,16},{16,24},{24,0},{32,40},{40,48},{48,56},{56,32},{64,72... | collective-permute-start | bytes 2555912 | tf_op jit(solution)/shard_map/ppermute | solution.py:138
  75.6 248.5 %all-gather.15.cloned.1.call-start = ((), (), s32[]{:S(2)}) async-start(), calls=%async_computation.12 | async-start | bytes 10027008 | tf_op jit(solution)/shard_map/all_gather | solution.py:234
  158.1 31.5 %collective-permute-start.12 = (bf16[8,96,1536]{2,1,0:T(8,128)(2,1)S(1)}, bf16[8,96,1536]{2,1,0:T(8,128)(2,1)}, u32[]{:S(2)}, u32[]{:S(2)}) collective-permute-start(bf16[8,96,1536]{2,1,0:T(8,128)(2,1)S(1)} %bitcast.334), channel_id=1, source_target_pairs={{0,128},{128,0},{1,129},{129,1},{2,130},{130,2},{3,131},{131,3},{4... | collective-permute-start | bytes 7077896 | tf_op jit(solution)/shard_map/ppermute | solution.py:146
  170.1 374.9 %all-gather.17.cloned.1.call-start = ((), (), s32[]{:S(2)}) async-start(), calls=%async_computation.13 | async-start | bytes 4423680 | tf_op jit(solution)/shard_map/all_gather | solution.py:226
  220.1 45.3 %collective-permute-start.16 = (bf16[4,64,1664]{2,1,0:T(8,128)(2,1)}, bf16[4,64,1664]{2,1,0:T(8,128)(2,1)}, u32[]{:S(2)}, u32[]{:S(2)}) collective-permute-start(bf16[4,64,1664]{2,1,0:T(8,128)(2,1)} %copy.203), channel_id=1, source_target_pairs={{0,32},{8,40},{16,48},{24,56},{32,64},{40,72},{48,80},{56,88},{64,... | collective-permute-start | bytes 2555912 | tf_op jit(solution)/shard_map/ppermute | solution.py:138
  221.4 26.5 %collective-permute-start.19 = (bf16[64,1664]{0,1:T(8,128)(2,1)}, bf16[64,1664]{0,1:T(8,128)(2,1)S(1)}, u32[]{:S(2)}, u32[]{:S(2)}) collective-permute-start(bf16[64,1664]{0,1:T(8,128)(2,1)} %get-tuple-element.150), channel_id=1, source_target_pairs={{0,32},{8,40},{16,48},{24,56},{32,64},{40,72},{48,80},{56,88},{64,... | collective-permute-start | bytes 638984 | tf_op jit(solution)/shard_map/ppermute | solution.py:138
  222.6 26.9 %collective-permute-start.20 = (bf16[64,1664]{0,1:T(8,128)(2,1)}, bf16[64,1664]{0,1:T(8,128)(2,1)S(1)}, u32[]{:S(2)}, u32[]{:S(2)}) collective-permute-start(bf16[64,1664]{0,1:T(8,128)(2,1)} %get-tuple-element.150), channel_id=1, source_target_pairs={{0,96},{8,104},{16,112},{24,120},{32,0},{40,8},{48,16},{56,24},{64... | collective-permute-start | bytes 638984 | tf_op jit(solution)/shard_map/ppermute | solution.py:138
  224.1 33.9 %collective-permute-start.21 = (bf16[64,1664]{0,1:T(8,128)(2,1)}, bf16[64,1664]{0,1:T(8,128)(2,1)S(1)}, u32[]{:S(2)}, u32[]{:S(2)}) collective-permute-start(bf16[64,1664]{0,1:T(8,128)(2,1)} %get-tuple-element.150), channel_id=1, source_target_pairs={{0,64},{8,72},{16,80},{24,88},{32,96},{40,104},{48,112},{56,120},{... | collective-permute-start | bytes 638984 | tf_op jit(solution)/shard_map/ppermute | solution.py:138
  228.6 48.1 %collective-permute-start.17 = (bf16[4,64,1664]{2,1,0:T(8,128)(2,1)}, bf16[4,64,1664]{2,1,0:T(8,128)(2,1)}, u32[]{:S(2)}, u32[]{:S(2)}) collective-permute-start(bf16[4,64,1664]{2,1,0:T(8,128)(2,1)} %copy.203), channel_id=1, source_target_pairs={{0,96},{8,104},{16,112},{24,120},{32,0},{40,8},{48,16},{56,24},{64... | collective-permute-start | bytes 2555912 | tf_op jit(solution)/shard_map/ppermute | solution.py:138
  247.9 31.3 %collective-permute-start.18 = (bf16[4,64,1664]{2,1,0:T(8,128)(2,1)}, bf16[4,64,1664]{2,1,0:T(8,128)(2,1)}, u32[]{:S(2)}, u32[]{:S(2)}) collective-permute-start(bf16[4,64,1664]{2,1,0:T(8,128)(2,1)} %copy.203), channel_id=1, source_target_pairs={{0,64},{8,72},{16,80},{24,88},{32,96},{40,104},{48,112},{56,120},{... | collective-permute-start | bytes 2555912 | tf_op jit(solution)/shard_map/ppermute | solution.py:138
  265.5 27.6 %collective-permute-start.24 = (bf16[4,64,1664]{2,1,0:T(8,128)(2,1)}, bf16[4,64,1664]{2,1,0:T(8,128)(2,1)}, u32[]{:S(2)}, u32[]{:S(2)}) collective-permute-start(bf16[4,64,1664]{2,1,0:T(8,128)(2,1)} %copy.209), channel_id=1, source_target_pairs={{0,16},{8,24},{16,0},{24,8},{32,48},{40,56},{48,32},{56,40},{64,80... | collective-permute-start | bytes 2555912 | tf_op jit(solution)/shard_map/ppermute | solution.py:138
  400.4 138.5 %collective-permute-start.37 = (bf16[8,2,288,512]{3,2,1,0:T(8,128)(2,1)}, bf16[8,2,288,512]{3,2,1,0:T(8,128)(2,1)}, u32[]{:S(2)}, u32[]{:S(2)}) collective-permute-start(bf16[8,2,288,512]{3,2,1,0:T(8,128)(2,1)} %bitcast.321), channel_id=1, source_target_pairs={{0,128},{128,0},{1,129},{129,1},{2,130},{130,2},{3,131},{131,3},{4... | collective-permute-start | bytes 14155784 | tf_op jit(solution)/shard_map/ppermute | solution.py:146
  423.6 186.2 %reduce-scatter.5.cloned.1.call-start = ((), (), s32[]{:S(2)}) async-start(), calls=%async_computation.9 | async-start | bytes 5308416 | tf_op jit(solution)/shard_map/reduce_scatter | solution.py:379
  443.1 26.3 %collective-permute-start.25 = (bf16[4,64,1664]{2,1,0:T(8,128)(2,1)}, bf16[4,64,1664]{2,1,0:T(8,128)(2,1)}, u32[]{:S(2)}, u32[]{:S(2)}) collective-permute-start(bf16[4,64,1664]{2,1,0:T(8,128)(2,1)} %get-tuple-element.120), channel_id=1, source_target_pairs={{0,96},{8,104},{16,112},{24,120},{32,0},{40,8},{48,16},{56,24},{64... | collective-permute-start | bytes 2555912 | tf_op jit(solution)/shard_map/ppermute | solution.py:138
  443.1 30.1 %collective-permute-start.26 = (bf16[4,64,1664]{2,1,0:T(8,128)(2,1)}, bf16[4,64,1664]{2,1,0:T(8,128)(2,1)}, u32[]{:S(2)}, u32[]{:S(2)}) collective-permute-start(bf16[4,64,1664]{2,1,0:T(8,128)(2,1)} %get-tuple-element.119), channel_id=1, source_target_pairs={{0,32},{8,40},{16,48},{24,56},{32,64},{40,72},{48,80},{56,88},{64,... | collective-permute-start | bytes 2555912 | tf_op jit(solution)/shard_map/ppermute | solution.py:138
  444.6 36.2 %collective-permute-start.27 = (bf16[4,64,1664]{2,1,0:T(8,128)(2,1)}, bf16[4,64,1664]{2,1,0:T(8,128)(2,1)}, u32[]{:S(2)}, u32[]{:S(2)}) collective-permute-start(bf16[4,64,1664]{2,1,0:T(8,128)(2,1)} %get-tuple-element.118), channel_id=1, source_target_pairs={{0,64},{8,72},{16,80},{24,88},{32,96},{40,104},{48,112},{56,120},{... | collective-permute-start | bytes 2555912 | tf_op jit(solution)/shard_map/ppermute | solution.py:138
  450.4 39.0 %collective-permute-start.31 = (bf16[4,64,1664]{2,1,0:T(8,128)(2,1)}, bf16[4,64,1664]{2,1,0:T(8,128)(2,1)}, u32[]{:S(2)}, u32[]{:S(2)}) collective-permute-start(bf16[4,64,1664]{2,1,0:T(8,128)(2,1)} %get-tuple-element.124), channel_id=1, source_target_pairs={{0,24},{8,0},{16,8},{24,16},{32,56},{40,32},{48,40},{56,48},{64,88... | collective-permute-start | bytes 2555912 | tf_op jit(solution)/shard_map/ppermute | solution.py:138
  469.4 23.8 %collective-permute-start.32 = (bf16[4,64,1664]{2,1,0:T(8,128)(2,1)}, bf16[4,64,1664]{2,1,0:T(8,128)(2,1)}, u32[]{:S(2)}, u32[]{:S(2)}) collective-permute-start(bf16[4,64,1664]{2,1,0:T(8,128)(2,1)} %get-tuple-element.123), channel_id=1, source_target_pairs={{0,8},{8,16},{16,24},{24,0},{32,40},{40,48},{48,56},{56,32},{64,72... | collective-permute-start | bytes 2555912 | tf_op jit(solution)/shard_map/ppermute | solution.py:138
  473.2 32.6 %collective-permute-start.33 = (bf16[4,64,1664]{2,1,0:T(8,128)(2,1)}, bf16[4,64,1664]{2,1,0:T(8,128)(2,1)}, u32[]{:S(2)}, u32[]{:S(2)}) collective-permute-start(bf16[4,64,1664]{2,1,0:T(8,128)(2,1)} %get-tuple-element.122), channel_id=1, source_target_pairs={{0,16},{8,24},{16,0},{24,8},{32,48},{40,56},{48,32},{56,40},{64,80... | collective-permute-start | bytes 2555912 | tf_op jit(solution)/shard_map/ppermute | solution.py:138
  489.2 25.0 %collective-permute-start.28 = (bf16[64,1664]{0,1:T(8,128)(2,1)}, bf16[64,1664]{0,1:T(8,128)(2,1)}, u32[]{:S(2)}, u32[]{:S(2)}) collective-permute-start(bf16[64,1664]{0,1:T(8,128)(2,1)} %get-tuple-element.127), channel_id=1, source_target_pairs={{0,24},{8,0},{16,8},{24,16},{32,56},{40,32},{48,40},{56,48},{64,88... | collective-permute-start | bytes 638984 | tf_op jit(solution)/shard_map/ppermute | solution.py:138
  489.5 37.6 %collective-permute-start.29 = (bf16[64,1664]{0,1:T(8,128)(2,1)S(1)}, bf16[64,1664]{0,1:T(8,128)(2,1)}, u32[]{:S(2)}, u32[]{:S(2)}) collective-permute-start(bf16[64,1664]{0,1:T(8,128)(2,1)S(1)} %get-tuple-element.129), channel_id=1, source_target_pairs={{0,8},{8,16},{16,24},{24,0},{32,40},{40,48},{48,56},{56,32},{64,72... | collective-permute-start | bytes 638984 | tf_op jit(solution)/shard_map/ppermute | solution.py:138
  493.3 36.2 %collective-permute-start.30 = (bf16[64,1664]{0,1:T(8,128)(2,1)S(1)}, bf16[64,1664]{0,1:T(8,128)(2,1)}, u32[]{:S(2)}, u32[]{:S(2)}) collective-permute-start(bf16[64,1664]{0,1:T(8,128)(2,1)S(1)} %get-tuple-element.128), channel_id=1, source_target_pairs={{0,16},{8,24},{16,0},{24,8},{32,48},{40,56},{48,32},{56,40},{64,80... | collective-permute-start | bytes 638984 | tf_op jit(solution)/shard_map/ppermute | solution.py:138
  545.0 128.0 %all-gather.11.cloned.1.call-start = ((), (), s32[]{:S(2)}) async-start(), calls=%async_computation.10 | async-start | bytes 3538944 | tf_op jit(solution)/shard_map/all_gather | solution.py:396
  558.5 246.4 %reduce-scatter.7.cloned.1.call-start = ((), (), s32[]{:S(2)}) async-start(), calls=%async_computation.14 | async-start | bytes 6684672
  558.6 126.2 %collective-permute-start.38 = (bf16[8,160,1536]{2,1,0:T(8,128)(2,1)}, bf16[8,160,1536]{2,1,0:T(8,128)(2,1)}, u32[]{:S(2)}, u32[]{:S(2)}) collective-permute-start(bf16[8,160,1536]{2,1,0:T(8,128)(2,1)} %bitcast.352), channel_id=1, source_target_pairs={{0,128},{128,0},{1,129},{129,1},{2,130},{130,2},{3,131},{131,3},{4... | collective-permute-start | bytes 11796488 | tf_op jit(solution)/shard_map/ppermute | solution.py:146
  630.6 54.2 %all-to-all-start.2 = ((bf16[8,128,320]{1,2,0:T(8,128)(2,1)}), bf16[8,128,320]{1,2,0:T(8,128)(2,1)}, u32[]{:S(2)}, u32[]{:S(2)}) async-start(bf16[8,128,320]{1,2,0:T(8,128)(2,1)} %copy_bitcast_fusion.1), calls=%async_computation.3 | async-start | bytes 1310720 | tf_op jit(solution)/shard_map/all_to_all | solution.py:393
  735.8 33.4 %all-to-all-start.4 = ((bf16[32,208,128]{2,1,0:T(8,128)(2,1)}), bf16[32,208,128]{2,1,0:T(8,128)(2,1)S(1)}, u32[]{:S(2)}, u32[]{:S(2)}) async-start(bf16[32,208,128]{2,1,0:T(8,128)(2,1)} %broadcast_in_dim.68), calls=%async_computation.5 | async-start | bytes 3407872 | tf_op jit(solution)/shard_map/all_to_all | solution.py:419
  770.4 29.4 %all-to-all-start.5 = ((bf16[8,408,128]{2,1,0:T(8,128)(2,1)}), bf16[8,408,128]{2,1,0:T(8,128)(2,1)}, u32[]{:S(2)}, u32[]{:S(2)}) async-start(bf16[8,408,128]{2,1,0:T(8,128)(2,1)} %broadcast_in_dim.69), calls=%async_computation.6 | async-start | bytes 1671168 | tf_op jit(solution)/shard_map/all_to_all | solution.py:427
  (104 other events, 1969.4 us)
Sparse Core Ops, SparseCore 0:
  11.6 55.4 all-gather.8
  75.7 67.0 all-gather.12
  144.6 71.3 all-gather.14
  423.7 45.1 all-gather.16
  545.1 64.5 reduce-scatter.4
  611.9 61.1 all-gather.10
  676.8 115.4 reduce-scatter.6

commit v2 on v1

--- a/solution.py
+++ b/solution.py
@@ -1,12 +1,16 @@
 import jax
 import jax.numpy as jnp
 from jax import lax
+from jax.experimental import pallas as pl
+from jax.experimental.layout import Layout, with_layout_constraint
+from jax.experimental.pallas import tpu as pltpu
 from jax.sharding import PartitionSpec as P
 
 HEAD_DIM = 64
 HALF = HEAD_DIM // 2
 TOP = 8
 CAP = 64
+EXPERTS = 32
 LANES = 128
 
 epsilon_norm = 1e-06
@@ -121,21 +125,39 @@
 STEPS = (0, 1, -1, 2)
 
 
-def owner_of(place, me):
-    return jnp.asarray([0, 2, 3, 1])[(place - me) % SIDE]
-
-
-def along(axis, step):
+def by_rows(values):
+    return with_layout_constraint(values, Layout(major_to_minor=tuple(range(values.ndim))))
+
+
+def cross(values, stage, step):
     pairs = []
-    for a in range(SIDE):
-        for b in range(SIDE):
-            to = ((a + step) % SIDE, b) if axis == 0 else (a, (b + step) % SIDE)
-            pairs.append((a * SIDE + b, to[0] * SIDE + to[1]))
-    return pairs
-
-
-def move(values, axis, step):
-    return lax.ppermute(values, "expert", along(axis, step))
+    plane = SIDE * SIDE
+    for core in range(2):
+        for x in range(SIDE):
+            for y in range(SIDE):
+                if core == stage:
+                    to = x * SIDE + (y + step) % SIDE
+                else:
+                    to = (x + step) % SIDE * SIDE + y
+                pairs.append((core * plane + x * SIDE + y, core * plane + to))
+    return lax.ppermute(values, ("dp", "expert"), pairs)
+
+
+def gather_plane(values):
+    values = by_rows(values)
+    line = jnp.stack([values] + [cross(values, 0, step) for step in STEPS[1:]])
+    line = by_rows(line)
+    return [line] + [cross(line, 1, step) for step in STEPS[1:]]
+
+
+def scatter_plane(parts):
+    arrived = [parts[0]] + [by_rows(cross(part, 1, -step)) for part, step in zip(parts[1:], STEPS[1:])]
+    line = [
+        by_rows(sum(part[place].astype(f32) for part in arrived).astype(bf16))
+        for place in range(SIDE)
+    ]
+    arrived = [line[0]] + [cross(part, 0, -step) for part, step in zip(line[1:], STEPS[1:])]
+    return by_rows(sum(part.astype(f32) for part in arrived))
 
 
 def together(*values):
@@ -146,30 +168,186 @@
     return lax.ppermute(values, "dp", [(0, 1), (1, 0)])
 
 
-def line_gather(values, axis):
-    return [values] + [move(values, axis, step) for step in STEPS[1:]]
-
-
-def gather_plane(values):
-    half = values.shape[0] // 2
-    first = line_gather(jnp.stack(line_gather(values[:half], 1)), 0)
-    second = line_gather(jnp.stack(line_gather(values[half:], 0)), 1)
-    return first, second
-
-
-def line_scatter(parts, axis):
-    total = parts[0].astype(f32)
-    for part, step in zip(parts[1:], STEPS[1:]):
-        total = total + move(part, axis, -step).astype(f32)
-    return total.astype(bf16)
-
-
-def scatter_plane(first, second):
-    first = line_scatter(first, 0)
-    second = line_scatter(second, 1)
-    first = line_scatter([first[i] for i in range(SIDE)], 1)
-    second = line_scatter([second[i] for i in range(SIDE)], 0)
-    return jnp.concatenate([first, second], axis=0)
+def contract(left, right, left_dim, right_dim):
+    return lax.dot_general(
+        left, right, (((left_dim,), (right_dim,)), ((), ())), preferred_element_type=f32
+    )
+
+
+def expert_kernel(
+    first_ref, rows_ref, cots_ref, w_ref, out_ref, x_ref, c_ref, gate_ref, up_ref, hid_ref, *scratch
+):
+    pick_ref, down_ref, back_ref, gates_ref = scratch
+    sources, tokens, _ = rows_ref.shape
+    pair = 2 * CAP
+    width = x_ref.shape[2]
+    inner = w_ref.shape[2]
+    experts = EXPERTS
+    first = first_ref[0]
+    lane = lax.broadcasted_iota(jnp.int32, (pair, LANES), 1)
+    expert_of = first + lax.broadcasted_iota(jnp.int32, (pair, LANES), 0) // CAP
+    own_high = lane == expert_of
+    own_low = lane == expert_of + experts
+    row_id = lax.broadcasted_iota(jnp.int32, (experts, tokens), 0)
+    slot = lax.broadcasted_iota(jnp.int32, (pair, tokens), 0)
+    for source in range(sources):
+        table = cots_ref[source, :experts, width:].astype(f32)
+        ranks = [
+            jnp.sum(jnp.where(row_id == first + e, table, 0.0), axis=0, keepdims=True)
+            for e in range(2)
+        ]
+        rank = jnp.where(slot < CAP, ranks[0], ranks[1])
+        pick = (rank == (slot % CAP).astype(f32)).astype(bf16)
+        pick_ref[source] = pick
+        rows = jnp.dot(pick, rows_ref[source], preferred_element_type=f32)
+        cots = jnp.dot(pick, cots_ref[source, :, :width], preferred_element_type=f32)
+        gate = jnp.sum(jnp.where(own_high | own_low, rows[:, width:], 0.0), axis=1, keepdims=True)
+        place = slice(source * CAP, (source + 1) * CAP)
+        for e in range(2):
+            part = slice(e * CAP, (e + 1) * CAP)
+            x_ref[e, place] = rows[part, :width].astype(bf16)
+            c_ref[e, place] = cots[part].astype(bf16)
+            gates_ref[e, place] = jnp.broadcast_to(gate[part], (CAP, LANES))
+
+    down_rows = inner // 16
+    chunks = width // inner
+    for e in range(2):
+        for holder in range(16):
+            for chunk in range(chunks):
+                at = (holder * chunks + chunk) * down_rows
+                down_ref[
+                    e,
+                    holder * down_rows : (holder + 1) * down_rows,
+                    chunk * inner : (chunk + 1) * inner,
+                ] = w_ref[4 + e, at : at + down_rows, :]
+
+    def one_expert(e, carry):
+        x = x_ref[e]
+        cot = c_ref[e]
+        gate = gates_ref[e][:, :1]
+        gate_pre = jnp.dot(x, w_ref[e], preferred_element_type=f32)
+        up_pre = jnp.dot(x, w_ref[2 + e], preferred_element_type=f32)
+        back = contract(cot, down_ref[e], 1, 1)
+        sig = 1.0 / (1.0 + jnp.exp(-gate_pre))
+        silu = gate_pre * sig
+        hidden = (silu * up_pre).astype(bf16)
+        gate_grad = jnp.sum(back * hidden.astype(f32), axis=1, keepdims=True)
+        grad = gate * back
+        gate_pre_grad = (grad * up_pre * (sig + silu * (1.0 - sig))).astype(bf16)
+        up_pre_grad = (grad * silu).astype(bf16)
+        gate_ref[e] = gate_pre_grad
+        up_ref[e] = up_pre_grad
+        hid_ref[e] = (gate * hidden.astype(f32)).astype(bf16)
+        row_grad = contract(gate_pre_grad, w_ref[e], 1, 1) + contract(
+            up_pre_grad, w_ref[2 + e], 1, 1
+        )
+        mixed = gate * jnp.dot(hidden, down_ref[e], preferred_element_type=f32)
+        high = gate_grad.astype(bf16).astype(f32)
+        lane = lax.broadcasted_iota(jnp.int32, (gate_grad.shape[0], LANES), 1)
+        tail = jnp.where(lane == first + e, high, 0.0) + jnp.where(
+            lane == first + e + experts, gate_grad - high, 0.0
+        )
+        for source in range(sources):
+            place = slice(source * CAP, (source + 1) * CAP)
+            to = pl.ds(pl.multiple_of(e * CAP, CAP), CAP)
+            back_ref[source, to, :width] = row_grad[place].astype(bf16)
+            back_ref[source, to, width : 2 * width] = mixed[place].astype(bf16)
+            back_ref[source, to, 2 * width :] = tail[place].astype(bf16)
+        return carry
+
+    lax.fori_loop(0, 2, one_expert, 0)
+    for source in range(sources):
+        out_ref[source] = contract(pick_ref[source], back_ref[source], 0, 0).astype(bf16)
+
+
+def run_experts(first, rows, cots, weights):
+    sources, tokens, padded = rows.shape
+    width = padded - LANES
+    inner = weights.shape[2]
+    slots = sources * CAP
+    vmem = pl.BlockSpec(memory_space=pltpu.VMEM)
+    acts = jax.ShapeDtypeStruct((2, slots, inner), bf16)
+    wide = jax.ShapeDtypeStruct((2, slots, width), bf16)
+    return pl.pallas_call(
+        expert_kernel,
+        out_shape=(
+            jax.ShapeDtypeStruct((sources, tokens, 2 * width + LANES), bf16),
+            wide,
+            wide,
+            acts,
+            acts,
+            acts,
+        ),
+        in_specs=[pl.BlockSpec(memory_space=pltpu.SMEM), vmem, vmem, vmem],
+        out_specs=(vmem,) * 6,
+        scratch_shapes=[
+            pltpu.VMEM((sources, 2 * CAP, tokens), bf16),
+            pltpu.VMEM((2, inner, width), bf16),
+            pltpu.VMEM((sources, 2 * CAP, 2 * width + LANES), bf16),
+            pltpu.VMEM((2, slots, LANES), f32),
+        ],
+        compiler_params=pltpu.CompilerParams(vmem_limit_bytes=50 * 1024 * 1024),
+        cost_estimate=pl.CostEstimate(
+            flops=2 * 2 * 7 * slots * width * inner, bytes_accessed=24 << 20, transcendentals=0
+        ),
+    )(first, rows, cots, weights)
+
+
+def weight_grad_kernel(half_ref, *refs):
+    groups = SIDE
+    x_refs, c_refs, gate_refs, up_refs, hid_refs = (
+        refs[i * groups : (i + 1) * groups] for i in range(5)
+    )
+    out_ref = refs[5 * groups]
+    slots, width = x_refs[0].shape[1:]
+    inner = gate_refs[0].shape[2]
+    half = half_ref[0]
+    rows = width // 2
+    cols = pl.ds(pl.multiple_of(half * rows, LANES), rows)
+    down_cols = pl.ds(pl.multiple_of(half * (inner // 2), LANES), inner // 2)
+    down_rows = inner // 16
+    chunks = width // inner
+
+    def one_expert(e, carry):
+        gate = jnp.zeros((rows, inner), f32)
+        up = jnp.zeros((rows, inner), f32)
+        down = jnp.zeros((inner // 2, width), f32)
+        for i in range(groups):
+            x = x_refs[i][e, :, cols]
+            gate += contract(x, gate_refs[i][e], 0, 0)
+            up += contract(x, up_refs[i][e], 0, 0)
+        out_ref[e] = gate.astype(bf16)
+        out_ref[2 + e] = up.astype(bf16)
+        for i in range(groups):
+            down += contract(hid_refs[i][e, :, down_cols], c_refs[i][e], 0, 0)
+        for holder in range(8):
+            for chunk in range(chunks):
+                at = (holder * chunks + chunk) * down_rows
+                out_ref[4 + e, at : at + down_rows, :] = down[
+                    holder * down_rows : (holder + 1) * down_rows,
+                    chunk * inner : (chunk + 1) * inner,
+                ].astype(bf16)
+        return carry
+
+    lax.fori_loop(0, 2, one_expert, 0)
+
+
+def run_weight_grads(half, saved):
+    x, c, gate, up, hid = zip(*saved)
+    slots, width = x[0].shape[1:]
+    inner = gate[0].shape[2]
+    vmem = pl.BlockSpec(memory_space=pltpu.VMEM)
+    operands = (*x, *c, *gate, *up, *hid)
+    return pl.pallas_call(
+        weight_grad_kernel,
+        out_shape=jax.ShapeDtypeStruct((6, width // 2, inner), bf16),
+        in_specs=[pl.BlockSpec(memory_space=pltpu.SMEM)] + [vmem] * len(operands),
+        out_specs=vmem,
+        compiler_params=pltpu.CompilerParams(vmem_limit_bytes=50 * 1024 * 1024),
+        cost_estimate=pl.CostEstimate(
+            flops=2 * 3 * 4 * slots * width * inner, bytes_accessed=24 << 20, transcendentals=0
+        ),
+    )(half, *operands)
 
 
 def local(
@@ -206,6 +384,7 @@
     inverse_one = rms_inverse(token_f32)
     normed_low = (token_f32 * inverse_one * norm1_gain).astype(bf16)
     joined_weights = jnp.concatenate([w_query, w_key, w_value], axis=1)
+    normed_low = by_rows(normed_low)
     normed_all = lax.all_gather(normed_low, "tensor", axis=0, tiled=True)
     core = lax.axis_index("dp")
 
@@ -218,20 +397,23 @@
     extra = jnp.pad(rank, ((0, tok_rows - experts), (0, LANES - tok_rows)))
     cot_payload = jnp.concatenate([cotangent, extra], axis=1)
 
-    cot_halves = gather_plane(cot_payload)
+    cot_parts = gather_plane(cot_payload)
 
     def half_gather(shard):
         count = shard.shape[0] // 2
         half = lax.dynamic_slice_in_dim(shard, core * count, count, 0)
         return lax.all_gather(half, "tensor", axis=0)
 
-    normed_all, cot_halves, w_out = together(normed_all, cot_halves, w_out)
+    normed_all, cot_parts, w_out = together(normed_all, cot_parts, w_out)
     half_out = half_gather(w_out)
-    weights = jnp.concatenate(
-        [w_gate, w_up, w_down.reshape(local_experts, -1, hidden_width)], axis=1
-    )
+    chunks = width // hidden_width
+    down_rows = w_down.shape[1]
+    part_rows = w_gate.shape[1]
+    down_parts = w_down.reshape(local_experts, down_rows, chunks, hidden_width)
+    down_parts = down_parts.transpose(0, 2, 1, 3).reshape(local_experts, part_rows, hidden_width)
+    weights = jnp.concatenate([w_gate, w_up, down_parts], axis=0)
     half_out, weights = together(half_out, weights)
-    weights_all = lax.all_gather(weights, ("dp", "tensor"), axis=0)
+    weights_all = lax.all_gather(weights, ("dp", "tensor"), axis=1, tiled=True)
     weights_all, joined_rows = together(weights_all, joined_weights.T)
     half_joined = half_gather(joined_rows)
 
@@ -264,109 +446,34 @@
         [normed_two, gate_high, gate_low, jnp.zeros((tok_rows, LANES - 2 * experts), bf16)],
         axis=1,
     )
-    rows_halves = gather_plane(payload)
-
-    def whole(halves):
-        first, second = halves
-        first = jnp.stack(first)
-        second = jnp.stack(second).transpose(1, 0, 2, 3)
-        return jnp.concatenate([first, second], axis=2).reshape(owners, tok_rows, width + LANES)
-
-    cot_all = whole(cot_halves)
-    rows_all = whole(rows_halves)
-    ranks = lax.dynamic_slice_in_dim(
-        cot_all[:, :experts, width : width + tok_rows], first_expert, local_experts, 1
-    )
-    slots = jnp.arange(CAP, dtype=f32)
-    pick = (ranks[:, :, None, :].astype(f32) == slots[:, None]).astype(bf16)
-    rows = jnp.einsum("sect,std->secd", pick, rows_all, preferred_element_type=f32).astype(bf16)
-    cots = jnp.einsum(
-        "sect,std->secd", pick, cot_all[:, :, :width], preferred_element_type=f32
-    ).astype(bf16)
-    lane = jnp.arange(LANES, dtype=jnp.int32)
-    mine = first_expert + jnp.arange(local_experts, dtype=jnp.int32)[:, None]
-    mine_mask = ((lane == mine) | (lane == mine + experts)).astype(f32)
-    gate_col = jnp.sum(
-        rows[..., width:].astype(f32) * mine_mask[:, None, :], axis=-1, keepdims=True
-    )
-    rows = rows[..., :width]
-
-    group = weights_all.shape[0]
-    part_rows = w_gate.shape[1]
-    down_rows = w_down.shape[1]
-    full_gate = weights_all[:, :, :part_rows].transpose(1, 0, 2, 3).reshape(
-        local_experts, group * part_rows, hidden_width
-    )
-    full_up = weights_all[:, :, part_rows : 2 * part_rows].transpose(1, 0, 2, 3).reshape(
-        local_experts, group * part_rows, hidden_width
-    )
-    full_down = (
-        weights_all[:, :, 2 * part_rows :]
-        .transpose(1, 0, 2, 3)
-        .reshape(local_experts, group * down_rows, width)
-    )
-    gate_pre = jnp.einsum("secd,edf->secf", rows, full_gate, preferred_element_type=f32)
-    up_pre = jnp.einsum("secd,edf->secf", rows, full_up, preferred_element_type=f32)
-    gate_sig = jax.nn.sigmoid(gate_pre)
-    silu = gate_pre * gate_sig
-    hidden = (silu * up_pre).astype(bf16)
-    back = jnp.einsum("secd,efd->secf", cots, full_down, preferred_element_type=f32)
-    gate_grad = jnp.sum(back * hidden.astype(f32), axis=-1, keepdims=True)
-    hidden_grad = gate_col * back
-    gate_pre_grad = (hidden_grad * up_pre * (gate_sig + silu * (1.0 - gate_sig))).astype(bf16)
-    up_pre_grad = (hidden_grad * silu).astype(bf16)
-    row_grads = jnp.einsum("secf,edf->secd", gate_pre_grad, full_gate, preferred_element_type=f32)
-    row_grads = row_grads + jnp.einsum(
-        "secf,edf->secd", up_pre_grad, full_up, preferred_element_type=f32
-    )
-    grad_high, grad_low = split_two(gate_grad)
-    high_mask = (lane == mine)[:, None, :]
-    low_mask = (lane == mine + experts)[:, None, :]
-    tail = jnp.where(high_mask, grad_high, jnp.where(low_mask, grad_low, jnp.zeros((), bf16)))
-    row_grads = jnp.concatenate([row_grads.astype(bf16), tail], axis=-1)
-    back_part = jnp.einsum("sect,secd->std", pick, row_grads, preferred_element_type=f32)
-    back_part = back_part.astype(bf16).reshape(SIDE, SIDE, tok_rows, width + LANES)
-    half = tok_rows // 2
-    back_home = scatter_plane(
-        [back_part[i, :, :half] for i in range(SIDE)],
-        [back_part[:, i, half:] for i in range(SIDE)],
-    )
-
-    expert_out = jnp.einsum("secf,efd->secd", hidden, full_down, preferred_element_type=f32)
-    mixture_part = jnp.einsum(
-        "sect,secd->std", pick, (gate_col * expert_out).astype(bf16), preferred_element_type=f32
-    )
-    place = (owner_of(jnp.arange(SIDE), owner // SIDE)[:, None] * SIDE) + owner_of(
-        jnp.arange(SIDE), owner % SIDE
-    )
-    gate_w = jnp.einsum("secd,secf->edf", rows, gate_pre_grad, preferred_element_type=f32)
-    up_w = jnp.einsum("secd,secf->edf", rows, up_pre_grad, preferred_element_type=f32)
-    scaled_hidden = (gate_col * hidden.astype(f32)).astype(bf16)
-    down_w = jnp.einsum("secf,secd->efd", scaled_hidden, cots, preferred_element_type=f32)
-
-    def by_holder(part):
-        return part.astype(bf16).reshape(local_experts, group, -1, hidden_width)
-
-    weight_part = jnp.concatenate([by_holder(gate_w), by_holder(up_w), by_holder(down_w)], axis=2)
-    weight_part = weight_part.transpose(1, 0, 2, 3)
-    kept = lax.dynamic_slice_in_dim(weight_part, core * planes, planes, 0)
-    given = lax.dynamic_slice_in_dim(weight_part, (1 - core) * planes, planes, 0)
+    rows_parts = gather_plane(payload)
+
+    first_expert = first_expert.astype(jnp.int32).reshape(1)
+    done = [
+        run_experts(first_expert, rows, cots, weights_all)
+        for rows, cots in zip(rows_parts, cot_parts)
+    ]
+    back_home = scatter_plane([part[0] for part in done])
+    saved_rows = [part[1:] for part in done]
+    given = run_weight_grads((1 - core).astype(jnp.int32).reshape(1), saved_rows)
+    kept = run_weight_grads(core.astype(jnp.int32).reshape(1), saved_rows)
     kept = (kept.astype(f32) + swap_cores(given).astype(f32)).astype(bf16)
-    back_home, mixture_part, kept, half_joined = together(
-        back_home, mixture_part.astype(bf16)[place.reshape(-1)], kept, half_joined
-    )
+    weight_sum = lax.psum_scatter(kept, "tensor", scatter_dimension=1, tiled=True)
+    back_home, kept, half_joined = together(back_home, kept, half_joined)
+    output = (mid + back_home[:, width : 2 * width]).astype(bf16)
+
     cot_f32 = cotangent.astype(f32)
-    grad_tail = back_home[:, width:].astype(f32)
+    grad_tail = back_home[:, 2 * width :]
     gate_grad = grad_tail[:, :experts] + grad_tail[:, experts : 2 * experts]
     chosen_grad = gates * (gate_grad - jnp.sum(gates * gate_grad, axis=1, keepdims=True))
     logit_grad = chosen_grad.astype(bf16)
     router_part = jnp.einsum("td,te->de", normed_two, logit_grad, preferred_element_type=f32)
-    normed_two_grad = back_home[:, :width].astype(f32) + jnp.einsum(
+    normed_two_grad = back_home[:, :width] + jnp.einsum(
         "te,de->td", logit_grad, w_router, preferred_element_type=f32
     )
     mid_part, norm2_part = rms_backward(mid, inverse_two, norm2_gain, normed_two_grad)
     mid_grad = cot_f32 + mid_part
-    attention_low = mid_grad.astype(bf16)
+    attention_low = by_rows(mid_grad.astype(bf16))
     def both_back(rows, mine, other):
         first = jnp.einsum("td,jqd->jtq", rows, mine, preferred_element_type=f32)
         second = jnp.einsum("td,jqd->jtq", rows, other, preferred_element_type=f32)
@@ -376,20 +483,9 @@
 
     context_grad = both_back(attention_low, half_out, other_out)
     context_grad = lax.all_to_all(context_grad, "tensor", split_axis=0, concat_axis=0)
-    weight_sum = lax.psum_scatter(kept, "tensor", scatter_dimension=0, tiled=True)[0].astype(f32)
-    mixture_part, weight_sum = together(mixture_part, weight_sum)
-    mixture = lax.psum_scatter(
-        mixture_part.reshape(owners * tok_rows, width), "expert", scatter_dimension=0, tiled=True
-    )
-    output = (mid + mixture.astype(f32)).astype(bf16)
-    w_gate_grad = weight_sum[:, :part_rows]
-    w_up_grad = weight_sum[:, part_rows : 2 * part_rows]
-    w_down_grad = weight_sum[:, 2 * part_rows :].reshape(local_experts, down_rows, width)
-
     joined_grad = attention_backward(
         saved, context_grad.reshape(seq_len, query_width), key_seg, tables
     )
-    joined_grad, weight_sum = together(joined_grad, weight_sum)
     joined_home = lax.all_to_all(
         joined_grad.reshape(planes, tok_rows, joined_width), "tensor", split_axis=0, concat_axis=0
     )
@@ -412,6 +508,7 @@
     flat_rows = flat_part.shape[0]
     block = -(-flat_rows // (16 * sharers)) * 16
     flat_part = jnp.pad(flat_part, ((0, sharers * block - flat_rows), (0, 0)))
+    flat_part, weight_sum = together(flat_part, weight_sum)
     arrived = lax.all_to_all(
         flat_part.reshape(sharers, block, LANES), ("dp", "expert"), split_axis=0, concat_axis=0
     )
@@ -431,6 +528,13 @@
         concat_axis=0,
     )
     shared = jnp.sum(shared.astype(f32), axis=0).reshape(-1)
+    w_gate_grad = weight_sum[:local_experts].astype(f32)
+    w_up_grad = weight_sum[local_experts : 2 * local_experts].astype(f32)
+    w_down_grad = weight_sum[2 * local_experts :].reshape(
+        local_experts, chunks, down_rows, hidden_width
+    )
+    w_down_grad = w_down_grad.transpose(0, 2, 1, 3).reshape(local_experts, down_rows, width)
+    w_down_grad = w_down_grad.astype(f32)
     router_size = width * experts
     return (
         output,

time: 829 us -> 608 us (0.73)
  local copies, waits for them, and re-layouts: 148 us -> 42.4 us
  matrix products: 129 us -> 38.9 us
  Pallas kernels: 0 us -> 83 us
  waiting for transfers between devices: 317 us -> 243 us
  other arithmetic: 82.5 us -> 47.3 us
  starting transfers between devices: 86.4 us -> 101 us
  blocking collectives: 41.7 us -> 31.2 us
    pallas_call x0 -> x6, Pallas kernels: none -> 83 us  [the longest x4 57.3 us: run_experts(): pl.pallas_call(expert_kernel, out_shape=(jax.ShapeDtypeStruct((sources, t...]
    dot_general x12 -> x0, matrix products: 80.4 us -> none  [the longest x1 11.1 us: local(): jnp.einsum('secd,efd->secf', cots, full_down, preferred_element_type=f32)]
    all_gather x1, waiting for transfers between devices: 37.4 us -> 0.02 us  [local(): attention_all = lax.all_gather(attention_low, 'tensor', axis=0, tiled=True)]
    ppermute x36 -> x18, waiting for transfers between devices: 127 us -> 94.1 us  [cross(): return lax.ppermute(values, ('dp', 'expert'), pairs)]
    ppermute x12 -> x0, local copies, waits for them, and re-layouts: 31 us -> none  [move(): return lax.ppermute(values, 'expert', along(axis, step))]
    all_gather x2, waiting for transfers between devices: 64 us -> 39.1 us  [half_gather(): return lax.all_gather(half, 'tensor', axis=0)]
    reduce_scatter x1, waiting for transfers between devices: 23.9 us -> 48.7 us  [local(): lax.psum_scatter(kept, 'tensor', scatter_dimension=1, tiled=True)]
    concatenate x7 -> x1, other arithmetic: 19.8 us -> 1.9 us  [local(): weights = jnp.concatenate([w_gate, w_up, down_parts], axis=0)]
  transfers between devices with their start and end apart: 51 -> 32, of which waited for: 24 -> 19; matrix products, arithmetic and copies ran while one was open for 31% -> 17% of each run, Pallas kernels for 0% -> 14%
where the time goes in v2:
time: 608 us; the launch traced here: 602 us
  waiting for transfers between devices  243 us (40%)
  starting transfers between devices  101 us (17%)
  Pallas kernels  83 us (14%)
  other arithmetic  47.3 us (8%)
  local copies, waits for them, and re-layouts  42.4 us (7%)
  matrix products  38.9 us (6%)
  blocking collectives  31.2 us (5%)
  between operations  15.6 us (3%)
    ppermute x18, waiting for transfers between devices, cross(): return lax.ppermute(values, ('dp', 'expert'), pairs)  94.1 us
    pallas_call x4, Pallas kernels, run_experts(): pl.pallas_call(expert_kernel, out_shape=(jax.ShapeDtypeStruct((sources, t...  57.3 us
    reduce_scatter x1, waiting for transfers between devices, local(): lax.psum_scatter(kept, 'tensor', scatter_dimension=1, tiled=True)  48.7 us
    all_gather x2, waiting for transfers between devices, half_gather(): return lax.all_gather(half, 'tensor', axis=0)  39.1 us
    ppermute x3, starting transfers between devices, swap_cores(): return lax.ppermute(values, 'dp', [(0, 1), (1, 0)])  36.3 us
    all_to_all x1, blocking collectives, local(): lax.all_to_all(flat_part.reshape(sharers, block, LANES), ('dp', 'expert')...  31.2 us
    ppermute x18, starting transfers between devices, cross(): return lax.ppermute(values, ('dp', 'expert'), pairs)  27.7 us
    pallas_call x2, Pallas kernels, run_weight_grads(): pl.pallas_call(weight_grad_kernel, out_shape=jax.ShapeDtypeStruct((6, wid...  25.7 us
  transfers between devices with their start and end apart: 32, of which 19 were waited for; matrix products, arithmetic and copies ran while one was open for 17% of the time, Pallas kernels for 14%

profile of v2, /device:TPU:1, one launch (start us, length us, event | category | flops | bytes accessed | tf_op | source)
XLA Modules:
  0.0 602.1 jit_solution(3941266866598435941)
XLA Ops:
  23.0 5.5 collective-permute-done.2
  33.1 18.3 %collective-permute-done.3.cots_ref = bf16[4,128,1664]{2,1,0:T(8,128)(2,1)} collective-permute-done((bf16[4,128,1664]{2,1,0:T(8,128)(2,1)S(1)}, bf16[4,128,1664]{2,1,0:T(8,128)(2,1)}, u32[]{:S(2)}, u32[]{:S(2)}) %collective-permute-start.3) | collective-permute-done | bytes 1703968 | tf_op jit(solution)/shard_map/ppermute | solution.py:143
  51.3 17.5 %collective-permute-done.4.cots_ref = bf16[4,128,1664]{2,1,0:T(8,128)(2,1)} collective-permute-done((bf16[4,128,1664]{2,1,0:T(8,128)(2,1)S(1)}, bf16[4,128,1664]{2,1,0:T(8,128)(2,1)}, u32[]{:S(2)}, u32[]{:S(2)}) %collective-permute-start.4) | collective-permute-done | bytes 1703968 | tf_op jit(solution)/shard_map/ppermute | solution.py:143
  73.9 39.1 %all-gather.14.cloned.1.call-done = bf16[768,1536]{1,0:T(8,128)(2,1)} async-done(((bf16[96,1536]{1,0:T(8,128)(2,1)}), bf16[768,1536]{1,0:T(8,128)(2,1)}) %all-gather.14.cloned.1.call-update) | async-done | bytes 2359312 | tf_op jit(solution)/shard_map/all_gather | solution.py:405
  134.2 4.1 all-to-all-start
  138.4 18.0 %all-to-all-done = bf16[8,128,192]{1,2,0:T(8,128)(2,1)S(1)} async-done(((bf16[8,128,192]{1,2,0:T(8,128)(2,1)}), bf16[8,128,192]{1,2,0:T(8,128)(2,1)S(1)}, u32[]{:S(2)}, u32[]{:S(2)}) %all-to-all-start) | async-done | bytes 393248 | tf_op jit(solution)/shard_map/all_to_all | solution.py:422
  165.2 4.2 collective-permute-done.7
  169.6 5.2 collective-permute-done.9
  180.2 6.7 %all-gather.10.cloned.1.call-done.w_ref = bf16[6,1536,512]{2,1,0:T(8,128)(2,1)} async-done(((bf16[6,96,512]{2,1,0:T(8,128)(2,1)}), bf16[6,1536,512]{2,1,0:T(8,128)(2,1)}) %all-gather.10.cloned.1.call-update) | async-done | bytes 9437200 | tf_op jit(solution)/shard_map/all_gather | solution.py:416
  186.9 11.8 %collective-permute-done.10.rows_ref = bf16[4,128,1664]{2,1,0:T(8,128)(2,1)S(1)} collective-permute-done((bf16[4,128,1664]{2,1,0:T(8,128)(2,1)}, bf16[4,128,1664]{2,1,0:T(8,128)(2,1)S(1)}, u32[]{:S(2)}, u32[]{:S(2)}) %collective-permute-start.10) | collective-permute-done | bytes 1703968 | tf_op jit(solution)/shard_map/ppermute | solution.py:143
  199.8 14.3 %shard_map.230 = (bf16[4,128,3200]{2,1,0:T(8,128)(2,1)}, bf16[2,256,1536]{2,1,0:T(8,128)(2,1)S(1)}, bf16[2,256,1536]{2,1,0:T(8,128)(2,1)}, bf16[2,256,512]{2,1,0...) custom-call(s32[1]{0:T(128)} %bitcast.16.first_ref, ...), custom_call_target="tpu_custom_call" | custom-call | flops 5637144576 | bytes 25165824 | tf_op jit(solution)/shard_map/pallas_call | solution.py:271
  217.9 14.3 %shard_map.231 = (bf16[4,128,3200]{2,1,0:T(8,128)(2,1)}, bf16[2,256,1536]{2,1,0:T(8,128)(2,1)S(1)}, bf16[2,256,1536]{2,1,0:T(8,128)(2,1)}, bf16[2,256,512]{2,1,0...) custom-call(s32[1]{0:T(128)} %bitcast.16.first_ref, ...), custom_call_target="tpu_custom_call" | custom-call | flops 5637144576 | bytes 25165824 | tf_op jit(solution)/shard_map/pallas_call | solution.py:271
  234.3 14.4 %shard_map.232 = (bf16[4,128,3200]{2,1,0:T(8,128)(2,1)}, bf16[2,256,1536]{2,1,0:T(8,128)(2,1)S(1)}, bf16[2,256,1536]{2,1,0:T(8,128)(2,1)}, bf16[2,256,512]{2,1,0...) custom-call(s32[1]{0:T(128)} %bitcast.16.first_ref, ...), custom_call_target="tpu_custom_call" | custom-call | flops 5637144576 | bytes 25165824 | tf_op jit(solution)/shard_map/pallas_call | solution.py:271
  255.4 14.3 %shard_map.229 = (bf16[4,128,3200]{2,1,0:T(8,128)(2,1)}, bf16[2,256,1536]{2,1,0:T(8,128)(2,1)S(1)}, bf16[2,256,1536]{2,1,0:T(8,128)(2,1)}, bf16[2,256,512]{2,1,0...) custom-call(s32[1]{0:T(128)} %bitcast.16.first_ref, ...), custom_call_target="tpu_custom_call" | custom-call | flops 5637144576 | bytes 25165824 | tf_op jit(solution)/shard_map/pallas_call | solution.py:271
  271.7 12.9 %shard_map.234 = bf16[6,768,512]{2,1,0:T(8,128)(2,1)} custom-call(s32[1]{0:T(128)} %bitcast.27.half_ref, bf16[2,256,1536]{2,1,0:T(8,128)(2,1)} %copy-done.5, bf16[2,256,1536]{2,1,0:T(8,128)(2,1)} %copy-done.2, bf16[2,256,1536]{2,1,0:T(8,128)(2,1)} %copy-done.3, bf16[2,256,1536]{2,1,0:T(8,128)(2,1)} %copy-done.4, ...), custom_call_target="tpu_custom_call" | custom-call | flops 4831838208 | bytes 25165824 | tf_op jit(solution)/shard_map/pallas_call | solution.py:341
  284.5 5.5 collective-permute-start.19
  290.0 18.9 %collective-permute-done.15 = bf16[4,128,3200]{2,1,0:T(8,128)(2,1)} collective-permute-done((bf16[4,128,3200]{2,1,0:T(8,128)(2,1)}, bf16[4,128,3200]{2,1,0:T(8,128)(2,1)}, u32[]{:S(2)}, u32[]{:S(2)}) %collective-permute-start.15) | collective-permute-done | bytes 3276832 | tf_op jit(solution)/shard_map/ppermute | solution.py:143
  308.9 4.7 fusion.32
  318.9 12.8 %shard_map.233 = bf16[6,768,512]{2,1,0:T(8,128)(2,1)} custom-call(s32[1]{0:T(128)} %bitcast.26.half_ref, bf16[2,256,1536]{2,1,0:T(8,128)(2,1)} %copy-done.5, bf16[2,256,1536]{2,1,0:T(8,128)(2,1)} %copy-done.2, bf16[2,256,1536]{2,1,0:T(8,128)(2,1)} %copy-done.3, bf16[2,256,1536]{2,1,0:T(8,128)(2,1)} %copy-done.4, ...), custom_call_target="tpu_custom_call" | custom-call | flops 4831838208 | bytes 25165824 | tf_op jit(solution)/shard_map/pallas_call | solution.py:341
  331.7 6.3 %collective-permute-done.17 = bf16[128,3200]{1,0:T(8,128)(2,1)S(1)} collective-permute-done((bf16[128,3200]{1,0:T(8,128)(2,1)}, bf16[128,3200]{1,0:T(8,128)(2,1)S(1)}, u32[]{:S(2)}, u32[]{:S(2)}) %collective-permute-start.17) | collective-permute-done | bytes 819232 | tf_op jit(solution)/shard_map/ppermute | solution.py:143
  352.7 15.9 %all-to-all-start.1 = ((bf16[8,128,192]{1,2,0:T(8,128)(2,1)}), bf16[8,128,192]{1,2,0:T(8,128)(2,1)S(1)}, u32[]{:S(2)}, u32[]{:S(2)}) async-start(bf16[8,128,192]{1,2,0:T(8,128)(2,1)} %pad_maximum_fusion.4), calls=%async_computation.1 | async-start | bytes 786432 | tf_op jit(solution)/shard_map/all_to_all | solution.py:485
  368.7 27.2 %collective-permute-start.20 = (bf16[8,160,1536]{2,1,0:T(8,128)(2,1)}, bf16[8,160,1536]{2,1,0:T(8,128)(2,1)}, u32[]{:S(2)}, u32[]{:S(2)}) collective-permute-start(bf16[8,160,1536]{2,1,0:T(8,128)(2,1)} %bitcast.151), channel_id=1, source_target_pairs={{0,128},{128,0},{1,129},{129,1},{2,130},{130,2},{3,131},{131,3},{4... | collective-permute-start | bytes 11796488 | tf_op jit(solution)/shard_map/ppermute | solution.py:168
  396.3 6.0 fusion
  402.3 6.8 %fusion.2 = bf16[3,1024,1024]{1,2,0:T(8,128)(2,1)S(1)} fusion(f32[1024,1024,3]{1,0,2:T(8,128)S(1)} %get-tuple-element.162, f32[3,1024,1024]{1,2,0:T(8,128)} %copy-done.11, f32[3,1024]{1,0:T(4,128)S(1)} %get-tuple-element.161, f32[3,1024]{1,0:T(4,128)S(1)} %log_add_fusion), kind=kLoop, calls=%fused_computation.4 | loop fusion | flops 12582912 | bytes 31481856 | tf_op jit(solution)/shard_map/convert_element_type | solution.py:106
  417.5 7.3 %all-to-all-start.2 = ((bf16[8,128,320]{1,2,0:T(8,128)(2,1)}), bf16[8,128,320]{1,2,0:T(8,128)(2,1)}, u32[]{:S(2)}, u32[]{:S(2)}) async-start(bf16[8,128,320]{1,2,0:T(8,128)(2,1)} %pad_maximum_fusion.2), calls=%async_computation.2 | async-start | bytes 1310720 | tf_op jit(solution)/shard_map/all_to_all | solution.py:489
  430.7 7.7 %all-to-all-done.2 = bf16[8,128,320]{1,2,0:T(8,128)(2,1)} async-done(((bf16[8,128,320]{1,2,0:T(8,128)(2,1)}), bf16[8,128,320]{1,2,0:T(8,128)(2,1)}, u32[]{:S(2)}, u32[]{:S(2)}) %all-to-all-start.2) | async-done | bytes 655392 | tf_op jit(solution)/shard_map/all_to_all | solution.py:489
  450.0 48.7 %reduce-scatter.2.cloned.1.call-done = bf16[6,96,512]{2,1,0:T(8,128)(2,1)} async-done(((bf16[6,768,512]{2,1,0:T(8,128)(2,1)}), bf16[6,96,512]{2,1,0:T(8,128)(2,1)}) %reduce-scatter.2.cloned.1.call-update) | async-done | bytes 589840 | tf_op jit(solution)/shard_map/reduce_scatter | solution.py:461
  498.7 31.2 %all_to_all.30 = bf16[32,208,128]{2,1,0:T(8,128)(2,1)} all-to-all(bf16[32,208,128]{2,1,0:T(8,128)(2,1)S(1)} %bitcast.158), channel_id=1, replica_groups=mesh['dp'=2,'expert'=16,'tensor'=8] {'dp','expert'}, dimensions={0} | all-to-all | bytes 3407872 | tf_op jit(solution)/shard_map/all_to_all | solution.py:512
  533.0 4.8 all-to-all-start.4
  542.4 19.2 %all-to-all-done.4 = bf16[32,208,128]{2,1,0:T(8,128)(2,1)S(1)} async-done(((bf16[32,208,128]{2,1,0:T(8,128)(2,1)}), bf16[32,208,128]{2,1,0:T(8,128)(2,1)S(1)}, u32[]{:S(2)}, u32[]{:S(2)}) %all-to-all-start.4) | async-done | bytes 1703968 | tf_op jit(solution)/shard_map/all_to_all | solution.py:516
  562.8 4.2 all-to-all-start.5
  583.1 8.5 %all-to-all-done.5 = bf16[8,408,128]{2,1,0:T(8,128)(2,1)} async-done(((bf16[8,408,128]{2,1,0:T(8,128)(2,1)}), bf16[8,408,128]{2,1,0:T(8,128)(2,1)}, u32[]{:S(2)}, u32[]{:S(2)}) %all-to-all-start.5) | async-done | bytes 835616 | tf_op jit(solution)/shard_map/all_to_all | solution.py:524
  (259 shorter events, 150.2 us)
Async XLA Ops:
  7.2 63.5 %all-gather.8.cloned.1.call-start = ((), (), s32[]{:S(2)}) async-start(), calls=%async_computation.7 | async-start | bytes 3538944 | tf_op jit(solution)/shard_map/all_gather | solution.py:388
  11.4 101.6 %all-gather.14.cloned.1.call-start = ((), (), s32[]{:S(2)}) async-start(), calls=%async_computation.11 | async-start | bytes 2654208 | tf_op jit(solution)/shard_map/all_gather | solution.py:405
  13.6 9.2 %collective-permute-start = (bf16[128,1664]{1,0:T(8,128)(2,1)S(1)}, bf16[128,1664]{1,0:T(8,128)(2,1)S(1)}, u32[]{:S(2)}, u32[]{:S(2)}) collective-permute-start(bf16[128,1664]{1,0:T(8,128)(2,1)S(1)} %get-tuple-element.137), channel_id=1, source_target_pairs={{0,8},{8,16},{16,24},{24,0},{32,40},{40,48},{48,56},{56,32},{64,72... | collective-permute-start | bytes 1277960 | tf_op jit(solution)/shard_map/ppermute | solution.py:143
  15.8 7.3 %collective-permute-start.1 = (bf16[128,1664]{1,0:T(8,128)(2,1)S(1)}, bf16[128,1664]{1,0:T(8,128)(2,1)S(1)}, u32[]{:S(2)}, u32[]{:S(2)}) collective-permute-start(bf16[128,1664]{1,0:T(8,128)(2,1)S(1)} %get-tuple-element.137), channel_id=1, source_target_pairs={{0,24},{8,0},{16,8},{24,16},{32,56},{40,32},{48,40},{56,48},{64,88... | collective-permute-start | bytes 1277960 | tf_op jit(solution)/shard_map/ppermute | solution.py:143
  17.1 11.5 %collective-permute-start.2 = (bf16[128,1664]{1,0:T(8,128)(2,1)S(1)}, bf16[128,1664]{1,0:T(8,128)(2,1)S(1)}, u32[]{:S(2)}, u32[]{:S(2)}) collective-permute-start(bf16[128,1664]{1,0:T(8,128)(2,1)S(1)} %get-tuple-element.137), channel_id=1, source_target_pairs={{0,16},{8,24},{16,0},{24,8},{32,48},{40,56},{48,32},{56,40},{64,80... | collective-permute-start | bytes 1277960 | tf_op jit(solution)/shard_map/ppermute | solution.py:143
  28.9 22.4 %collective-permute-start.3 = (bf16[4,128,1664]{2,1,0:T(8,128)(2,1)S(1)}, bf16[4,128,1664]{2,1,0:T(8,128)(2,1)}, u32[]{:S(2)}, u32[]{:S(2)}) collective-permute-start(bf16[4,128,1664]{2,1,0:T(8,128)(2,1)S(1)} %pad_maximum_fusion.cots_ref), channel_id=1, source_target_pairs={{0,32},{8,40},{16,48},{24,56},{32,64},{40,72},{48,80},{56,88},{64,... | collective-permute-start | bytes 5111816 | tf_op jit(solution)/shard_map/ppermute | solution.py:143
  30.0 38.8 %collective-permute-start.4 = (bf16[4,128,1664]{2,1,0:T(8,128)(2,1)S(1)}, bf16[4,128,1664]{2,1,0:T(8,128)(2,1)}, u32[]{:S(2)}, u32[]{:S(2)}) collective-permute-start(bf16[4,128,1664]{2,1,0:T(8,128)(2,1)S(1)} %pad_maximum_fusion.cots_ref), channel_id=1, source_target_pairs={{0,96},{8,104},{16,112},{24,120},{32,0},{40,8},{48,16},{56,24},{64... | collective-permute-start | bytes 5111816 | tf_op jit(solution)/shard_map/ppermute | solution.py:143
  31.8 39.0 %collective-permute-start.5 = (bf16[4,128,1664]{2,1,0:T(8,128)(2,1)S(1)}, bf16[4,128,1664]{2,1,0:T(8,128)(2,1)}, u32[]{:S(2)}, u32[]{:S(2)}) collective-permute-start(bf16[4,128,1664]{2,1,0:T(8,128)(2,1)S(1)} %pad_maximum_fusion.cots_ref), channel_id=1, source_target_pairs={{0,64},{8,72},{16,80},{24,88},{32,96},{40,104},{48,112},{56,120},{... | collective-permute-start | bytes 5111816 | tf_op jit(solution)/shard_map/ppermute | solution.py:143
  71.5 115.3 %all-gather.10.cloned.1.call-start = ((), (), s32[]{:S(2)}) async-start(), calls=%async_computation.8 | async-start | bytes 10027008 | tf_op jit(solution)/shard_map/all_gather | solution.py:416
  126.6 30.4 %collective-permute-start.6 = (bf16[8,96,1536]{2,1,0:T(8,128)(2,1)S(1)}, bf16[8,96,1536]{2,1,0:T(8,128)(2,1)}, u32[]{:S(2)}, u32[]{:S(2)}) collective-permute-start(bf16[8,96,1536]{2,1,0:T(8,128)(2,1)S(1)} %bitcast.153), channel_id=1, source_target_pairs={{0,128},{128,0},{1,129},{129,1},{2,130},{130,2},{3,131},{131,3},{4... | collective-permute-start | bytes 7077896 | tf_op jit(solution)/shard_map/ppermute | solution.py:168
  134.2 22.2 %all-to-all-start = ((bf16[8,128,192]{1,2,0:T(8,128)(2,1)}), bf16[8,128,192]{1,2,0:T(8,128)(2,1)S(1)}, u32[]{:S(2)}, u32[]{:S(2)}) async-start(bf16[8,128,192]{1,2,0:T(8,128)(2,1)} %copy.65), calls=%async_computation | async-start | bytes 786432 | tf_op jit(solution)/shard_map/all_to_all | solution.py:422
  138.3 206.1 %all-gather.16.cloned.1.call-start = ((), (), s32[]{:S(2)}) async-start(), calls=%async_computation.12 | async-start | bytes 4423680 | tf_op jit(solution)/shard_map/all_gather | solution.py:405
  160.7 8.7 %collective-permute-start.7 = (bf16[128,1664]{1,0:T(8,128)(2,1)S(1)}, bf16[128,1664]{1,0:T(8,128)(2,1)S(1)}, u32[]{:S(2)}, u32[]{:S(2)}) collective-permute-start(bf16[128,1664]{1,0:T(8,128)(2,1)S(1)} %concatenate.66), channel_id=1, source_target_pairs={{0,8},{8,16},{16,24},{24,0},{32,40},{40,48},{48,56},{56,32},{64,72... | collective-permute-start | bytes 1277960 | tf_op jit(solution)/shard_map/ppermute | solution.py:143
  162.0 7.6 %collective-permute-start.8 = (bf16[128,1664]{1,0:T(8,128)(2,1)S(1)}, bf16[128,1664]{1,0:T(8,128)(2,1)S(1)}, u32[]{:S(2)}, u32[]{:S(2)}) collective-permute-start(bf16[128,1664]{1,0:T(8,128)(2,1)S(1)} %concatenate.66), channel_id=1, source_target_pairs={{0,24},{8,0},{16,8},{24,16},{32,56},{40,32},{48,40},{56,48},{64,88... | collective-permute-start | bytes 1277960 | tf_op jit(solution)/shard_map/ppermute | solution.py:143
  163.7 11.1 %collective-permute-start.9 = (bf16[128,1664]{1,0:T(8,128)(2,1)S(1)}, bf16[128,1664]{1,0:T(8,128)(2,1)S(1)}, u32[]{:S(2)}, u32[]{:S(2)}) collective-permute-start(bf16[128,1664]{1,0:T(8,128)(2,1)S(1)} %concatenate.66), channel_id=1, source_target_pairs={{0,16},{8,24},{16,0},{24,8},{32,48},{40,56},{48,32},{56,40},{64,80... | collective-permute-start | bytes 1277960 | tf_op jit(solution)/shard_map/ppermute | solution.py:143
  176.3 22.4 %collective-permute-start.10 = (bf16[4,128,1664]{2,1,0:T(8,128)(2,1)}, bf16[4,128,1664]{2,1,0:T(8,128)(2,1)S(1)}, u32[]{:S(2)}, u32[]{:S(2)}) collective-permute-start(bf16[4,128,1664]{2,1,0:T(8,128)(2,1)} %pad_maximum_fusion.1.rows_ref), channel_id=1, source_target_pairs={{0,32},{8,40},{16,48},{24,56},{32,64},{40,72},{48,80},{56,88},{64,... | collective-permute-start | bytes 5111816 | tf_op jit(solution)/shard_map/ppermute | solution.py:143
  177.2 40.6 %collective-permute-start.12 = (bf16[4,128,1664]{2,1,0:T(8,128)(2,1)}, bf16[4,128,1664]{2,1,0:T(8,128)(2,1)}, u32[]{:S(2)}, u32[]{:S(2)}) collective-permute-start(bf16[4,128,1664]{2,1,0:T(8,128)(2,1)} %pad_maximum_fusion.1.rows_ref), channel_id=1, source_target_pairs={{0,96},{8,104},{16,112},{24,120},{32,0},{40,8},{48,16},{56,24},{64... | collective-permute-start | bytes 5111816 | tf_op jit(solution)/shard_map/ppermute | solution.py:143
  178.9 55.3 %collective-permute-start.14 = (bf16[4,128,1664]{2,1,0:T(8,128)(2,1)}, bf16[4,128,1664]{2,1,0:T(8,128)(2,1)}, u32[]{:S(2)}, u32[]{:S(2)}) collective-permute-start(bf16[4,128,1664]{2,1,0:T(8,128)(2,1)} %pad_maximum_fusion.1.rows_ref), channel_id=1, source_target_pairs={{0,64},{8,72},{16,80},{24,88},{32,96},{40,104},{48,112},{56,120},{... | collective-permute-start | bytes 5111816 | tf_op jit(solution)/shard_map/ppermute | solution.py:143
  216.1 74.0 %collective-permute-start.11 = (bf16[4,128,3200]{2,1,0:T(8,128)(2,1)}, bf16[4,128,3200]{2,1,0:T(8,128)(2,1)}, u32[]{:S(2)}, u32[]{:S(2)}) collective-permute-start(bf16[4,128,3200]{2,1,0:T(8,128)(2,1)} %get-tuple-element.58), channel_id=1, source_target_pairs={{0,96},{8,104},{16,112},{24,120},{32,0},{40,8},{48,16},{56,24},{64... | collective-permute-start | bytes 9830408 | tf_op jit(solution)/shard_map/ppermute | solution.py:143
  234.1 55.9 %collective-permute-start.13 = (bf16[4,128,3200]{2,1,0:T(8,128)(2,1)}, bf16[4,128,3200]{2,1,0:T(8,128)(2,1)}, u32[]{:S(2)}, u32[]{:S(2)}) collective-permute-start(bf16[4,128,3200]{2,1,0:T(8,128)(2,1)} %get-tuple-element.60), channel_id=1, source_target_pairs={{0,32},{8,40},{16,48},{24,56},{32,64},{40,72},{48,80},{56,88},{64,... | collective-permute-start | bytes 9830408 | tf_op jit(solution)/shard_map/ppermute | solution.py:143
  251.5 57.4 %collective-permute-start.15 = (bf16[4,128,3200]{2,1,0:T(8,128)(2,1)}, bf16[4,128,3200]{2,1,0:T(8,128)(2,1)}, u32[]{:S(2)}, u32[]{:S(2)}) collective-permute-start(bf16[4,128,3200]{2,1,0:T(8,128)(2,1)} %get-tuple-element.62), channel_id=1, source_target_pairs={{0,64},{8,72},{16,80},{24,88},{32,96},{40,104},{48,112},{56,120},{... | collective-permute-start | bytes 9830408 | tf_op jit(solution)/shard_map/ppermute | solution.py:143
  255.2 189.4 %all-gather.12.cloned.1.call-start = ((), (), s32[]{:S(2)}) async-start(), calls=%async_computation.9 | async-start | bytes 3538944 | tf_op jit(solution)/shard_map/all_gather | solution.py:492
  284.5 56.1 %collective-permute-start.19 = (bf16[6,768,512]{2,1,0:T(8,128)(2,1)}, bf16[6,768,512]{2,1,0:T(8,128)(2,1)S(1)}, u32[]{:S(2)}, u32[]{:S(2)}) collective-permute-start(bf16[6,768,512]{2,1,0:T(8,128)(2,1)} %shard_map.234), channel_id=1, source_target_pairs={{0,128},{128,0},{1,129},{129,1},{2,130},{130,2},{3,131},{131,3},{4... | collective-permute-start | bytes 14155784 | tf_op jit(solution)/shard_map/ppermute | solution.py:168
  313.6 18.1 %collective-permute-start.16 = (bf16[128,3200]{1,0:T(8,128)(2,1)}, bf16[128,3200]{1,0:T(8,128)(2,1)S(1)}, u32[]{:S(2)}, u32[]{:S(2)}) collective-permute-start(bf16[128,3200]{1,0:T(8,128)(2,1)} %get-tuple-element.121), channel_id=1, source_target_pairs={{0,24},{8,0},{16,8},{24,16},{32,56},{40,32},{48,40},{56,48},{64,88... | collective-permute-start | bytes 2457608 | tf_op jit(solution)/shard_map/ppermute | solution.py:143
  316.7 21.4 %collective-permute-start.17 = (bf16[128,3200]{1,0:T(8,128)(2,1)}, bf16[128,3200]{1,0:T(8,128)(2,1)S(1)}, u32[]{:S(2)}, u32[]{:S(2)}) collective-permute-start(bf16[128,3200]{1,0:T(8,128)(2,1)} %get-tuple-element.122), channel_id=1, source_target_pairs={{0,8},{8,16},{16,24},{24,0},{32,40},{40,48},{48,56},{56,32},{64,72... | collective-permute-start | bytes 2457608 | tf_op jit(solution)/shard_map/ppermute | solution.py:143
  317.0 21.1 %collective-permute-start.18 = (bf16[128,3200]{1,0:T(8,128)(2,1)}, bf16[128,3200]{1,0:T(8,128)(2,1)}, u32[]{:S(2)}, u32[]{:S(2)}) collective-permute-start(bf16[128,3200]{1,0:T(8,128)(2,1)} %get-tuple-element.123), channel_id=1, source_target_pairs={{0,16},{8,24},{16,0},{24,8},{32,48},{40,56},{48,32},{56,40},{64,80... | collective-permute-start | bytes 2457608 | tf_op jit(solution)/shard_map/ppermute | solution.py:143
  347.0 151.7 %reduce-scatter.2.cloned.1.call-start = ((), (), s32[]{:S(2)}) async-start(), calls=%async_computation.10 | async-start | bytes 5308416 | tf_op jit(solution)/shard_map/reduce_scatter | solution.py:461
  352.7 43.1 %all-to-all-start.1 = ((bf16[8,128,192]{1,2,0:T(8,128)(2,1)}), bf16[8,128,192]{1,2,0:T(8,128)(2,1)S(1)}, u32[]{:S(2)}, u32[]{:S(2)}) async-start(bf16[8,128,192]{1,2,0:T(8,128)(2,1)} %pad_maximum_fusion.4), calls=%async_computation.1 | async-start | bytes 786432 | tf_op jit(solution)/shard_map/all_to_all | solution.py:485
  368.7 69.7 %collective-permute-start.20 = (bf16[8,160,1536]{2,1,0:T(8,128)(2,1)}, bf16[8,160,1536]{2,1,0:T(8,128)(2,1)}, u32[]{:S(2)}, u32[]{:S(2)}) collective-permute-start(bf16[8,160,1536]{2,1,0:T(8,128)(2,1)} %bitcast.151), channel_id=1, source_target_pairs={{0,128},{128,0},{1,129},{129,1},{2,130},{130,2},{3,131},{131,3},{4... | collective-permute-start | bytes 11796488 | tf_op jit(solution)/shard_map/ppermute | solution.py:168
  417.5 20.9 %all-to-all-start.2 = ((bf16[8,128,320]{1,2,0:T(8,128)(2,1)}), bf16[8,128,320]{1,2,0:T(8,128)(2,1)}, u32[]{:S(2)}, u32[]{:S(2)}) async-start(bf16[8,128,320]{1,2,0:T(8,128)(2,1)} %pad_maximum_fusion.2), calls=%async_computation.2 | async-start | bytes 1310720 | tf_op jit(solution)/shard_map/all_to_all | solution.py:489
  533.0 28.6 %all-to-all-start.4 = ((bf16[32,208,128]{2,1,0:T(8,128)(2,1)}), bf16[32,208,128]{2,1,0:T(8,128)(2,1)S(1)}, u32[]{:S(2)}, u32[]{:S(2)}) async-start(bf16[32,208,128]{2,1,0:T(8,128)(2,1)} %broadcast_in_dim.27), calls=%async_computation.5 | async-start | bytes 3407872 | tf_op jit(solution)/shard_map/all_to_all | solution.py:516
  562.8 28.9 %all-to-all-start.5 = ((bf16[8,408,128]{2,1,0:T(8,128)(2,1)}), bf16[8,408,128]{2,1,0:T(8,128)(2,1)}, u32[]{:S(2)}, u32[]{:S(2)}) async-start(bf16[8,408,128]{2,1,0:T(8,128)(2,1)} %broadcast_in_dim.28), calls=%async_computation.6 | async-start | bytes 1671168 | tf_op jit(solution)/shard_map/all_to_all | solution.py:524
  (54 other events, 737.6 us)
Sparse Core Ops, SparseCore 0:
  11.5 48.5 all-gather.7
  71.6 41.3 all-gather.13
  115.5 71.3 all-gather.9
  255.3 68.7 all-gather.15
  347.1 80.4 all-gather.11
  430.0 68.6 reduce-scatter.1

commit v3 on v2

--- a/solution.py
+++ b/solution.py
@@ -11,6 +11,7 @@
 TOP = 8
 CAP = 64
 EXPERTS = 32
+HOLDERS = 16
 LANES = 128
 
 epsilon_norm = 1e-06
@@ -143,21 +144,83 @@
     return lax.ppermute(values, ("dp", "expert"), pairs)
 
 
-def gather_plane(values):
+def gather_first(values):
     values = by_rows(values)
     line = jnp.stack([values] + [cross(values, 0, step) for step in STEPS[1:]])
-    line = by_rows(line)
+    return by_rows(line)
+
+
+def gather_second(line):
     return [line] + [cross(line, 1, step) for step in STEPS[1:]]
 
 
-def scatter_plane(parts):
-    arrived = [parts[0]] + [by_rows(cross(part, 1, -step)) for part, step in zip(parts[1:], STEPS[1:])]
-    line = [
+def scatter_first(parts):
+    arrived = [parts[0]] + [
+        by_rows(cross(part, 1, -step)) for part, step in zip(parts[1:], STEPS[1:])
+    ]
+    return [
         by_rows(sum(part[place].astype(f32) for part in arrived).astype(bf16))
         for place in range(SIDE)
     ]
+
+
+def scatter_second(line):
     arrived = [line[0]] + [cross(part, 0, -step) for part, step in zip(line[1:], STEPS[1:])]
     return by_rows(sum(part.astype(f32) for part in arrived))
+
+
+def ring_gather(block):
+    size = lax.axis_size("tensor")
+    me = lax.axis_index("tensor")
+    half = block.shape[0] // 2
+    held = jnp.zeros((size,) + block.shape, block.dtype)
+
+    def shift(values, step):
+        return lax.ppermute(values, "tensor", [(i, (i + step) % size) for i in range(size)])
+
+    def put(held, values, place, row):
+        return lax.dynamic_update_slice(held, values[None], ((me + place) % size, row, 0))
+
+    held = put(held, block, 0, 0)
+    up = down = block
+    for step in range(1, size // 2):
+        up, down = shift(up, 1), shift(down, -1)
+        held = put(held, up, size - step, 0)
+        held = put(held, down, step, 0)
+    held = put(held, shift(up[:half], 1), size // 2, 0)
+    return put(held, shift(down[half:], -1), size // 2, half)
+
+
+def ring_scatter(parts):
+    size = lax.axis_size("tensor")
+    me = lax.axis_index("tensor")
+    half = parts.shape[1] // 2
+
+    def shift(values, step):
+        return lax.ppermute(values, "tensor", [(i, (i + step) % size) for i in range(size)])
+
+    def part_for(place):
+        return lax.dynamic_index_in_dim(parts, (me + place) % size, 0, keepdims=False)
+
+    far = part_for(size // 2)
+    up, down = shift(far[:half], 1), shift(far[half:], -1)
+    up = jnp.pad(up, ((0, half), (0, 0)))
+    down = jnp.pad(down, ((half, 0), (0, 0)))
+    for place in range(size // 2 - 1, 0, -1):
+        up = (part_for(place).astype(f32) + up.astype(f32)).astype(bf16)
+        down = (part_for(-place).astype(f32) + down.astype(f32)).astype(bf16)
+        up, down = together(shift(by_rows(up), 1), shift(by_rows(down), -1))
+    return part_for(0).astype(f32) + up.astype(f32) + down.astype(f32)
+
+
+def ring_sum(values):
+    size = lax.axis_size("tensor")
+    step = 1
+    while step < size:
+        pairs = [(i, i ^ step) for i in range(size)]
+        values = values + lax.ppermute(values, "tensor", pairs)
+        step *= 2
+    return values
 
 
 def together(*values):
@@ -175,89 +238,74 @@
 
 
 def expert_kernel(
-    first_ref, rows_ref, cots_ref, w_ref, out_ref, x_ref, c_ref, gate_ref, up_ref, hid_ref, *scratch
+    first_ref, rows_ref, cots_ref, w_ref, back_out, mix_out, x_ref, c_ref, gate_ref, up_ref, hid_ref, *scratch
 ):
-    pick_ref, down_ref, back_ref, gates_ref = scratch
+    pick_ref, down_ref, back_ref, mix_ref = scratch
     sources, tokens, _ = rows_ref.shape
-    pair = 2 * CAP
     width = x_ref.shape[2]
     inner = w_ref.shape[2]
-    experts = EXPERTS
-    first = first_ref[0]
-    lane = lax.broadcasted_iota(jnp.int32, (pair, LANES), 1)
-    expert_of = first + lax.broadcasted_iota(jnp.int32, (pair, LANES), 0) // CAP
-    own_high = lane == expert_of
-    own_low = lane == expert_of + experts
-    row_id = lax.broadcasted_iota(jnp.int32, (experts, tokens), 0)
-    slot = lax.broadcasted_iota(jnp.int32, (pair, tokens), 0)
+    e = pl.program_id(0)
+    expert = first_ref[0] + e
+    lane = lax.broadcasted_iota(jnp.int32, (CAP, LANES), 1)
+    row_id = lax.broadcasted_iota(jnp.int32, (EXPERTS, tokens), 0)
+    slot = lax.broadcasted_iota(jnp.int32, (CAP, tokens), 0).astype(f32)
+    at = pl.ds(pl.multiple_of(e * CAP, CAP), CAP)
+    gates = []
     for source in range(sources):
-        table = cots_ref[source, :experts, width:].astype(f32)
-        ranks = [
-            jnp.sum(jnp.where(row_id == first + e, table, 0.0), axis=0, keepdims=True)
-            for e in range(2)
-        ]
-        rank = jnp.where(slot < CAP, ranks[0], ranks[1])
-        pick = (rank == (slot % CAP).astype(f32)).astype(bf16)
-        pick_ref[source] = pick
+        table = cots_ref[source, :EXPERTS, width:].astype(f32)
+        rank = jnp.sum(jnp.where(row_id == expert, table, 0.0), axis=0, keepdims=True)
+        pick = (rank == slot).astype(bf16)
+        pick_ref[source, at] = pick
         rows = jnp.dot(pick, rows_ref[source], preferred_element_type=f32)
         cots = jnp.dot(pick, cots_ref[source, :, :width], preferred_element_type=f32)
-        gate = jnp.sum(jnp.where(own_high | own_low, rows[:, width:], 0.0), axis=1, keepdims=True)
+        own = (lane == expert) | (lane == expert + EXPERTS)
+        gates.append(jnp.sum(jnp.where(own, rows[:, width:], 0.0), axis=1, keepdims=True))
+        x_ref[0, source * CAP : (source + 1) * CAP] = rows[:, :width].astype(bf16)
+        c_ref[0, source * CAP : (source + 1) * CAP] = cots.astype(bf16)
+    gate = jnp.concatenate(gates, axis=0)
+
+    down_rows = inner // HOLDERS
+    chunks = width // inner
+    for holder in range(HOLDERS):
+        for chunk in range(chunks):
+            start = (holder * chunks + chunk) * down_rows
+            down_ref[
+                holder * down_rows : (holder + 1) * down_rows,
+                chunk * inner : (chunk + 1) * inner,
+            ] = w_ref[2, start : start + down_rows, :]
+
+    x = x_ref[0]
+    gate_pre = jnp.dot(x, w_ref[0], preferred_element_type=f32)
+    up_pre = jnp.dot(x, w_ref[1], preferred_element_type=f32)
+    back = contract(c_ref[0], down_ref[...], 1, 1)
+    sig = 1.0 / (1.0 + jnp.exp(-gate_pre))
+    silu = gate_pre * sig
+    hidden = (silu * up_pre).astype(bf16)
+    gate_grad = jnp.sum(back * hidden.astype(f32), axis=1, keepdims=True)
+    grad = gate * back
+    gate_pre_grad = (grad * up_pre * (sig + silu * (1.0 - sig))).astype(bf16)
+    up_pre_grad = (grad * silu).astype(bf16)
+    gate_ref[0] = gate_pre_grad
+    up_ref[0] = up_pre_grad
+    hid_ref[0] = (gate * hidden.astype(f32)).astype(bf16)
+    row_grad = contract(gate_pre_grad, w_ref[0], 1, 1) + contract(up_pre_grad, w_ref[1], 1, 1)
+    mixed = gate * jnp.dot(hidden, down_ref[...], preferred_element_type=f32)
+    high = gate_grad.astype(bf16).astype(f32)
+    lane = lax.broadcasted_iota(jnp.int32, (sources * CAP, LANES), 1)
+    tail = jnp.where(lane == expert, high, 0.0)
+    tail += jnp.where(lane == expert + EXPERTS, gate_grad - high, 0.0)
+    for source in range(sources):
         place = slice(source * CAP, (source + 1) * CAP)
-        for e in range(2):
-            part = slice(e * CAP, (e + 1) * CAP)
-            x_ref[e, place] = rows[part, :width].astype(bf16)
-            c_ref[e, place] = cots[part].astype(bf16)
-            gates_ref[e, place] = jnp.broadcast_to(gate[part], (CAP, LANES))
-
-    down_rows = inner // 16
-    chunks = width // inner
-    for e in range(2):
-        for holder in range(16):
-            for chunk in range(chunks):
-                at = (holder * chunks + chunk) * down_rows
-                down_ref[
-                    e,
-                    holder * down_rows : (holder + 1) * down_rows,
-                    chunk * inner : (chunk + 1) * inner,
-                ] = w_ref[4 + e, at : at + down_rows, :]
-
-    def one_expert(e, carry):
-        x = x_ref[e]
-        cot = c_ref[e]
-        gate = gates_ref[e][:, :1]
-        gate_pre = jnp.dot(x, w_ref[e], preferred_element_type=f32)
-        up_pre = jnp.dot(x, w_ref[2 + e], preferred_element_type=f32)
-        back = contract(cot, down_ref[e], 1, 1)
-        sig = 1.0 / (1.0 + jnp.exp(-gate_pre))
-        silu = gate_pre * sig
-        hidden = (silu * up_pre).astype(bf16)
-        gate_grad = jnp.sum(back * hidden.astype(f32), axis=1, keepdims=True)
-        grad = gate * back
-        gate_pre_grad = (grad * up_pre * (sig + silu * (1.0 - sig))).astype(bf16)
-        up_pre_grad = (grad * silu).astype(bf16)
-        gate_ref[e] = gate_pre_grad
-        up_ref[e] = up_pre_grad
-        hid_ref[e] = (gate * hidden.astype(f32)).astype(bf16)
-        row_grad = contract(gate_pre_grad, w_ref[e], 1, 1) + contract(
-            up_pre_grad, w_ref[2 + e], 1, 1
-        )
-        mixed = gate * jnp.dot(hidden, down_ref[e], preferred_element_type=f32)
-        high = gate_grad.astype(bf16).astype(f32)
-        lane = lax.broadcasted_iota(jnp.int32, (gate_grad.shape[0], LANES), 1)
-        tail = jnp.where(lane == first + e, high, 0.0) + jnp.where(
-            lane == first + e + experts, gate_grad - high, 0.0
-        )
+        back_ref[source, at, :width] = row_grad[place].astype(bf16)
+        back_ref[source, at, width:] = tail[place].astype(bf16)
+        mix_ref[source, at] = mixed[place].astype(bf16)
+
+    @pl.when(e == 1)
+    def _():
         for source in range(sources):
-            place = slice(source * CAP, (source + 1) * CAP)
-            to = pl.ds(pl.multiple_of(e * CAP, CAP), CAP)
-            back_ref[source, to, :width] = row_grad[place].astype(bf16)
-            back_ref[source, to, width : 2 * width] = mixed[place].astype(bf16)
-            back_ref[source, to, 2 * width :] = tail[place].astype(bf16)
-        return carry
-
-    lax.fori_loop(0, 2, one_expert, 0)
-    for source in range(sources):
-        out_ref[source] = contract(pick_ref[source], back_ref[source], 0, 0).astype(bf16)
+            pick = pick_ref[source]
+            back_out[source] = contract(pick, back_ref[source], 0, 0).astype(bf16)
+            mix_out[source] = contract(pick, mix_ref[source], 0, 0).astype(bf16)
 
 
 def run_experts(first, rows, cots, weights):
@@ -265,28 +313,49 @@
     width = padded - LANES
     inner = weights.shape[2]
     slots = sources * CAP
-    vmem = pl.BlockSpec(memory_space=pltpu.VMEM)
+
+    def whole(columns):
+        return pl.BlockSpec((sources, tokens, columns), lambda e: (0, 0, 0))
+
+    def by_expert(*shape):
+        return pl.BlockSpec(shape, lambda e: (e, 0, 0))
+
     acts = jax.ShapeDtypeStruct((2, slots, inner), bf16)
     wide = jax.ShapeDtypeStruct((2, slots, width), bf16)
     return pl.pallas_call(
         expert_kernel,
+        grid=(2,),
         out_shape=(
-            jax.ShapeDtypeStruct((sources, tokens, 2 * width + LANES), bf16),
+            jax.ShapeDtypeStruct((sources, tokens, padded), bf16),
+            jax.ShapeDtypeStruct((sources, tokens, width), bf16),
             wide,
             wide,
             acts,
             acts,
             acts,
         ),
-        in_specs=[pl.BlockSpec(memory_space=pltpu.SMEM), vmem, vmem, vmem],
-        out_specs=(vmem,) * 6,
+        in_specs=[
+            pl.BlockSpec(memory_space=pltpu.SMEM),
+            whole(padded),
+            whole(padded),
+            by_expert(3, width, inner),
+        ],
+        out_specs=(
+            whole(padded),
+            whole(width),
+            by_expert(1, slots, width),
+            by_expert(1, slots, width),
+            by_expert(1, slots, inner),
+            by_expert(1, slots, inner),
+            by_expert(1, slots, inner),
+        ),
         scratch_shapes=[
             pltpu.VMEM((sources, 2 * CAP, tokens), bf16),
-            pltpu.VMEM((2, inner, width), bf16),
-            pltpu.VMEM((sources, 2 * CAP, 2 * width + LANES), bf16),
-            pltpu.VMEM((2, slots, LANES), f32),
+            pltpu.VMEM((inner, width), bf16),
+            pltpu.VMEM((sources, 2 * CAP, padded), bf16),
+            pltpu.VMEM((sources, 2 * CAP, width), bf16),
         ],
-        compiler_params=pltpu.CompilerParams(vmem_limit_bytes=50 * 1024 * 1024),
+        compiler_params=pltpu.CompilerParams(vmem_limit_bytes=52 * 1024 * 1024),
         cost_estimate=pl.CostEstimate(
             flops=2 * 2 * 7 * slots * width * inner, bytes_accessed=24 << 20, transcendentals=0
         ),
@@ -298,56 +367,54 @@
     x_refs, c_refs, gate_refs, up_refs, hid_refs = (
         refs[i * groups : (i + 1) * groups] for i in range(5)
     )
-    out_ref = refs[5 * groups]
+    outs = refs[5 * groups :]
     slots, width = x_refs[0].shape[1:]
     inner = gate_refs[0].shape[2]
-    half = half_ref[0]
     rows = width // 2
-    cols = pl.ds(pl.multiple_of(half * rows, LANES), rows)
-    down_cols = pl.ds(pl.multiple_of(half * (inner // 2), LANES), inner // 2)
-    down_rows = inner // 16
+    down_rows = inner // HOLDERS
     chunks = width // inner
-
-    def one_expert(e, carry):
+    for out_ref, half in zip(outs, (1 - half_ref[0], half_ref[0])):
+        cols = pl.ds(pl.multiple_of(half * rows, LANES), rows)
+        down_cols = pl.ds(pl.multiple_of(half * (inner // 2), LANES), inner // 2)
         gate = jnp.zeros((rows, inner), f32)
         up = jnp.zeros((rows, inner), f32)
         down = jnp.zeros((inner // 2, width), f32)
         for i in range(groups):
-            x = x_refs[i][e, :, cols]
-            gate += contract(x, gate_refs[i][e], 0, 0)
-            up += contract(x, up_refs[i][e], 0, 0)
-        out_ref[e] = gate.astype(bf16)
-        out_ref[2 + e] = up.astype(bf16)
+            x = x_refs[i][0, :, cols]
+            gate += contract(x, gate_refs[i][0], 0, 0)
+            up += contract(x, up_refs[i][0], 0, 0)
+        out_ref[0] = gate.astype(bf16)
+        out_ref[1] = up.astype(bf16)
         for i in range(groups):
-            down += contract(hid_refs[i][e, :, down_cols], c_refs[i][e], 0, 0)
-        for holder in range(8):
+            down += contract(hid_refs[i][0, :, down_cols], c_refs[i][0], 0, 0)
+        for holder in range(HOLDERS // 2):
             for chunk in range(chunks):
                 at = (holder * chunks + chunk) * down_rows
-                out_ref[4 + e, at : at + down_rows, :] = down[
+                out_ref[2, at : at + down_rows, :] = down[
                     holder * down_rows : (holder + 1) * down_rows,
                     chunk * inner : (chunk + 1) * inner,
                 ].astype(bf16)
-        return carry
-
-    lax.fori_loop(0, 2, one_expert, 0)
-
-
-def run_weight_grads(half, saved):
+
+
+def run_weight_grads(core, saved):
     x, c, gate, up, hid = zip(*saved)
     slots, width = x[0].shape[1:]
     inner = gate[0].shape[2]
-    vmem = pl.BlockSpec(memory_space=pltpu.VMEM)
     operands = (*x, *c, *gate, *up, *hid)
+    out = jax.ShapeDtypeStruct((6, width // 2, inner), bf16)
+    out_spec = pl.BlockSpec((3, width // 2, inner), lambda e: (e, 0, 0))
     return pl.pallas_call(
         weight_grad_kernel,
-        out_shape=jax.ShapeDtypeStruct((6, width // 2, inner), bf16),
-        in_specs=[pl.BlockSpec(memory_space=pltpu.SMEM)] + [vmem] * len(operands),
-        out_specs=vmem,
-        compiler_params=pltpu.CompilerParams(vmem_limit_bytes=50 * 1024 * 1024),
+        grid=(2,),
+        out_shape=(out, out),
+        in_specs=[pl.BlockSpec(memory_space=pltpu.SMEM)]
+        + [pl.BlockSpec((1,) + v.shape[1:], lambda e: (e, 0, 0)) for v in operands],
+        out_specs=(out_spec, out_spec),
+        compiler_params=pltpu.CompilerParams(vmem_limit_bytes=52 * 1024 * 1024),
         cost_estimate=pl.CostEstimate(
-            flops=2 * 3 * 4 * slots * width * inner, bytes_accessed=24 << 20, transcendentals=0
+            flops=2 * 2 * 3 * 4 * slots * width * inner, bytes_accessed=28 << 20, transcendentals=0
         ),
-    )(half, *operands)
+    )(core, *operands)
 
 
 def local(
@@ -397,32 +464,28 @@
     extra = jnp.pad(rank, ((0, tok_rows - experts), (0, LANES - tok_rows)))
     cot_payload = jnp.concatenate([cotangent, extra], axis=1)
 
-    cot_parts = gather_plane(cot_payload)
-
-    def half_gather(shard):
-        count = shard.shape[0] // 2
-        half = lax.dynamic_slice_in_dim(shard, core * count, count, 0)
-        return lax.all_gather(half, "tensor", axis=0)
-
-    normed_all, cot_parts, w_out = together(normed_all, cot_parts, w_out)
-    half_out = half_gather(w_out)
+    count = w_out.shape[0] // 2
+    half_out = ring_gather(lax.dynamic_slice_in_dim(w_out, core * count, count, 0))
+    other_out = swap_cores(half_out)
+
     chunks = width // hidden_width
     down_rows = w_down.shape[1]
     part_rows = w_gate.shape[1]
     down_parts = w_down.reshape(local_experts, down_rows, chunks, hidden_width)
     down_parts = down_parts.transpose(0, 2, 1, 3).reshape(local_experts, part_rows, hidden_width)
-    weights = jnp.concatenate([w_gate, w_up, down_parts], axis=0)
-    half_out, weights = together(half_out, weights)
+    weights = jnp.stack([w_gate, w_up, down_parts], axis=1)
+    weights = weights.reshape(3 * local_experts, part_rows, hidden_width)
+    normed_all, half_out, cot_line, weights = together(
+        normed_all, half_out, gather_first(cot_payload), weights
+    )
     weights_all = lax.all_gather(weights, ("dp", "tensor"), axis=1, tiled=True)
-    weights_all, joined_rows = together(weights_all, joined_weights.T)
-    half_joined = half_gather(joined_rows)
+    cot_parts = gather_second(cot_line)
 
     tables = rope_tables(seq_len, HEAD_DIM)
     context, saved = attention_forward(normed_all, joined_weights, key_seg, tables)
     context_home = lax.all_to_all(
         context.reshape(planes, tok_rows, query_width), "tensor", split_axis=0, concat_axis=0
     )
-    other_out = swap_cores(half_out)
 
     def both_halves(blocks, mine, other):
         count = blocks.shape[2] // 2
@@ -446,28 +509,32 @@
         [normed_two, gate_high, gate_low, jnp.zeros((tok_rows, LANES - 2 * experts), bf16)],
         axis=1,
     )
-    rows_parts = gather_plane(payload)
+    payload, *cot_parts = together(payload, *cot_parts)
+    rows_parts = gather_second(gather_first(payload))
 
     first_expert = first_expert.astype(jnp.int32).reshape(1)
-    done = [
-        run_experts(first_expert, rows, cots, weights_all)
-        for rows, cots in zip(rows_parts, cot_parts)
-    ]
-    back_home = scatter_plane([part[0] for part in done])
-    saved_rows = [part[1:] for part in done]
-    given = run_weight_grads((1 - core).astype(jnp.int32).reshape(1), saved_rows)
-    kept = run_weight_grads(core.astype(jnp.int32).reshape(1), saved_rows)
+    done = [run_experts(first_expert, rows_parts[0], cot_parts[0], weights_all)]
+    *travelled, done[0] = together(*rows_parts[1:], done[0])
+    rows_parts[1:] = travelled
+    for rows, cots in zip(rows_parts[1:], cot_parts[1:]):
+        done.append(run_experts(first_expert, rows, cots, weights_all))
+    back_line = scatter_first([part[0] for part in done])
+    *both, given, kept = together(
+        *back_line,
+        *[part[1] for part in done],
+        *run_weight_grads(core.astype(jnp.int32).reshape(1), [part[2:] for part in done]),
+    )
+    back_line, mix_parts = both[:SIDE], both[SIDE:]
     kept = (kept.astype(f32) + swap_cores(given).astype(f32)).astype(bf16)
     weight_sum = lax.psum_scatter(kept, "tensor", scatter_dimension=1, tiled=True)
-    back_home, kept, half_joined = together(back_home, kept, half_joined)
-    output = (mid + back_home[:, width : 2 * width]).astype(bf16)
+    back_home = scatter_second(back_line)
+    back_home, kept = together(back_home, kept)
 
     cot_f32 = cotangent.astype(f32)
-    grad_tail = back_home[:, 2 * width :]
+    grad_tail = back_home[:, width:]
     gate_grad = grad_tail[:, :experts] + grad_tail[:, experts : 2 * experts]
     chosen_grad = gates * (gate_grad - jnp.sum(gates * gate_grad, axis=1, keepdims=True))
     logit_grad = chosen_grad.astype(bf16)
-    router_part = jnp.einsum("td,te->de", normed_two, logit_grad, preferred_element_type=f32)
     normed_two_grad = back_home[:, :width] + jnp.einsum(
         "te,de->td", logit_grad, w_router, preferred_element_type=f32
     )
@@ -482,64 +549,70 @@
         return jnp.concatenate([low, high], axis=2).astype(bf16)
 
     context_grad = both_back(attention_low, half_out, other_out)
+    context_grad, logit_grad, *mix_parts = together(context_grad, logit_grad, *mix_parts)
+    mix_line = scatter_first(mix_parts)
+    router_part = contract(normed_two, logit_grad, 0, 0)
     context_grad = lax.all_to_all(context_grad, "tensor", split_axis=0, concat_axis=0)
     joined_grad = attention_backward(
         saved, context_grad.reshape(seq_len, query_width), key_seg, tables
     )
-    joined_home = lax.all_to_all(
-        joined_grad.reshape(planes, tok_rows, joined_width), "tensor", split_axis=0, concat_axis=0
+    shared_early = ring_sum(
+        jnp.concatenate([router_part.reshape(-1), norm2_part]).astype(bf16).reshape(-1, LANES)
+    )
+    joined_grad, shared_early, *mix_line = together(joined_grad, shared_early, *mix_line)
+    output = (mid + scatter_second(mix_line)).astype(bf16)
+    normed_one_grad = ring_scatter(
+        contract(joined_grad, joined_weights, 1, 1).astype(bf16).reshape(planes, tok_rows, width)
     )
     attention_all = lax.all_gather(attention_low, "tensor", axis=0, tiled=True)
-    out_part = jnp.einsum("tq,td->qd", context, attention_all, preferred_element_type=f32)
-    joined_part = jnp.einsum("td,tq->dq", normed_all, joined_grad, preferred_element_type=f32)
-    normed_one_grad = both_halves(joined_home, half_joined, swap_cores(half_joined))
-    input_part, norm1_part = rms_backward(token_f32, inverse_one, norm1_gain, normed_one_grad)
-    input_grad = mid_grad + input_part
+    out_part = contract(context, attention_all, 0, 0)
+    joined_part = contract(normed_all, joined_grad, 0, 0)
+    norm1_part = jnp.sum(joined_part * joined_weights.astype(f32), axis=1) / norm1_gain
 
     sharers = lax.axis_size("dp") * owners
-    shared_part = jnp.concatenate([router_part.reshape(-1), norm2_part, norm1_part])
     flat_part = jnp.concatenate(
-        [
-            part.astype(bf16).reshape(-1, LANES)
-            for part in (joined_part, out_part, shared_part)
-        ],
+        [joined_part.astype(bf16).reshape(-1, LANES), out_part.astype(bf16).reshape(-1, LANES), shared_early],
         axis=0,
     )
     flat_rows = flat_part.shape[0]
     block = -(-flat_rows // (16 * sharers)) * 16
     flat_part = jnp.pad(flat_part, ((0, sharers * block - flat_rows), (0, 0)))
-    flat_part, weight_sum = together(flat_part, weight_sum)
     arrived = lax.all_to_all(
         flat_part.reshape(sharers, block, LANES), ("dp", "expert"), split_axis=0, concat_axis=0
     )
     total = jnp.sum(arrived.astype(f32), axis=0).astype(bf16)
-    flat_sum = lax.all_to_all(
-        jnp.broadcast_to(total[None], arrived.shape), ("dp", "expert"), split_axis=0, concat_axis=0
-    ).reshape(sharers * block, LANES)
+    norm1_rows = width // LANES
+    norm1_high, norm1_low = split_two(ring_sum(norm1_part).reshape(norm1_rows, LANES))
+    norm1_pad = jnp.zeros((-2 * norm1_rows % 16, LANES), bf16)
+    total = jnp.concatenate([total, norm1_high, norm1_low, norm1_pad], axis=0)
+    spread = lax.all_to_all(
+        jnp.broadcast_to(total[None], (sharers,) + total.shape),
+        ("dp", "expert"),
+        split_axis=0,
+        concat_axis=0,
+    )
+    spread, weight_sum = together(spread, weight_sum)
+    flat_sum = spread[:, :block].reshape(sharers * block, LANES)
+    norm1_sum = jnp.sum(spread[:, block : block + 2 * norm1_rows].astype(f32), axis=0)
+    norm1_sum = norm1_sum[:norm1_rows] + norm1_sum[norm1_rows:]
     cut = width * joined_width // LANES
     end = cut + query_width * width // LANES
     joined_sum = flat_sum[:cut].reshape(width, joined_width).astype(f32)
     out_sum = flat_sum[cut:end].reshape(query_width, width).astype(f32)
-    shared = flat_sum[end:flat_rows]
-    shared = lax.all_to_all(
-        jnp.broadcast_to(shared[None], (planes,) + shared.shape),
-        "tensor",
-        split_axis=0,
-        concat_axis=0,
-    )
-    shared = jnp.sum(shared.astype(f32), axis=0).reshape(-1)
-    w_gate_grad = weight_sum[:local_experts].astype(f32)
-    w_up_grad = weight_sum[local_experts : 2 * local_experts].astype(f32)
-    w_down_grad = weight_sum[2 * local_experts :].reshape(
-        local_experts, chunks, down_rows, hidden_width
-    )
+    shared = flat_sum[end:flat_rows].astype(f32).reshape(-1)
+    weight_sum = weight_sum.reshape(local_experts, 3, part_rows, hidden_width)
+    w_gate_grad = weight_sum[:, 0].astype(f32)
+    w_up_grad = weight_sum[:, 1].astype(f32)
+    w_down_grad = weight_sum[:, 2].reshape(local_experts, chunks, down_rows, hidden_width)
     w_down_grad = w_down_grad.transpose(0, 2, 1, 3).reshape(local_experts, down_rows, width)
     w_down_grad = w_down_grad.astype(f32)
+    input_part, _ = rms_backward(token_f32, inverse_one, norm1_gain, normed_one_grad)
+    input_grad = mid_grad + input_part
     router_size = width * experts
     return (
         output,
         input_grad,
-        shared[router_size + width : router_size + 2 * width],
+        norm1_sum.reshape(width),
         joined_sum[:, :query_width],
         joined_sum[:, query_width : query_width + kv_width],
         joined_sum[:, query_width + kv_width :],

time: 608 us -> 517 us (0.85)
  waiting for transfers between devices: 243 us -> 193 us
  blocking collectives: 31.2 us -> 0 us
  Pallas kernels: 83 us -> 68.9 us
    ppermute x0 -> x22, waiting for transfers between devices: none -> 80.5 us  [the longest x6 41.7 us: ring_sum(): values = values + lax.ppermute(values, 'tensor', pairs)]
    reduce_scatter x1, waiting for transfers between devices: 48.7 us -> 0.01 us  [local(): lax.psum_scatter(kept, 'tensor', scatter_dimension=1, tiled=True)]
    all_gather x2 -> x0, waiting for transfers between devices: 39.1 us -> none  [half_gather(): return lax.all_gather(half, 'tensor', axis=0)]
    ppermute x0 -> x22, starting transfers between devices: none -> 35.2 us  [the longest x16 22.1 us: shift(): lax.ppermute(values, 'tensor', [(i, (i + step) % size) for i in range(siz...]
    all_to_all x1 -> x0, blocking collectives: 31.2 us -> none  [local(): lax.all_to_all(flat_part.reshape(sharers, block, LANES), ('dp', 'expert')...]
    ppermute x3 -> x2, starting transfers between devices: 36.3 us -> 5.65 us  [swap_cores(): return lax.ppermute(values, 'dp', [(0, 1), (1, 0)])]
    all_to_all x3 -> x2, waiting for transfers between devices: 35.4 us -> 8.75 us  [the longest x1 8.75 us: local(): lax.all_to_all(jnp.broadcast_to(total[None], (sharers,) + total.shape), (...]
    pallas_call x6 -> x5, Pallas kernels: 83 us -> 68.9 us  [the longest x4 53.2 us: run_experts(): pl.pallas_call(expert_kernel, grid=(2,), out_shape=(jax.ShapeDtypeStruct(...]
  transfers between devices with their start and end apart: 32 -> 56, of which waited for: 19 -> 24; matrix products, arithmetic and copies ran while one was open for 17% -> 18% of each run, Pallas kernels for 14% -> 11%
where the time goes in v3:
time: 517 us; the launch traced here: 508 us
  waiting for transfers between devices  193 us (37%)
  starting transfers between devices  97.4 us (19%)
  Pallas kernels  68.9 us (13%)
  other arithmetic  51.1 us (10%)
  local copies, waits for them, and re-layouts  44.2 us (9%)
  matrix products  38.1 us (7%)
  between operations  15.2 us (3%)
    ppermute x24, waiting for transfers between devices, cross(): return lax.ppermute(values, ('dp', 'expert'), pairs)  81.3 us
    pallas_call x4, Pallas kernels, run_experts(): pl.pallas_call(expert_kernel, grid=(2,), out_shape=(jax.ShapeDtypeStruct(...  53.2 us
    ppermute x6, waiting for transfers between devices, ring_sum(): values = values + lax.ppermute(values, 'tensor', pairs)  41.7 us
    ppermute x16, waiting for transfers between devices, shift(): lax.ppermute(values, 'tensor', [(i, (i + step) % size) for i in range(siz...  38.8 us
    ppermute x24, starting transfers between devices, cross(): return lax.ppermute(values, ('dp', 'expert'), pairs)  30 us
    ppermute x16, starting transfers between devices, shift(): lax.ppermute(values, 'tensor', [(i, (i + step) % size) for i in range(siz...  22.1 us
    unnamed x118, local copies, waits for them, and re-layouts  19 us
    pallas_call x1, Pallas kernels, run_weight_grads(): pl.pallas_call(weight_grad_kernel, grid=(2,), out_shape=(out, out), in_sp...  15.7 us
  transfers between devices with their start and end apart: 56, of which 24 were waited for; matrix products, arithmetic and copies ran while one was open for 18% of the time, Pallas kernels for 11%

profile of v3, /device:TPU:1, one launch (start us, length us, event | category | flops | bytes accessed | tf_op | source)
XLA Modules:
  0.0 507.9 jit_solution(17130208325079177539)
XLA Ops:
  36.1 6.2 %collective-permute-done.2 = bf16[96,1536]{1,0:T(8,128)(2,1)S(1)} collective-permute-done((bf16[96,1536]{1,0:T(8,128)(2,1)S(1)}, bf16[96,1536]{1,0:T(8,128)(2,1)S(1)}, u32[]{:S(2)}, u32[]{:S(2)}) %collective-permute-start.2) | collective-permute-done | bytes 294944 | tf_op jit(solution)/shard_map/ppermute | solution.py:179
  46.5 11.3 %collective-permute-done.4 = bf16[96,1536]{1,0:T(8,128)(2,1)S(1)} collective-permute-done((bf16[96,1536]{1,0:T(8,128)(2,1)S(1)}, bf16[96,1536]{1,0:T(8,128)(2,1)S(1)}, u32[]{:S(2)}, u32[]{:S(2)}) %collective-permute-start.4) | collective-permute-done | bytes 294944 | tf_op jit(solution)/shard_map/ppermute | solution.py:179
  62.1 4.7 collective-permute-done.6
  68.1 7.6 %all-gather.4.cloned.1.call-done = bf16[1024,1536]{1,0:T(8,128)(2,1)} async-done(((bf16[128,1536]{1,0:T(8,128)(2,1)}), bf16[1024,1536]{1,0:T(8,128)(2,1)}) %all-gather.4.cloned.1.call-update) | async-done | bytes 3145744 | tf_op jit(solution)/shard_map/all_gather | solution.py:455
  93.9 4.0 all-to-all-start
  102.3 14.8 %all-to-all-done = bf16[8,128,192]{1,2,0:T(8,128)(2,1)S(1)} async-done(((bf16[8,128,192]{1,2,0:T(8,128)(2,1)}), bf16[8,128,192]{1,2,0:T(8,128)(2,1)S(1)}, u32[]{:S(2)}, u32[]{:S(2)}) %all-to-all-start) | async-done | bytes 393248 | tf_op jit(solution)/shard_map/all_to_all | solution.py:486
  123.2 16.0 %collective-permute-done.13.cots_ref = bf16[4,128,1664]{2,1,0:T(8,128)(2,1)} collective-permute-done((bf16[4,128,1664]{2,1,0:T(8,128)(2,1)}, bf16[4,128,1664]{2,1,0:T(8,128)(2,1)}, u32[]{:S(2)}, u32[]{:S(2)}) %collective-permute-start.13) | collective-permute-done | bytes 1703968 | tf_op jit(solution)/shard_map/ppermute | solution.py:144
  143.6 7.7 %collective-permute-done.16 = bf16[128,1664]{1,0:T(8,128)(2,1)S(1)} collective-permute-done((bf16[128,1664]{1,0:T(8,128)(2,1)S(1)}, bf16[128,1664]{1,0:T(8,128)(2,1)S(1)}, u32[]{:S(2)}, u32[]{:S(2)}) %collective-permute-start.16) | collective-permute-done | bytes 426016 | tf_op jit(solution)/shard_map/ppermute | solution.py:144
  160.1 13.2 %shard_map.229 = (bf16[4,128,1664]{2,1,0:T(8,128)(2,1)}, bf16[4,128,1536]{2,1,0:T(8,128)(2,1)}, bf16[2,256,1536]{2,1,0:T(8,128)(2,1)}, bf16[2,256,1536]{2,1,0:T(...) custom-call(s32[1]{0:T(128)} %bitcast.31.first_ref, ...), custom_call_target="tpu_custom_call" | custom-call | flops 5637144576 | bytes 25165824 | tf_op jit(solution)/shard_map/pallas_call | solution.py:325
  175.0 4.2 collective-permute-done.20.rows_ref
  179.2 17.9 %collective-permute-done.19.rows_ref = bf16[4,128,1664]{2,1,0:T(8,128)(2,1)} collective-permute-done((bf16[4,128,1664]{2,1,0:T(8,128)(2,1)}, bf16[4,128,1664]{2,1,0:T(8,128)(2,1)}, u32[]{:S(2)}, u32[]{:S(2)}) %collective-permute-start.19) | collective-permute-done | bytes 1703968 | tf_op jit(solution)/shard_map/ppermute | solution.py:144
  197.4 13.2 %shard_map.230 = (bf16[4,128,1664]{2,1,0:T(8,128)(2,1)}, bf16[4,128,1536]{2,1,0:T(8,128)(2,1)}, bf16[2,256,1536]{2,1,0:T(8,128)(2,1)}, bf16[2,256,1536]{2,1,0:T(...) custom-call(s32[1]{0:T(128)} %bitcast.31.first_ref, ...), custom_call_target="tpu_custom_call" | custom-call | flops 5637144576 | bytes 25165824 | tf_op jit(solution)/shard_map/pallas_call | solution.py:325
  214.7 13.4 %shard_map.231 = (bf16[4,128,1664]{2,1,0:T(8,128)(2,1)}, bf16[4,128,1536]{2,1,0:T(8,128)(2,1)}, bf16[2,256,1536]{2,1,0:T(8,128)(2,1)}, bf16[2,256,1536]{2,1,0:T(...) custom-call(s32[1]{0:T(128)} %bitcast.31.first_ref, ...), custom_call_target="tpu_custom_call" | custom-call | flops 5637144576 | bytes 25165824 | tf_op jit(solution)/shard_map/pallas_call | solution.py:325
  229.7 13.2 %shard_map.232 = (bf16[4,128,1664]{2,1,0:T(8,128)(2,1)}, bf16[4,128,1536]{2,1,0:T(8,128)(2,1)}, bf16[2,256,1536]{2,1,0:T(8,128)(2,1)}, bf16[2,256,1536]{2,1,0:T(...) custom-call(s32[1]{0:T(128)} %bitcast.31.first_ref, ...), custom_call_target="tpu_custom_call" | custom-call | flops 5637144576 | bytes 25165824 | tf_op jit(solution)/shard_map/pallas_call | solution.py:325
  247.3 15.7 %shard_map.233 = (bf16[6,768,512]{2,1,0:T(8,128)(2,1)}, bf16[6,768,512]{2,1,0:T(8,128)(2,1)}) custom-call(s32[1]{0:T(128)} %bitcast.36.half_ref, bf16[2,256,1536]{2,1,0:T(8,128)(2,1)} %get-tuple-element.119.refs_0_, bf16[2,256,1536]{2,1,0:T(8,128)(2,1)} %get-tuple-element.120.refs_1_, bf16[2,256,1536]{2,1,0:T(8,128)(2,1)} %get-tuple-element.121.refs_2_, ...), custom_call_target="tpu_custom_call" | custom-call | flops 9663676416 | bytes 29360128 | tf_op jit(solution)/shard_map/pallas_call | solution.py:406
  263.0 7.4 %collective-permute-done.22 = bf16[4,128,1664]{2,1,0:T(8,128)(2,1)S(1)} collective-permute-done((bf16[4,128,1664]{2,1,0:T(8,128)(2,1)}, bf16[4,128,1664]{2,1,0:T(8,128)(2,1)S(1)}, u32[]{:S(2)}, u32[]{:S(2)}) %collective-permute-start.22) | collective-permute-done | bytes 1703968 | tf_op jit(solution)/shard_map/ppermute | solution.py:144
  271.3 4.7 collective-permute-start.27
  277.9 5.3 %collective-permute-done.24 = bf16[128,1664]{1,0:T(8,128)(2,1)S(1)} collective-permute-done((bf16[128,1664]{1,0:T(8,128)(2,1)S(1)}, bf16[128,1664]{1,0:T(8,128)(2,1)S(1)}, u32[]{:S(2)}, u32[]{:S(2)}) %collective-permute-start.24) | collective-permute-done | bytes 426016 | tf_op jit(solution)/shard_map/ppermute | solution.py:144
  283.3 6.4 %collective-permute-done.25 = bf16[128,1664]{1,0:T(8,128)(2,1)S(1)} collective-permute-done((bf16[128,1664]{1,0:T(8,128)(2,1)S(1)}, bf16[128,1664]{1,0:T(8,128)(2,1)S(1)}, u32[]{:S(2)}, u32[]{:S(2)}) %collective-permute-start.25) | collective-permute-done | bytes 426016 | tf_op jit(solution)/shard_map/ppermute | solution.py:144
  304.4 5.5 %all-to-all-start.1 = ((bf16[8,128,192]{1,2,0:T(8,128)(2,1)}), bf16[8,128,192]{1,2,0:T(8,128)(2,1)S(1)}, u32[]{:S(2)}, u32[]{:S(2)}) async-start(bf16[8,128,192]{1,2,0:T(8,128)(2,1)} %pad_maximum_fusion.4), calls=%async_computation.1 | async-start | bytes 786432 | tf_op jit(solution)/shard_map/all_to_all | solution.py:555
  312.4 18.6 %collective-permute-done.29 = bf16[396,128]{1,0:T(8,128)(2,1)S(1)} collective-permute-done((bf16[396,128]{1,0:T(8,128)(2,1)S(1)}, bf16[396,128]{1,0:T(8,128)(2,1)S(1)}, u32[]{:S(2)}, u32[]{:S(2)}) %collective-permute-start.29) | collective-permute-done | bytes 101408 | tf_op jit(solution)/shard_map/ppermute | solution.py:221
  336.9 5.0 collective-permute-done.30
  342.4 6.0 %fusion = (f32[3,1024]{1,0:T(4,128)S(1)}, f32[1024,1024,3]{1,0,2:T(8,128)S(1)}) fusion(f32[3,1024,1024]{1,2,0:T(8,128)} %copy-done.11, f32[3,1024]{1,0:T(4,128)S(1)} %log_add_fusion, bf16[1024,3,64]{0,2,1:T(8,128)(2,1)S(1)} %reshape_reshape.3, f32[1024,320]{0,1:T(8,128)} %copy-done.21), kind=kOutput, calls=%fused_computation.2 | convolution fusion | flops 412087296 | bytes 25714688 | tf_op jit(solution)/shard_map/qrd,kd->rqk/dot_general | solution.py:105
  348.4 7.7 %fusion.2 = bf16[3,1024,1024]{1,2,0:T(8,128)(2,1)S(1)} fusion(f32[1024,1024,3]{1,0,2:T(8,128)S(1)} %get-tuple-element.270, f32[3,1024,1024]{1,2,0:T(8,128)} %copy-done.11, f32[3,1024]{1,0:T(4,128)S(1)} %get-tuple-element.269, f32[3,1024]{1,0:T(4,128)S(1)} %log_add_fusion), kind=kLoop, calls=%fused_computation.4 | loop fusion | flops 12582912 | bytes 31481856 | tf_op jit(solution)/shard_map/convert_element_type | solution.py:107
  363.2 9.9 %collective-permute-done.32 = bf16[4,128,1536]{2,1,0:T(8,128)(2,1)} collective-permute-done((bf16[4,128,1536]{2,1,0:T(8,128)(2,1)}, bf16[4,128,1536]{2,1,0:T(8,128)(2,1)}, u32[]{:S(2)}, u32[]{:S(2)}) %collective-permute-start.32) | collective-permute-done | bytes 1572896 | tf_op jit(solution)/shard_map/ppermute | solution.py:144
  373.1 4.1 fusion.56
  392.7 8.0 %all-to-all-start.2 = ((bf16[32,208,128]{2,1,0:T(8,128)(2,1)}), bf16[32,208,128]{2,1,0:T(8,128)(2,1)S(1)}, u32[]{:S(2)}, u32[]{:S(2)}) async-start(bf16[32,208,128]{2,1,0:T(8,128)(2,1)} %bitcast.61), calls=%async_computation.2 | async-start | bytes 3407872 | tf_op jit(solution)/shard_map/all_to_all | solution.py:580
  404.4 18.0 %collective-permute-done.45 = f32[1536]{0:T(1024)S(1)} collective-permute-done((f32[1536]{0:T(1024)S(1)}, f32[1536]{0:T(1024)S(1)}, u32[]{:S(2)}, u32[]{:S(2)}) %collective-permute-start.45) | collective-permute-done | bytes 6176 | tf_op jit(solution)/shard_map/ppermute | solution.py:221
  437.0 6.3 %collective-permute-done.42 = bf16[128,1536]{1,0:T(8,128)(2,1)S(1)} collective-permute-done((bf16[128,1536]{1,0:T(8,128)(2,1)S(1)}, bf16[128,1536]{1,0:T(8,128)(2,1)S(1)}, u32[]{:S(2)}, u32[]{:S(2)}) %collective-permute-start.42) | collective-permute-done | bytes 393248 | tf_op jit(solution)/shard_map/ppermute | solution.py:200
  447.5 8.8 %all-to-all-start.3 = ((bf16[32,240,128]{2,1,0:T(8,128)(2,1)}), bf16[32,240,128]{2,1,0:T(8,128)(2,1)S(1)}, u32[]{:S(2)}, u32[]{:S(2)}) async-start(bf16[32,240,128]{2,1,0:T(8,128)(2,1)} %broadcast_in_dim.106), calls=%async_computation.3 | async-start | bytes 3932160 | tf_op jit(solution)/shard_map/all_to_all | solution.py:588
  462.0 6.5 %collective-permute-done.44 = bf16[128,1536]{1,0:T(8,128)(2,1)S(1)} collective-permute-done((bf16[128,1536]{1,0:T(8,128)(2,1)S(1)}, bf16[128,1536]{1,0:T(8,128)(2,1)S(1)}, u32[]{:S(2)}, u32[]{:S(2)}) %collective-permute-start.44) | collective-permute-done | bytes 393248 | tf_op jit(solution)/shard_map/ppermute | solution.py:200
  474.5 8.7 %all-to-all-done.3 = bf16[32,240,128]{2,1,0:T(8,128)(2,1)S(1)} async-done(((bf16[32,240,128]{2,1,0:T(8,128)(2,1)}), bf16[32,240,128]{2,1,0:T(8,128)(2,1)S(1)}, u32[]{:S(2)}, u32[]{:S(2)}) %all-to-all-start.3) | async-done | bytes 1966112 | tf_op jit(solution)/shard_map/all_to_all | solution.py:588
  (332 shorter events, 192.2 us)
Async XLA Ops:
  7.2 68.5 %all-gather.4.cloned.1.call-start = ((), (), s32[]{:S(2)}) async-start(), calls=%async_computation.5 | async-start | bytes 3538944 | tf_op jit(solution)/shard_map/all_gather | solution.py:455
  11.0 149.1 %all-gather.6.cloned.1.call-start = ((), (), s32[]{:S(2)}) async-start(), calls=%async_computation.6 | async-start | bytes 10027008 | tf_op jit(solution)/shard_map/all_gather | solution.py:481
  27.0 15.4 %collective-permute-start.2 = (bf16[96,1536]{1,0:T(8,128)(2,1)S(1)}, bf16[96,1536]{1,0:T(8,128)(2,1)S(1)}, u32[]{:S(2)}, u32[]{:S(2)}) collective-permute-start(bf16[96,1536]{1,0:T(8,128)(2,1)S(1)} %collective-permute-done), channel_id=1, source_target_pairs={{0,1},{1,2},{2,3},{3,4},{4,5},{5,6},{6,7},{7,0},{8,9},{9,10},{10,1... | collective-permute-start | bytes 884744 | tf_op jit(solution)/shard_map/ppermute | solution.py:179
  42.3 15.5 %collective-permute-start.4 = (bf16[96,1536]{1,0:T(8,128)(2,1)S(1)}, bf16[96,1536]{1,0:T(8,128)(2,1)S(1)}, u32[]{:S(2)}, u32[]{:S(2)}) collective-permute-start(bf16[96,1536]{1,0:T(8,128)(2,1)S(1)} %collective-permute-done.2), channel_id=1, source_target_pairs={{0,1},{1,2},{2,3},{3,4},{4,5},{5,6},{6,7},{7,0},{8,9},{9,10},{10,1... | collective-permute-start | bytes 884744 | tf_op jit(solution)/shard_map/ppermute | solution.py:179
  42.3 15.6 %collective-permute-start.5 = (bf16[96,1536]{1,0:T(8,128)(2,1)S(1)}, bf16[96,1536]{1,0:T(8,128)(2,1)S(1)}, u32[]{:S(2)}, u32[]{:S(2)}) collective-permute-start(bf16[96,1536]{1,0:T(8,128)(2,1)S(1)} %collective-permute-done.3), channel_id=1, source_target_pairs={{0,7},{1,0},{2,1},{3,2},{4,3},{5,4},{6,5},{7,6},{8,15},{9,8},{10,9... | collective-permute-start | bytes 884744 | tf_op jit(solution)/shard_map/ppermute | solution.py:179
  77.8 41.5 %collective-permute-start.11 = (bf16[8,96,1536]{2,1,0:T(8,128)(2,1)}, bf16[8,96,1536]{2,1,0:T(8,128)(2,1)}, u32[]{:S(2)}, u32[]{:S(2)}) collective-permute-start(bf16[8,96,1536]{2,1,0:T(8,128)(2,1)} %bitcast_dynamic-update-slice_fusion.7), channel_id=1, source_target_pairs={{0,128},{128,0},{1,129},{129,1},{2,130},{130,2},{3,131},{131,3},{4... | collective-permute-start | bytes 7077896 | tf_op jit(solution)/shard_map/ppermute | solution.py:231
  93.9 23.2 %all-to-all-start = ((bf16[8,128,192]{1,2,0:T(8,128)(2,1)}), bf16[8,128,192]{1,2,0:T(8,128)(2,1)S(1)}, u32[]{:S(2)}, u32[]{:S(2)}) async-start(bf16[8,128,192]{1,2,0:T(8,128)(2,1)} %copy.87), calls=%async_computation | async-start | bytes 786432 | tf_op jit(solution)/shard_map/all_to_all | solution.py:486
  97.9 290.0 %all-gather.8.cloned.1.call-start = ((), (), s32[]{:S(2)}) async-start(), calls=%async_computation.7 | async-start | bytes 3538944 | tf_op jit(solution)/shard_map/all_gather | solution.py:567
  98.0 25.2 %collective-permute-start.14 = (bf16[4,128,1664]{2,1,0:T(8,128)(2,1)}, bf16[4,128,1664]{2,1,0:T(8,128)(2,1)}, u32[]{:S(2)}, u32[]{:S(2)}) collective-permute-start(bf16[4,128,1664]{2,1,0:T(8,128)(2,1)} %pad_maximum_fusion.cots_ref), channel_id=1, source_target_pairs={{0,64},{8,72},{16,80},{24,88},{32,96},{40,104},{48,112},{56,120},{... | collective-permute-start | bytes 5111816 | tf_op jit(solution)/shard_map/ppermute | solution.py:144
  100.8 38.4 %collective-permute-start.13 = (bf16[4,128,1664]{2,1,0:T(8,128)(2,1)}, bf16[4,128,1664]{2,1,0:T(8,128)(2,1)}, u32[]{:S(2)}, u32[]{:S(2)}) collective-permute-start(bf16[4,128,1664]{2,1,0:T(8,128)(2,1)} %pad_maximum_fusion.cots_ref), channel_id=1, source_target_pairs={{0,96},{8,104},{16,112},{24,120},{32,0},{40,8},{48,16},{56,24},{64... | collective-permute-start | bytes 5111816 | tf_op jit(solution)/shard_map/ppermute | solution.py:144
  101.7 37.6 %collective-permute-start.12 = (bf16[4,128,1664]{2,1,0:T(8,128)(2,1)}, bf16[4,128,1664]{2,1,0:T(8,128)(2,1)}, u32[]{:S(2)}, u32[]{:S(2)}) collective-permute-start(bf16[4,128,1664]{2,1,0:T(8,128)(2,1)} %pad_maximum_fusion.cots_ref), channel_id=1, source_target_pairs={{0,32},{8,40},{16,48},{24,56},{32,64},{40,72},{48,80},{56,88},{64,... | collective-permute-start | bytes 5111816 | tf_op jit(solution)/shard_map/ppermute | solution.py:144
  156.3 22.8 %collective-permute-start.20 = (bf16[4,128,1664]{2,1,0:T(8,128)(2,1)}, bf16[4,128,1664]{2,1,0:T(8,128)(2,1)}, u32[]{:S(2)}, u32[]{:S(2)}) collective-permute-start(bf16[4,128,1664]{2,1,0:T(8,128)(2,1)} %pad_maximum_fusion.1.rows_ref), channel_id=1, source_target_pairs={{0,64},{8,72},{16,80},{24,88},{32,96},{40,104},{48,112},{56,120},{... | collective-permute-start | bytes 5111816 | tf_op jit(solution)/shard_map/ppermute | solution.py:144
  158.7 38.4 %collective-permute-start.19 = (bf16[4,128,1664]{2,1,0:T(8,128)(2,1)}, bf16[4,128,1664]{2,1,0:T(8,128)(2,1)}, u32[]{:S(2)}, u32[]{:S(2)}) collective-permute-start(bf16[4,128,1664]{2,1,0:T(8,128)(2,1)} %pad_maximum_fusion.1.rows_ref), channel_id=1, source_target_pairs={{0,96},{8,104},{16,112},{24,120},{32,0},{40,8},{48,16},{56,24},{64... | collective-permute-start | bytes 5111816 | tf_op jit(solution)/shard_map/ppermute | solution.py:144
  159.6 37.8 %collective-permute-start.18 = (bf16[4,128,1664]{2,1,0:T(8,128)(2,1)}, bf16[4,128,1664]{2,1,0:T(8,128)(2,1)}, u32[]{:S(2)}, u32[]{:S(2)}) collective-permute-start(bf16[4,128,1664]{2,1,0:T(8,128)(2,1)} %pad_maximum_fusion.1.rows_ref), channel_id=1, source_target_pairs={{0,32},{8,40},{16,48},{24,56},{32,64},{40,72},{48,80},{56,88},{64,... | collective-permute-start | bytes 5111816 | tf_op jit(solution)/shard_map/ppermute | solution.py:144
  212.2 50.7 %collective-permute-start.21 = (bf16[4,128,1664]{2,1,0:T(8,128)(2,1)}, bf16[4,128,1664]{2,1,0:T(8,128)(2,1)S(1)}, u32[]{:S(2)}, u32[]{:S(2)}) collective-permute-start(bf16[4,128,1664]{2,1,0:T(8,128)(2,1)} %get-tuple-element.108), channel_id=1, source_target_pairs={{0,96},{8,104},{16,112},{24,120},{32,0},{40,8},{48,16},{56,24},{64... | collective-permute-start | bytes 5111816 | tf_op jit(solution)/shard_map/ppermute | solution.py:144
  229.7 40.6 %collective-permute-start.22 = (bf16[4,128,1664]{2,1,0:T(8,128)(2,1)}, bf16[4,128,1664]{2,1,0:T(8,128)(2,1)S(1)}, u32[]{:S(2)}, u32[]{:S(2)}) collective-permute-start(bf16[4,128,1664]{2,1,0:T(8,128)(2,1)} %get-tuple-element.111), channel_id=1, source_target_pairs={{0,32},{8,40},{16,48},{24,56},{32,64},{40,72},{48,80},{56,88},{64,... | collective-permute-start | bytes 5111816 | tf_op jit(solution)/shard_map/ppermute | solution.py:144
  245.4 25.0 %collective-permute-start.23 = (bf16[4,128,1664]{2,1,0:T(8,128)(2,1)}, bf16[4,128,1664]{2,1,0:T(8,128)(2,1)S(1)}, u32[]{:S(2)}, u32[]{:S(2)}) collective-permute-start(bf16[4,128,1664]{2,1,0:T(8,128)(2,1)} %get-tuple-element.114), channel_id=1, source_target_pairs={{0,64},{8,72},{16,80},{24,88},{32,96},{40,104},{48,112},{56,120},{... | collective-permute-start | bytes 5111816 | tf_op jit(solution)/shard_map/ppermute | solution.py:144
  271.3 18.6 %collective-permute-start.27 = (bf16[6,768,512]{2,1,0:T(8,128)(2,1)S(1)}, bf16[6,768,512]{2,1,0:T(8,128)(2,1)S(1)}, u32[]{:S(2)}, u32[]{:S(2)}) collective-permute-start(bf16[6,768,512]{2,1,0:T(8,128)(2,1)S(1)} %copy-done.50), channel_id=1, source_target_pairs={{0,128},{128,0},{1,129},{129,1},{2,130},{130,2},{3,131},{131,3},{4... | collective-permute-start | bytes 14155784 | tf_op jit(solution)/shard_map/ppermute | solution.py:231
  304.4 37.5 %all-to-all-start.1 = ((bf16[8,128,192]{1,2,0:T(8,128)(2,1)}), bf16[8,128,192]{1,2,0:T(8,128)(2,1)S(1)}, u32[]{:S(2)}, u32[]{:S(2)}) async-start(bf16[8,128,192]{1,2,0:T(8,128)(2,1)} %pad_maximum_fusion.4), calls=%async_computation.1 | async-start | bytes 786432 | tf_op jit(solution)/shard_map/all_to_all | solution.py:555
  309.9 173.3 %reduce-scatter.2.cloned.1.call-start = ((), (), s32[]{:S(2)}) async-start(), calls=%async_computation.8 | async-start | bytes 5308416 | tf_op jit(solution)/shard_map/reduce_scatter | solution.py:529
  310.0 21.1 %collective-permute-start.29 = (bf16[396,128]{1,0:T(8,128)(2,1)S(1)}, bf16[396,128]{1,0:T(8,128)(2,1)S(1)}, u32[]{:S(2)}, u32[]{:S(2)}) collective-permute-start(bf16[396,128]{1,0:T(8,128)(2,1)S(1)} %fusion.85), channel_id=1, source_target_pairs={{0,2},{1,3},{2,0},{3,1},{4,6},{5,7},{6,4},{7,5},{8,10},{9,11},{10,... | collective-permute-start | bytes 304136 | tf_op jit(solution)/shard_map/ppermute | solution.py:221
  334.9 28.2 %collective-permute-start.31 = (bf16[4,128,1536]{2,1,0:T(8,128)(2,1)}, bf16[4,128,1536]{2,1,0:T(8,128)(2,1)}, u32[]{:S(2)}, u32[]{:S(2)}) collective-permute-start(bf16[4,128,1536]{2,1,0:T(8,128)(2,1)} %get-tuple-element.155), channel_id=1, source_target_pairs={{0,96},{8,104},{16,112},{24,120},{32,0},{40,8},{48,16},{56,24},{64... | collective-permute-start | bytes 4718600 | tf_op jit(solution)/shard_map/ppermute | solution.py:144
  335.0 38.0 %collective-permute-start.32 = (bf16[4,128,1536]{2,1,0:T(8,128)(2,1)}, bf16[4,128,1536]{2,1,0:T(8,128)(2,1)}, u32[]{:S(2)}, u32[]{:S(2)}) collective-permute-start(bf16[4,128,1536]{2,1,0:T(8,128)(2,1)} %get-tuple-element.156), channel_id=1, source_target_pairs={{0,32},{8,40},{16,48},{24,56},{32,64},{40,72},{48,80},{56,88},{64,... | collective-permute-start | bytes 4718600 | tf_op jit(solution)/shard_map/ppermute | solution.py:144
  336.5 36.6 %collective-permute-start.33 = (bf16[4,128,1536]{2,1,0:T(8,128)(2,1)}, bf16[4,128,1536]{2,1,0:T(8,128)(2,1)}, u32[]{:S(2)}, u32[]{:S(2)}) collective-permute-start(bf16[4,128,1536]{2,1,0:T(8,128)(2,1)} %get-tuple-element.157), channel_id=1, source_target_pairs={{0,64},{8,72},{16,80},{24,88},{32,96},{40,104},{48,112},{56,120},{... | collective-permute-start | bytes 4718600 | tf_op jit(solution)/shard_map/ppermute | solution.py:144
  392.7 53.0 %all-to-all-start.2 = ((bf16[32,208,128]{2,1,0:T(8,128)(2,1)}), bf16[32,208,128]{2,1,0:T(8,128)(2,1)S(1)}, u32[]{:S(2)}, u32[]{:S(2)}) async-start(bf16[32,208,128]{2,1,0:T(8,128)(2,1)} %bitcast.61), calls=%async_computation.2 | async-start | bytes 3407872 | tf_op jit(solution)/shard_map/all_to_all | solution.py:580
  402.9 27.3 %collective-permute-start.40 = (bf16[128,1536]{1,0:T(8,128)(2,1)}, bf16[128,1536]{1,0:T(8,128)(2,1)}, u32[]{:S(2)}, u32[]{:S(2)}) collective-permute-start(bf16[128,1536]{1,0:T(8,128)(2,1)} %get-tuple-element.229), channel_id=1, source_target_pairs={{0,7},{1,0},{2,1},{3,2},{4,3},{5,4},{6,5},{7,6},{8,15},{9,8},{10,9... | collective-permute-start | bytes 1179656 | tf_op jit(solution)/shard_map/ppermute | solution.py:200
  403.9 29.0 %collective-permute-start.38 = (bf16[128,1536]{1,0:T(8,128)(2,1)S(1)}, bf16[128,1536]{1,0:T(8,128)(2,1)}, u32[]{:S(2)}, u32[]{:S(2)}) collective-permute-start(bf16[128,1536]{1,0:T(8,128)(2,1)S(1)} %get-tuple-element.230), channel_id=1, source_target_pairs={{0,1},{1,2},{2,3},{3,4},{4,5},{5,6},{6,7},{7,0},{8,9},{9,10},{10,1... | collective-permute-start | bytes 1179656 | tf_op jit(solution)/shard_map/ppermute | solution.py:200
  404.3 18.1 %collective-permute-start.45 = (f32[1536]{0:T(1024)S(1)}, f32[1536]{0:T(1024)S(1)}, u32[]{:S(2)}, u32[]{:S(2)}) collective-permute-start(f32[1536]{0:T(1024)S(1)} %div.49), channel_id=1, source_target_pairs={{0,1},{1,0},{2,3},{3,2},{4,5},{5,4},{6,7},{7,6},{8,9},{9,8},{10,11... | collective-permute-start | bytes 18440 | tf_op jit(solution)/shard_map/ppermute | solution.py:221
  425.0 34.8 %collective-permute-start.34 = (bf16[128,1536]{1,0:T(8,128)(2,1)}, bf16[128,1536]{1,0:T(8,128)(2,1)}, u32[]{:S(2)}, u32[]{:S(2)}) collective-permute-start(bf16[128,1536]{1,0:T(8,128)(2,1)} %get-tuple-element.159), channel_id=1, source_target_pairs={{0,24},{8,0},{16,8},{24,16},{32,56},{40,32},{48,40},{56,48},{64,88... | collective-permute-start | bytes 1179656 | tf_op jit(solution)/shard_map/ppermute | solution.py:144
  427.7 32.1 %collective-permute-start.35 = (bf16[128,1536]{1,0:T(8,128)(2,1)}, bf16[128,1536]{1,0:T(8,128)(2,1)}, u32[]{:S(2)}, u32[]{:S(2)}) collective-permute-start(bf16[128,1536]{1,0:T(8,128)(2,1)} %get-tuple-element.160), channel_id=1, source_target_pairs={{0,8},{8,16},{16,24},{24,0},{32,40},{40,48},{48,56},{56,32},{64,72... | collective-permute-start | bytes 1179656 | tf_op jit(solution)/shard_map/ppermute | solution.py:144
  427.7 32.1 %collective-permute-start.36 = (bf16[128,1536]{1,0:T(8,128)(2,1)}, bf16[128,1536]{1,0:T(8,128)(2,1)}, u32[]{:S(2)}, u32[]{:S(2)}) collective-permute-start(bf16[128,1536]{1,0:T(8,128)(2,1)} %get-tuple-element.161), channel_id=1, source_target_pairs={{0,16},{8,24},{16,0},{24,8},{32,48},{40,56},{48,32},{56,40},{64,80... | collective-permute-start | bytes 1179656 | tf_op jit(solution)/shard_map/ppermute | solution.py:144
  447.5 35.7 %all-to-all-start.3 = ((bf16[32,240,128]{2,1,0:T(8,128)(2,1)}), bf16[32,240,128]{2,1,0:T(8,128)(2,1)S(1)}, u32[]{:S(2)}, u32[]{:S(2)}) async-start(bf16[32,240,128]{2,1,0:T(8,128)(2,1)} %broadcast_in_dim.106), calls=%async_computation.3 | async-start | bytes 3932160 | tf_op jit(solution)/shard_map/all_to_all | solution.py:588
  (81 other events, 938.6 us)
Sparse Core Ops, SparseCore 0:
  11.1 64.5 all-gather.3
  78.2 68.2 all-gather.5
  296.4 58.9 all-gather.7
  357.8 72.1 reduce-scatter.1

commit v4 on v3

v4 whole, which is shorter than its diff:
```python
import functools

import jax
import jax.numpy as jnp
from jax import lax
from jax.experimental import pallas as pl
from jax.experimental.layout import Layout, with_layout_constraint
from jax.experimental.pallas import tpu as pltpu
from jax.sharding import PartitionSpec as P

HEAD_DIM = 64
HALF = HEAD_DIM // 2
TOP = 8
CAP = 64
EXPERTS = 32
HOLDERS = 16
LANES = 128

epsilon_norm = 1e-06
rope_theta = 10000.0
masked_score = -1e30
QUERY_ROWS = 512
SCALE = HEAD_DIM ** (-0.5)
f32 = jnp.float32
bf16 = jnp.bfloat16


def rms_inverse(values):
    return lax.rsqrt(jnp.mean(values * values, axis=-1, keepdims=True) + epsilon_norm)


def rms_backward(values, inverse, norm_gain, grad_out):
    scaled = grad_out * norm_gain
    grad_in = inverse * scaled - values * (inverse * inverse * inverse) * jnp.mean(
        scaled * values, axis=-1, keepdims=True
    )
    return (grad_in, jnp.sum(grad_out * values * inverse, axis=0))


def dot32(left, right):
    return jnp.dot(left, right, preferred_element_type=f32)


def split_two(values):
    high = values.astype(bf16)
    return high, (values - high.astype(f32)).astype(bf16)


SIDE = 4
STEPS = (0, 1, -1, 2)


def by_rows(values):
    return with_layout_constraint(values, Layout(major_to_minor=tuple(range(values.ndim))))


def cross(values, stage, step):
    pairs = []
    plane = SIDE * SIDE
    for core in range(2):
        for x in range(SIDE):
            for y in range(SIDE):
                if core == stage:
                    to = x * SIDE + (y + step) % SIDE
                else:
                    to = (x + step) % SIDE * SIDE + y
                pairs.append((core * plane + x * SIDE + y, core * plane + to))
    return lax.ppermute(values, ("dp", "expert"), pairs)


def gather_first(values):
    values = by_rows(values)
    line = jnp.stack([values] + [cross(values, 0, step) for step in STEPS[1:]])
    return by_rows(line)


def gather_second(line):
    return [line] + [cross(line, 1, step) for step in STEPS[1:]]


def scatter_first(parts):
    arrived = [parts[0]] + [
        by_rows(cross(part, 1, -step)) for part, step in zip(parts[1:], STEPS[1:])
    ]
    return [
        by_rows(sum(part[place].astype(f32) for part in arrived).astype(bf16))
        for place in range(SIDE)
    ]


def scatter_second(line):
    arrived = [line[0]] + [cross(part, 0, -step) for part, step in zip(line[1:], STEPS[1:])]
    return by_rows(sum(part.astype(f32) for part in arrived))


def ring_gather(block):
    size = lax.axis_size("tensor")
    me = lax.axis_index("tensor")
    half = block.shape[0] // 2
    held = jnp.zeros((size,) + block.shape, block.dtype)

    def shift(values, step):
        return lax.ppermute(values, "tensor", [(i, (i + step) % size) for i in range(size)])

    def put(held, values, place, row):
        return lax.dynamic_update_slice(held, values[None], ((me + place) % size, row, 0))

    held = put(held, block, 0, 0)
    up = down = block
    for step in range(1, size // 2):
        up, down = shift(up, 1), shift(down, -1)
        held = put(held, up, size - step, 0)
        held = put(held, down, step, 0)
    held = put(held, shift(up[:half], 1), size // 2, 0)
    return put(held, shift(down[half:], -1), size // 2, half)


def ring_scatter(parts):
    size = lax.axis_size("tensor")
    me = lax.axis_index("tensor")
    half = parts.shape[1] // 2

    def shift(values, step):
        return lax.ppermute(values, "tensor", [(i, (i + step) % size) for i in range(size)])

    def part_for(place):
        return lax.dynamic_index_in_dim(parts, (me + place) % size, 0, keepdims=False)

    far = part_for(size // 2)
    up, down = shift(far[:half], 1), shift(far[half:], -1)
    up = jnp.pad(up, ((0, half), (0, 0)))
    down = jnp.pad(down, ((half, 0), (0, 0)))
    for place in range(size // 2 - 1, 0, -1):
        up = (part_for(place).astype(f32) + up.astype(f32)).astype(bf16)
        down = (part_for(-place).astype(f32) + down.astype(f32)).astype(bf16)
        up, down = together(shift(by_rows(up), 1), shift(by_rows(down), -1))
    return part_for(0).astype(f32) + up.astype(f32) + down.astype(f32)


def ring_sum(values):
    size = lax.axis_size("tensor")
    step = 1
    while step < size:
        pairs = [(i, i ^ step) for i in range(size)]
        values = values + lax.ppermute(values, "tensor", pairs)
        step *= 2
    return values


def together(*values):
    return lax.optimization_barrier(values)


def swap_cores(values):
    return lax.ppermute(values, "dp", [(0, 1), (1, 0)])


def contract(left, right, left_dim, right_dim):
    return lax.dot_general(
        left, right, (((left_dim,), (right_dim,)), ((), ())), preferred_element_type=f32
    )


def allowed(rows, first, wide, col_ref, row_ref):
    query = first + lax.broadcasted_iota(jnp.int32, (rows, wide), 0)
    key = lax.broadcasted_iota(jnp.int32, (rows, wide), 1)
    return (key <= query) & (col_ref[first : first + rows, :] == row_ref[:, :wide])


def probabilities(query, key, mask):
    scores = jnp.where(mask, contract(query, key, 1, 1), masked_score)
    weights = jnp.exp(scores - jnp.max(scores, axis=1, keepdims=True))
    return weights * (1.0 / jnp.sum(weights, axis=1, keepdims=True))


def turn(values, cosine, low, high):
    size = values.shape[1]
    return (
        values * cosine
        + pltpu.roll(values, size - HALF, 1) * low
        + pltpu.roll(values, HALF, 1) * high
    )


def attention_kernel(
    x_ref, w_ref, col_ref, row_ref, cos_ref, low_ref, high_ref, out_ref, turned_ref, qkv_ref
):
    seq_len = x_ref.shape[0]
    tokens = turned_ref.shape[2]
    heads = out_ref.shape[1] // HEAD_DIM
    last = (heads + 1) * HEAD_DIM
    step = QUERY_ROWS
    for first in range(0, seq_len, step):
        at = slice(first, first + step)
        wide = first + step
        joined = jnp.dot(x_ref[at, :], w_ref[...], preferred_element_type=f32)
        turned_part = turn(joined[:, :last], cos_ref[at, :], low_ref[at, :], high_ref[at, :])
        qkv_ref[at, :last] = turned_part.astype(bf16)
        qkv_ref[at, last:] = joined[:, last:].astype(bf16)
        mask = allowed(step, first, wide, col_ref, row_ref)
        key = qkv_ref[:wide, heads * HEAD_DIM : last]
        value = qkv_ref[:wide, last:]
        for head in range(heads):
            place = slice(head * HEAD_DIM, (head + 1) * HEAD_DIM)
            query = qkv_ref[at, place] * SCALE
            probs = probabilities(query, key, mask).astype(bf16)
            context = jnp.dot(probs, value, preferred_element_type=f32)
            out_ref[at, place] = context.astype(bf16)
            for block in range(step // tokens):
                turned_ref[first // tokens + block, place, :] = context[
                    block * tokens : (block + 1) * tokens
                ].T.astype(bf16)


def attention_back_kernel(
    qkv_ref, grad_ref, col_ref, row_ref, cos_ref, low_ref, high_ref, out_ref, key_sum, value_sum
):
    seq_len = qkv_ref.shape[0]
    heads = grad_ref.shape[1] // HEAD_DIM
    tokens = grad_ref.shape[2]
    last = (heads + 1) * HEAD_DIM
    step = QUERY_ROWS
    for first in reversed(range(0, seq_len, step)):
        at = slice(first, first + step)
        wide = first + step
        mask = allowed(step, first, wide, col_ref, row_ref)
        key = qkv_ref[:wide, heads * HEAD_DIM : last]
        value = qkv_ref[:wide, last:]
        key_grad = jnp.zeros((wide, HEAD_DIM), f32)
        value_grad = jnp.zeros((wide, HEAD_DIM), f32)
        query_grads = []
        for head in range(heads):
            place = slice(head * HEAD_DIM, (head + 1) * HEAD_DIM)
            query = qkv_ref[at, place] * SCALE
            grad = [
                grad_ref[first // tokens + block, place, :].astype(f32).T.astype(bf16)
                for block in range(step // tokens)
            ]
            grad = jnp.concatenate(grad, axis=0)
            probs = probabilities(query, key, mask)
            probs_grad = contract(grad, value, 1, 1)
            row_dot = jnp.sum(probs * probs_grad, axis=1, keepdims=True)
            score_grad = (probs * (probs_grad - row_dot)).astype(bf16)
            query_grads.append(jnp.dot(score_grad, key, preferred_element_type=f32) * SCALE)
            key_grad += contract(score_grad, query, 0, 0)
            value_grad += contract(probs.astype(bf16), grad, 0, 0)
        if wide == seq_len:
            key_sum[...] = key_grad
            value_sum[...] = value_grad
        else:
            key_sum[:wide, :] += key_grad
            value_sum[:wide, :] += value_grad
        both = jnp.concatenate(query_grads + [key_sum[at, :]], axis=1)
        both = turn(both, cos_ref[at, :], -low_ref[at, :], -high_ref[at, :])
        out_ref[at, :last] = both.astype(bf16)
        out_ref[at, last:] = value_sum[at, :].astype(bf16)


def run_attention(normed_all, joined_weights, marks, tables, planes):
    seq_len = normed_all.shape[0]
    joined_width = joined_weights.shape[1]
    query_width = joined_width - 2 * HEAD_DIM
    vmem = pl.BlockSpec(memory_space=pltpu.VMEM)
    return pl.pallas_call(
        attention_kernel,
        out_shape=(
            jax.ShapeDtypeStruct((seq_len, query_width), bf16),
            jax.ShapeDtypeStruct((planes, query_width, seq_len // planes), bf16),
            jax.ShapeDtypeStruct((seq_len, joined_width), bf16),
        ),
        in_specs=[vmem] * 7,
        out_specs=(vmem,) * 3,
        compiler_params=pltpu.CompilerParams(vmem_limit_bytes=48 * 1024 * 1024),
        cost_estimate=pl.CostEstimate(
            flops=4 << 30, bytes_accessed=8 << 20, transcendentals=0
        ),
    )(normed_all, joined_weights, *marks, *tables)


def run_attention_back(qkv, context_grad, marks, tables):
    seq_len, joined_width = qkv.shape
    vmem = pl.BlockSpec(memory_space=pltpu.VMEM)
    return pl.pallas_call(
        attention_back_kernel,
        out_shape=jax.ShapeDtypeStruct((seq_len, joined_width), bf16),
        in_specs=[vmem] * 7,
        out_specs=vmem,
        scratch_shapes=[pltpu.VMEM((seq_len, HEAD_DIM), f32)] * 2,
        compiler_params=pltpu.CompilerParams(vmem_limit_bytes=48 * 1024 * 1024),
        cost_estimate=pl.CostEstimate(
            flops=8 << 30, bytes_accessed=4 << 20, transcendentals=0
        ),
    )(qkv, context_grad, *marks, *tables)


def rope_tables(seq_len, repeats):
    frequency = rope_theta ** (-2.0 * jnp.arange(HALF, dtype=f32) / HEAD_DIM)
    angles = jnp.arange(seq_len, dtype=f32)[:, None] * frequency[None, :]
    sine = jnp.sin(angles)
    nothing = jnp.zeros_like(sine)

    def heads(first, second):
        return jnp.tile(jnp.concatenate([first, second], axis=1), (1, repeats))

    cosine = jnp.cos(angles)
    return heads(cosine, cosine), heads(-sine, nothing), heads(nothing, sine)


def segment_marks(key_seg):
    marks = jnp.where(key_seg == 0, -1 - jnp.arange(key_seg.shape[0], dtype=jnp.int32), key_seg)
    return marks[:, None], marks[None, :]


def expert_kernel(groups, first_ref, *refs):
    rows_refs, cots_refs, (w_ref,), back_outs, mix_outs, rest = (
        refs[:groups],
        refs[groups : 2 * groups],
        refs[2 * groups : 2 * groups + 1],
        refs[2 * groups + 1 : 3 * groups + 1],
        refs[3 * groups + 1 : 4 * groups + 1],
        refs[4 * groups + 1 :],
    )
    x_ref, c_ref, gate_ref, up_ref, hid_ref, pick_ref, down_ref = rest
    sources, tokens, _ = rows_refs[0].shape
    width = x_ref.shape[2]
    inner = w_ref.shape[2]
    e = pl.program_id(0)
    expert = first_ref[0] + e
    lane = lax.broadcasted_iota(jnp.int32, (CAP, LANES), 1)
    row_id = lax.broadcasted_iota(jnp.int32, (EXPERTS, tokens), 0)
    slot = lax.broadcasted_iota(jnp.int32, (CAP, tokens), 0).astype(f32)
    at = pl.ds(pl.multiple_of(e * CAP, CAP), CAP)
    every = [(group, source) for group in range(groups) for source in range(sources)]
    gates = []
    for order, (group, source) in enumerate(every):
        table = cots_refs[group][source, :EXPERTS, width:].astype(f32)
        rank = jnp.sum(jnp.where(row_id == expert, table, 0.0), axis=0, keepdims=True)
        pick = (rank == slot).astype(bf16)
        pick_ref[order, at] = pick
        rows = jnp.dot(pick, rows_refs[group][source], preferred_element_type=f32)
        cots = jnp.dot(pick, cots_refs[group][source, :, :width], preferred_element_type=f32)
        own = (lane == expert) | (lane == expert + EXPERTS)
        gates.append(jnp.sum(jnp.where(own, rows[:, width:], 0.0), axis=1, keepdims=True))
        x_ref[0, order * CAP : (order + 1) * CAP] = rows[:, :width].astype(bf16)
        c_ref[0, order * CAP : (order + 1) * CAP] = cots.astype(bf16)
    gate = jnp.concatenate(gates, axis=0)

    down_rows = inner // HOLDERS
    chunks = width // inner
    for holder in range(HOLDERS):
        for chunk in range(chunks):
            start = (holder * chunks + chunk) * down_rows
            down_ref[
                holder * down_rows : (holder + 1) * down_rows,
                chunk * inner : (chunk + 1) * inner,
            ] = w_ref[2, start : start + down_rows, :]

    x = x_ref[0]
    gate_pre = jnp.dot(x, w_ref[0], preferred_element_type=f32)
    up_pre = jnp.dot(x, w_ref[1], preferred_element_type=f32)
    back = contract(c_ref[0], down_ref[...], 1, 1)
    sig = 1.0 / (1.0 + jnp.exp(-gate_pre))
    silu = gate_pre * sig
    hidden = (silu * up_pre).astype(bf16)
    gate_grad = jnp.sum(back * hidden.astype(f32), axis=1, keepdims=True)
    grad = gate * back
    gate_pre_grad = (grad * up_pre * (sig + silu * (1.0 - sig))).astype(bf16)
    up_pre_grad = (grad * silu).astype(bf16)
    gate_ref[0] = gate_pre_grad
    up_ref[0] = up_pre_grad
    hid_ref[0] = (gate * hidden.astype(f32)).astype(bf16)
    row_grad = contract(gate_pre_grad, w_ref[0], 1, 1) + contract(up_pre_grad, w_ref[1], 1, 1)
    high = gate_grad.astype(bf16).astype(f32)
    lane = lax.broadcasted_iota(jnp.int32, (len(every) * CAP, LANES), 1)
    tail = jnp.where(lane == expert, high, 0.0)
    tail += jnp.where(lane == expert + EXPERTS, gate_grad - high, 0.0)
    for order, (group, source) in enumerate(every):
        place = slice(order * CAP, (order + 1) * CAP)
        back_outs[group][source, at, :width] = row_grad[place].astype(bf16)
        back_outs[group][source, at, width:] = tail[place].astype(bf16)
    mixed = gate * jnp.dot(hidden, down_ref[...], preferred_element_type=f32)
    for order, (group, source) in enumerate(every):
        place = slice(order * CAP, (order + 1) * CAP)
        mix_outs[group][source, at] = mixed[place].astype(bf16)

    @pl.when(e == 1)
    def _():
        for order, (group, source) in enumerate(every):
            pick = pick_ref[order]
            back_outs[group][source] = contract(pick, back_outs[group][source], 0, 0).astype(bf16)
            mix_outs[group][source] = contract(pick, mix_outs[group][source], 0, 0).astype(bf16)


def run_experts(first, rows, cots, weights):
    groups = len(rows)
    sources, tokens, padded = rows[0].shape
    width = padded - LANES
    inner = weights.shape[2]
    slots = groups * sources * CAP

    def once(columns):
        return pl.BlockSpec(
            (sources, tokens, columns), lambda e: (0, 0, 0), pipeline_mode=pl.Buffered(1)
        )

    def by_expert(*shape):
        return pl.BlockSpec(shape, lambda e: (e, 0, 0))

    acts = jax.ShapeDtypeStruct((2, slots, inner), bf16)
    wide = jax.ShapeDtypeStruct((2, slots, width), bf16)
    outs = pl.pallas_call(
        functools.partial(expert_kernel, groups),
        grid=(2,),
        out_shape=(
            *[jax.ShapeDtypeStruct((sources, tokens, padded), bf16)] * groups,
            *[jax.ShapeDtypeStruct((sources, tokens, width), bf16)] * groups,
            wide,
            wide,
            acts,
            acts,
            acts,
        ),
        in_specs=[pl.BlockSpec(memory_space=pltpu.SMEM)]
        + [once(padded)] * (2 * groups)
        + [by_expert(3, width, inner)],
        out_specs=(
            *[once(padded)] * groups,
            *[once(width)] * groups,
            by_expert(1, slots, width),
            by_expert(1, slots, width),
            by_expert(1, slots, inner),
            by_expert(1, slots, inner),
            by_expert(1, slots, inner),
        ),
        scratch_shapes=[
            pltpu.VMEM((groups * sources, 2 * CAP, tokens), bf16),
            pltpu.VMEM((inner, width), bf16),
        ],
        compiler_params=pltpu.CompilerParams(vmem_limit_bytes=56 * 1024 * 1024),
        cost_estimate=pl.CostEstimate(
            flops=2 * 2 * 7 * slots * width * inner, bytes_accessed=24 << 20, transcendentals=0
        ),
    )(first, *rows, *cots, weights)
    return outs[:groups], outs[groups : 2 * groups], outs[2 * groups :]


def weight_grad_kernel(half_ref, *refs):
    groups = (len(refs) - 2) // 5
    x_refs, c_refs, gate_refs, up_refs, hid_refs = (
        refs[i * groups : (i + 1) * groups] for i in range(5)
    )
    outs = refs[5 * groups :]
    width = x_refs[0].shape[2]
    inner = gate_refs[0].shape[2]
    rows = width // 2
    down_rows = inner // HOLDERS
    chunks = width // inner
    for out_ref, half in zip(outs, (1 - half_ref[0], half_ref[0])):
        cols = pl.ds(pl.multiple_of(half * rows, LANES), rows)
        down_cols = pl.ds(pl.multiple_of(half * (inner // 2), LANES), inner // 2)
        gate = jnp.zeros((rows, inner), f32)
        up = jnp.zeros((rows, inner), f32)
        down = jnp.zeros((inner // 2, width), f32)
        for i in range(groups):
            x = x_refs[i][0, :, cols]
            gate += contract(x, gate_refs[i][0], 0, 0)
            up += contract(x, up_refs[i][0], 0, 0)
        out_ref[0] = gate.astype(bf16)
        out_ref[1] = up.astype(bf16)
        for i in range(groups):
            down += contract(hid_refs[i][0, :, down_cols], c_refs[i][0], 0, 0)
        for holder in range(HOLDERS // 2):
            for chunk in range(chunks):
                at = (holder * chunks + chunk) * down_rows
                out_ref[2, at : at + down_rows, :] = down[
                    holder * down_rows : (holder + 1) * down_rows,
                    chunk * inner : (chunk + 1) * inner,
                ].astype(bf16)


def run_weight_grads(core, saved):
    x, c, gate, up, hid = zip(*saved)
    width = x[0].shape[2]
    inner = gate[0].shape[2]
    operands = (*x, *c, *gate, *up, *hid)
    out = jax.ShapeDtypeStruct((6, width // 2, inner), bf16)
    out_spec = pl.BlockSpec((3, width // 2, inner), lambda e: (e, 0, 0))
    return pl.pallas_call(
        weight_grad_kernel,
        grid=(2,),
        out_shape=(out, out),
        in_specs=[pl.BlockSpec(memory_space=pltpu.SMEM)]
        + [pl.BlockSpec((1,) + v.shape[1:], lambda e: (e, 0, 0)) for v in operands],
        out_specs=(out_spec, out_spec),
        compiler_params=pltpu.CompilerParams(vmem_limit_bytes=52 * 1024 * 1024),
        cost_estimate=pl.CostEstimate(
            flops=1 << 28, bytes_accessed=1 << 20, transcendentals=0
        ),
    )(core, *operands)


def local(
    tokens,
    segments,
    routes,
    norm1_gain,
    w_query,
    w_key,
    w_value,
    w_out,
    norm2_gain,
    w_router,
    w_gate,
    w_up,
    w_down,
    cotangent,
):
    tok_rows, width = tokens.shape
    seq_len = segments.shape[1]
    query_width = w_query.shape[1]
    kv_width = w_key.shape[1]
    joined_width = query_width + 2 * kv_width
    local_experts = w_gate.shape[0]
    experts = w_router.shape[1]
    owners = lax.axis_size("expert")
    planes = lax.axis_size("tensor")
    owner = lax.axis_index("expert")
    first_expert = owner * local_experts
    key_seg = segments[0]
    hidden_width = w_gate.shape[2]

    token_f32 = tokens.astype(f32)
    inverse_one = rms_inverse(token_f32)
    normed_low = (token_f32 * inverse_one * norm1_gain).astype(bf16)
    joined_weights = jnp.concatenate([w_query, w_key, w_value], axis=1)
    normed_low = by_rows(normed_low)
    normed_all = lax.all_gather(normed_low, "tensor", axis=0, tiled=True)
    core = lax.axis_index("dp")

    expert_ids = jnp.arange(experts, dtype=jnp.int32)
    onehot = (routes[:, :, None] == expert_ids[None, None, :]).astype(f32)
    member = jnp.sum(onehot, axis=1)
    lower = (jnp.arange(tok_rows)[:, None] <= jnp.arange(tok_rows)[None, :]).astype(bf16)
    rank = jnp.einsum("te,tu->eu", member.astype(bf16), lower, preferred_element_type=f32)
    rank = jnp.where(member.T > 0, rank - 1.0, -1.0).astype(bf16)
    extra = jnp.pad(rank, ((0, tok_rows - experts), (0, LANES - tok_rows)))
    cot_payload = jnp.concatenate([cotangent, extra], axis=1)

    count = w_out.shape[0] // 2
    half_out = ring_gather(lax.dynamic_slice_in_dim(w_out, core * count, count, 0))
    chunks = width // hidden_width
    down_rows = w_down.shape[1]
    part_rows = w_gate.shape[1]
    down_parts = w_down.reshape(local_experts, down_rows, chunks, hidden_width)
    down_parts = down_parts.transpose(0, 2, 1, 3).reshape(local_experts, part_rows, hidden_width)
    weights = jnp.stack([w_gate, w_up, down_parts], axis=1)
    weights = weights.reshape(3 * local_experts, part_rows, hidden_width)
    tables = rope_tables(seq_len, query_width // HEAD_DIM + 1)
    marks = segment_marks(key_seg)
    normed_all, half_out, cot_line, weights, joined_weights, *constants = together(
        normed_all, half_out, gather_first(cot_payload), weights, joined_weights, *tables, *marks
    )
    tables, marks = constants[:3], constants[3:]
    weights_all = lax.all_gather(weights, ("dp", "tensor"), axis=1, tiled=True)
    cot_parts = gather_second(cot_line)

    context, context_blocks, qkv = run_attention(
        normed_all, joined_weights, marks, tables, planes
    )
    context_blocks, cot_parts[1], cot_parts[2] = together(
        context_blocks, cot_parts[1], cot_parts[2]
    )
    context_home = lax.all_to_all(context_blocks, "tensor", split_axis=0, concat_axis=0)
    other_out = swap_cores(half_out)
    w_out_all = jnp.concatenate(
        [jnp.where(core == 0, half_out, other_out), jnp.where(core == 0, other_out, half_out)],
        axis=1,
    ).reshape(planes * query_width, width)
    context_home, w_out_all = together(context_home, w_out_all)
    context_home = context_home.reshape(planes * query_width, tok_rows)
    mid = token_f32 + contract(context_home, w_out_all, 0, 0)
    inverse_two = rms_inverse(mid)
    normed_two = (mid * inverse_two * norm2_gain).astype(bf16)
    logits = dot32(normed_two, w_router)
    logits = jnp.where(member > 0, logits, masked_score)
    chosen_exp = jnp.where(
        member > 0, jnp.exp(logits - jnp.max(logits, axis=1, keepdims=True)), 0.0
    )
    gates = chosen_exp / jnp.sum(chosen_exp, axis=1, keepdims=True)
    gate_high, gate_low = split_two(gates)
    payload = jnp.concatenate(
        [normed_two, gate_high, gate_low, jnp.zeros((tok_rows, LANES - 2 * experts), bf16)],
        axis=1,
    )
    payload, *cot_parts = together(payload, *cot_parts)
    line = gather_first(payload)
    before, behind = (cross(line, 1, step) for step in STEPS[1:3])

    first_expert = first_expert.astype(jnp.int32).reshape(1)
    def compute(rows, cots):
        return run_experts(first_expert, rows, cots, weights_all)

    own = compute([line], cot_parts[:1])
    line, before, behind, *own_saved = together(line, before, behind, *own[2])
    far = cross(line, 1, STEPS[3])
    near = compute([before, behind], cot_parts[1:3])
    far, *near_saved = together(far, *near[2])
    last = compute([far], cot_parts[3:])
    done = [(*own[:2], own_saved), (*near[:2], near_saved), last]
    back_line = scatter_first([part for some in done for part in some[0]])
    *both, given, kept = together(
        *back_line,
        *[part for some in done for part in some[1]],
        *run_weight_grads(core.astype(jnp.int32).reshape(1), [some[2] for some in done]),
    )
    back_line, mix_parts = both[:SIDE], both[SIDE:]
    kept = (kept.astype(f32) + swap_cores(given).astype(f32)).astype(bf16)
    weight_sum = lax.psum_scatter(kept, "tensor", scatter_dimension=1, tiled=True)
    back_home = scatter_second(back_line)
    back_home, kept = together(back_home, kept)

    cot_f32 = cotangent.astype(f32)
    grad_tail = back_home[:, width:]
    gate_grad = grad_tail[:, :experts] + grad_tail[:, experts : 2 * experts]
    chosen_grad = gates * (gate_grad - jnp.sum(gates * gate_grad, axis=1, keepdims=True))
    logit_grad = chosen_grad.astype(bf16)
    normed_two_grad = back_home[:, :width] + jnp.einsum(
        "te,de->td", logit_grad, w_router, preferred_element_type=f32
    )
    mid_part, norm2_part = rms_backward(mid, inverse_two, norm2_gain, normed_two_grad)
    mid_grad = cot_f32 + mid_part
    attention_low = by_rows(mid_grad.astype(bf16))
    context_grad = by_rows(contract(w_out_all, attention_low, 1, 1).astype(bf16))
    context_grad, logit_grad, *mix_parts = together(context_grad, logit_grad, *mix_parts)
    mix_line = scatter_first(mix_parts)
    router_part = contract(normed_two, logit_grad, 0, 0)
    context_grad = lax.all_to_all(
        context_grad.reshape(planes, query_width, tok_rows), "tensor", split_axis=0, concat_axis=0
    )
    joined_grad = run_attention_back(qkv, context_grad, marks, tables)
    normed_one_grad = ring_scatter(
        contract(joined_grad, joined_weights, 1, 1).astype(bf16).reshape(planes, tok_rows, width)
    )
    attention_all = lax.all_gather(attention_low, "tensor", axis=0, tiled=True)
    joined_part = contract(normed_all, joined_grad, 0, 0)
    out_part = contract(attention_all, context, 0, 0)
    norm1_part = jnp.sum(joined_part * joined_weights.astype(f32), axis=1) / norm1_gain

    sharers = lax.axis_size("dp") * owners
    sides = jnp.concatenate([joined_part.astype(bf16), out_part.astype(bf16)], axis=1)
    columns = sides.shape[1]
    block = width // sharers
    shared = jnp.concatenate([router_part.T, norm2_part[None], norm1_part[None]]).astype(bf16)
    shared_size = shared.size
    extra = -(-shared_size // (columns * sharers))
    shared = jnp.pad(shared.reshape(-1), (0, extra * columns * sharers - shared_size))
    blocks = jnp.concatenate(
        [sides.reshape(sharers, block, columns), shared.reshape(sharers, extra, columns)], axis=1
    )
    blocks, *mix_line = together(blocks, *mix_line)
    output = (mid + scatter_second(mix_line)).astype(bf16)
    arrived = lax.all_to_all(blocks, ("dp", "expert"), split_axis=0, concat_axis=0)
    total = jnp.sum(arrived.astype(f32), axis=0).astype(bf16)
    spread = lax.all_to_all(
        jnp.broadcast_to(total[None], arrived.shape), ("dp", "expert"), split_axis=0, concat_axis=0
    )
    spread, weight_sum = together(spread, weight_sum)
    sides = spread[:, :block].reshape(width, columns).astype(f32)
    shared = ring_sum(spread[:, block:].reshape(-1, LANES)).astype(f32).reshape(-1)
    shared = shared[:shared_size].reshape(experts + 2, width)
    joined_sum = sides[:, :joined_width]
    out_sum = sides[:, joined_width:].T
    weight_sum = weight_sum.reshape(local_experts, 3, part_rows, hidden_width)
    w_gate_grad = weight_sum[:, 0].astype(f32)
    w_up_grad = weight_sum[:, 1].astype(f32)
    w_down_grad = weight_sum[:, 2].reshape(local_experts, chunks, down_rows, hidden_width)
    w_down_grad = w_down_grad.transpose(0, 2, 1, 3).reshape(local_experts, down_rows, width)
    w_down_grad = w_down_grad.astype(f32)
    input_part, _ = rms_backward(token_f32, inverse_one, norm1_gain, normed_one_grad)
    input_grad = mid_grad + input_part
    return (
        output,
        input_grad,
        shared[experts + 1],
        joined_sum[:, :query_width],
        joined_sum[:, query_width : query_width + kv_width],
        joined_sum[:, query_width + kv_width :],
        out_sum,
        shared[experts],
        shared[:experts].T,
        w_gate_grad,
        w_up_grad,
        w_down_grad,
    )


def solution(mesh):
    rows = P(("dp", "expert", "tensor"), None)
    columns = P(None, "tensor")
    experts = P("expert", ("dp", "tensor"), None)
    return jax.shard_map(
        local,
        mesh=mesh,
        in_specs=(
            rows,
            P(("dp", "expert"), None),
            rows,
            P(),
            columns,
            columns,
            columns,
            P("tensor", None),
            P(),
            P(),
            experts,
            experts,
            experts,
            rows,
        ),
        out_specs=(
            rows,
            rows,
            P(),
            columns,
            columns,
            columns,
            P("tensor", None),
            P(),
            P(),
            experts,
            experts,
            experts,
        ),
        check_vma=False,
    )
```

time: 517 us -> 495 us (0.957)
  the two profiles are of different devices: /device:TPU:1 before, /device:TPU:9 now
where the time goes in v4:
time: 495 us; the launch traced here: 485 us
  waiting for transfers between devices  152 us (31%)
  starting transfers between devices  117 us (24%)
  Pallas kernels  86.3 us (17%)
  local copies, waits for them, and re-layouts  49.2 us (10%)
  other arithmetic  47.7 us (10%)
  matrix products  18.7 us (4%)
  between operations  15.2 us (3%)
    ppermute x24, waiting for transfers between devices, cross(): return lax.ppermute(values, ('dp', 'expert'), pairs)  54.8 us
    ppermute x24, starting transfers between devices, cross(): return lax.ppermute(values, ('dp', 'expert'), pairs)  53.6 us
    ppermute x16, waiting for transfers between devices, shift(): lax.ppermute(values, 'tensor', [(i, (i + step) % size) for i in range(siz...  51.5 us
    pallas_call x3, Pallas kernels, run_experts(): pl.pallas_call(functools.partial(expert_kernel, groups), grid=(2,), out_s...  50.2 us
    ppermute x16, starting transfers between devices, shift(): lax.ppermute(values, 'tensor', [(i, (i + step) % size) for i in range(siz...  25 us
    unnamed x108, local copies, waits for them, and re-layouts  20.7 us
    dot_general x6, matrix products, contract(): lax.dot_general(left, right, (((left_dim,), (right_dim,)), ((), ())), pre...  16.4 us
    pallas_call x1, Pallas kernels, run_weight_grads(): pl.pallas_call(weight_grad_kernel, grid=(2,), out_shape=(out, out), in_sp...  15.8 us
  transfers between devices with their start and end apart: 53, of which 23 were waited for; matrix products, arithmetic and copies ran while one was open for 17% of the time, Pallas kernels for 18%

profile of v4, /device:TPU:9, one launch (start us, length us, event | category | flops | bytes accessed | tf_op | source)
XLA Modules:
  0.0 485.4 jit_solution(16642794328567720060)
XLA Ops:
  37.7 8.0 %collective-permute-done.2 = bf16[96,1536]{1,0:T(8,128)(2,1)S(1)} collective-permute-done((bf16[96,1536]{1,0:T(8,128)(2,1)S(1)}, bf16[96,1536]{1,0:T(8,128)(2,1)S(1)}, u32[]{:S(2)}, u32[]{:S(2)}) %collective-permute-start.2) | collective-permute-done | bytes 294944 | tf_op jit(solution)/shard_map/ppermute | solution.py:103
  49.9 11.7 %collective-permute-done.4 = bf16[96,1536]{1,0:T(8,128)(2,1)S(1)} collective-permute-done((bf16[96,1536]{1,0:T(8,128)(2,1)S(1)}, bf16[96,1536]{1,0:T(8,128)(2,1)S(1)}, u32[]{:S(2)}, u32[]{:S(2)}) %collective-permute-start.4) | collective-permute-done | bytes 294944 | tf_op jit(solution)/shard_map/ppermute | solution.py:103
  66.1 4.4 collective-permute-done.6
  71.9 6.0 %all-gather.4.cloned.1.call-done.x_ref = bf16[1024,1536]{1,0:T(8,128)(2,1)} async-done(((bf16[128,1536]{1,0:T(8,128)(2,1)}), bf16[1024,1536]{1,0:T(8,128)(2,1)}) %all-gather.4.cloned.1.call-update) | async-done | bytes 3145744 | tf_op jit(solution)/shard_map/all_gather | solution.py:537
  86.7 8.5 %shard_map.229 = (bf16[1024,192]{1,0:T(8,128)(2,1)S(1)}, bf16[8,192,128]{2,1,0:T(8,128)(2,1)S(1)}, bf16[1024,320]{1,0:T(8,128)(2,1)S(1)}) custom-call(bf16[1024,1536]{1,0:T(8,128)(2,1)} %all-gather.4.cloned.1.call-done.x_ref, bf16[1536,320]{1,0:T(8,128)(2,1)} %pad_maximum_fusion.5.w_ref, s32[1024,1]{1,0:T(8,128)S(1)} %copy-done.7, ...), custom_call_target="tpu_custom_call" | custom-call | flops 4294967296 | bytes 8388608 | tf_op jit(solution)/shard_map/pallas_call | solution.py:264
  102.6 4.1 all-to-all-start
  112.1 9.6 %all-to-all-done = bf16[8,192,128]{2,1,0:T(8,128)(2,1)} async-done(((bf16[8,192,128]{2,1,0:T(8,128)(2,1)}), bf16[8,192,128]{2,1,0:T(8,128)(2,1)}, u32[]{:S(2)}, u32[]{:S(2)}) %all-to-all-start) | async-done | bytes 393248 | tf_op jit(solution)/shard_map/all_to_all | solution.py:573
  129.6 5.3 %collective-permute-start.15 = (bf16[128,1664]{1,0:T(8,128)(2,1)}, bf16[128,1664]{1,0:T(8,128)(2,1)S(1)}, u32[]{:S(2)}, u32[]{:S(2)}) collective-permute-start(bf16[128,1664]{1,0:T(8,128)(2,1)} %concatenate.37), channel_id=1, source_target_pairs={{0,8},{8,16},{16,24},{24,0},{32,40},{40,48},{48,56},{56,32},{64,72... | collective-permute-start | bytes 1277960 | tf_op jit(solution)/shard_map/ppermute | solution.py:68
  147.2 20.1 %collective-permute-start.18 = (bf16[4,128,1664]{2,1,0:T(8,128)(2,1)}, bf16[4,128,1664]{2,1,0:T(8,128)(2,1)}, u32[]{:S(2)}, u32[]{:S(2)}) collective-permute-start(bf16[4,128,1664]{2,1,0:T(8,128)(2,1)} %pad_maximum_fusion.3.refs_0_), channel_id=1, source_target_pairs={{0,32},{8,40},{16,48},{24,56},{32,64},{40,72},{48,80},{56,88},{64,... | collective-permute-start | bytes 5111816 | tf_op jit(solution)/shard_map/ppermute | solution.py:68
  167.4 13.5 %shard_map.230 = (bf16[4,128,1664]{2,1,0:T(8,128)(2,1)}, bf16[4,128,1536]{2,1,0:T(8,128)(2,1)}, bf16[2,256,1536]{2,1,0:T(8,128)(2,1)}, bf16[2,256,1536]{2,1,0:T(...) custom-call(s32[1]{0:T(128)} %bitcast.25.first_ref, ...), custom_call_target="tpu_custom_call" | custom-call | flops 5637144576 | bytes 25165824 | tf_op jit(solution)/shard_map/pallas_call | solution.py:411
  180.9 6.3 %collective-permute-done.18.refs_0_ = bf16[4,128,1664]{2,1,0:T(8,128)(2,1)} collective-permute-done((bf16[4,128,1664]{2,1,0:T(8,128)(2,1)}, bf16[4,128,1664]{2,1,0:T(8,128)(2,1)}, u32[]{:S(2)}, u32[]{:S(2)}) %collective-permute-start.18) | collective-permute-done | bytes 1703968 | tf_op jit(solution)/shard_map/ppermute | solution.py:68
  192.8 23.1 %shard_map.231 = (bf16[4,128,1664]{2,1,0:T(8,128)(2,1)}, bf16[4,128,1664]{2,1,0:T(8,128)(2,1)}, bf16[4,128,1536]{2,1,0:T(8,128)(2,1)}, bf16[4,128,1536]{2,1,0:T(...) custom-call(s32[1]{0:T(128)} %bitcast.25.first_ref, ...), custom_call_target="tpu_custom_call" | custom-call | flops 11274289152 | bytes 25165824 | tf_op jit(solution)/shard_map/pallas_call | solution.py:411
  218.7 13.6 %shard_map.232 = (bf16[4,128,1664]{2,1,0:T(8,128)(2,1)}, bf16[4,128,1536]{2,1,0:T(8,128)(2,1)}, bf16[2,256,1536]{2,1,0:T(8,128)(2,1)}, bf16[2,256,1536]{2,1,0:T(...) custom-call(s32[1]{0:T(128)} %bitcast.25.first_ref, ...), custom_call_target="tpu_custom_call" | custom-call | flops 5637144576 | bytes 25165824 | tf_op jit(solution)/shard_map/pallas_call | solution.py:411
  235.7 15.8 %shard_map.233 = (bf16[6,768,512]{2,1,0:T(8,128)(2,1)}, bf16[6,768,512]{2,1,0:T(8,128)(2,1)}) custom-call(s32[1]{0:T(128)} %bitcast.34.half_ref, bf16[2,256,1536]{2,1,0:T(8,128)(2,1)} %get-tuple-element.148.refs_0_, bf16[2,512,1536]{2,1,0:T(8,128)(2,1)} %get-tuple-element.149.refs_1_, bf16[2,256,1536]{2,1,0:T(8,128)(2,1)} %get-tuple-element.150.refs_2_, ...), custom_call_target="tpu_custom_call" | custom-call | flops 268435456 | bytes 1048576 | tf_op jit(solution)/shard_map/pallas_call | solution.py:488
  251.5 4.1 collective-permute-done.23
  258.6 8.0 %collective-permute-start.27 = (bf16[6,768,512]{2,1,0:T(8,128)(2,1)}, bf16[6,768,512]{2,1,0:T(8,128)(2,1)S(1)}, u32[]{:S(2)}, u32[]{:S(2)}) collective-permute-start(bf16[6,768,512]{2,1,0:T(8,128)(2,1)} %get-tuple-element.170), channel_id=1, source_target_pairs={{0,128},{128,0},{1,129},{129,1},{2,130},{130,2},{3,131},{131,3},{4... | collective-permute-start | bytes 14155784 | tf_op jit(solution)/shard_map/ppermute | solution.py:155
  269.4 4.5 collective-permute-done.24
  273.9 5.9 %collective-permute-done.25 = bf16[128,1664]{1,0:T(8,128)(2,1)S(1)} collective-permute-done((bf16[128,1664]{1,0:T(8,128)(2,1)S(1)}, bf16[128,1664]{1,0:T(8,128)(2,1)S(1)}, u32[]{:S(2)}, u32[]{:S(2)}) %collective-permute-start.25) | collective-permute-done | bytes 426016 | tf_op jit(solution)/shard_map/ppermute | solution.py:68
  290.6 4.5 convolution_convert_fusion.2
  295.1 4.1 all-to-all-start.1
  304.7 13.9 %all-to-all-done.1.grad_ref = bf16[8,192,128]{2,1,0:T(8,128)(2,1)} async-done(((bf16[8,192,128]{2,1,0:T(8,128)(2,1)}), bf16[8,192,128]{2,1,0:T(8,128)(2,1)}, u32[]{:S(2)}, u32[]{:S(2)}) %all-to-all-start.1) | async-done | bytes 393248 | tf_op jit(solution)/shard_map/all_to_all | solution.py:637
  320.8 11.8 %shard_map.234 = bf16[1024,320]{1,0:T(8,128)(2,1)S(1)} custom-call(bf16[1024,320]{1,0:T(8,128)(2,1)S(1)} %copy-done.13, bf16[8,192,128]{2,1,0:T(8,128)(2,1)} %all-to-all-done.1.grad_ref, s32[1024,1]{1,0:T(8,128)S(1)} %copy-done.8, s32[1,1024]{1,0:T(1,128)S(1)} %compare_select_fusion.1.row_ref, f32[1024,256]{1,0:T(8,128)S(1)} %copy.101.cos_ref, ...), custom_call_target="tpu_custom_call" | custom-call | flops 8589934592 | bytes 4194304 | tf_op jit(solution)/shard_map/pallas_call | solution.py:283
  355.8 4.3 fusion.26
  365.3 8.2 %all-to-all-start.2 = ((bf16[32,52,512]{2,1,0:T(8,128)(2,1)}), bf16[32,52,512]{2,1,0:T(8,128)(2,1)S(1)}, u32[]{:S(2)}, u32[]{:S(2)}) async-start(bf16[32,52,512]{2,1,0:T(8,128)(2,1)} %pad_maximum_fusion.1), calls=%async_computation.2 | async-start | bytes 3670016 | tf_op jit(solution)/shard_map/all_to_all | solution.py:662
  377.9 17.4 %collective-permute-done.38 = bf16[128,1536]{1,0:T(8,128)(2,1)S(1)} collective-permute-done((bf16[128,1536]{1,0:T(8,128)(2,1)S(1)}, bf16[128,1536]{1,0:T(8,128)(2,1)S(1)}, u32[]{:S(2)}, u32[]{:S(2)}) %collective-permute-start.38) | collective-permute-done | bytes 393248 | tf_op jit(solution)/shard_map/ppermute | solution.py:124
  402.1 9.4 %all-to-all-start.3 = ((bf16[32,52,512]{2,1,0:T(8,128)(2,1)}), bf16[32,52,512]{2,1,0:T(8,128)(2,1)S(1)}, u32[]{:S(2)}, u32[]{:S(2)}) async-start(bf16[32,52,512]{2,1,0:T(8,128)(2,1)} %broadcast_in_dim.88), calls=%async_computation.3 | async-start | bytes 3670016 | tf_op jit(solution)/shard_map/all_to_all | solution.py:664
  411.5 6.1 %collective-permute-done.40 = bf16[128,1536]{1,0:T(8,128)(2,1)S(1)} collective-permute-done((bf16[128,1536]{1,0:T(8,128)(2,1)}, bf16[128,1536]{1,0:T(8,128)(2,1)S(1)}, u32[]{:S(2)}, u32[]{:S(2)}) %collective-permute-start.40) | collective-permute-done | bytes 393248 | tf_op jit(solution)/shard_map/ppermute | solution.py:124
  419.0 4.0 collective-permute-start.31
  426.9 12.4 %collective-permute-done.31 = bf16[128,1536]{1,0:T(8,128)(2,1)S(1)} collective-permute-done((bf16[128,1536]{1,0:T(8,128)(2,1)}, bf16[128,1536]{1,0:T(8,128)(2,1)S(1)}, u32[]{:S(2)}, u32[]{:S(2)}) %collective-permute-start.31) | collective-permute-done | bytes 393248 | tf_op jit(solution)/shard_map/ppermute | solution.py:68
  439.3 5.5 %collective-permute-done.33 = bf16[128,1536]{1,0:T(8,128)(2,1)S(1)} collective-permute-done((bf16[128,1536]{1,0:T(8,128)(2,1)}, bf16[128,1536]{1,0:T(8,128)(2,1)S(1)}, u32[]{:S(2)}, u32[]{:S(2)}) %collective-permute-start.33) | collective-permute-done | bytes 393248 | tf_op jit(solution)/shard_map/ppermute | solution.py:68
  457.9 6.9 %collective-permute-done.43 = bf16[512,128]{1,0:T(8,128)(2,1)S(1)} collective-permute-done((bf16[512,128]{1,0:T(8,128)(2,1)S(1)}, bf16[512,128]{1,0:T(8,128)(2,1)S(1)}, u32[]{:S(2)}, u32[]{:S(2)}) %collective-permute-start.43) | collective-permute-done | bytes 131104 | tf_op jit(solution)/shard_map/ppermute | solution.py:145
  468.8 8.3 %collective-permute-done.44 = bf16[512,128]{1,0:T(8,128)(2,1)S(1)} collective-permute-done((bf16[512,128]{1,0:T(8,128)(2,1)S(1)}, bf16[512,128]{1,0:T(8,128)(2,1)S(1)}, u32[]{:S(2)}, u32[]{:S(2)}) %collective-permute-start.44) | collective-permute-done | bytes 131104 | tf_op jit(solution)/shard_map/ppermute | solution.py:145
  (295 shorter events, 180.8 us)
Async XLA Ops:
  7.2 70.7 %all-gather.4.cloned.1.call-start = ((), (), s32[]{:S(2)}) async-start(), calls=%async_computation.5 | async-start | bytes 3538944 | tf_op jit(solution)/shard_map/all_gather | solution.py:537
  9.8 20.1 %collective-permute-start = (bf16[96,1536]{1,0:T(8,128)(2,1)}, bf16[96,1536]{1,0:T(8,128)(2,1)S(1)}, u32[]{:S(2)}, u32[]{:S(2)}) collective-permute-start(bf16[96,1536]{1,0:T(8,128)(2,1)} %get-tuple-element.240), channel_id=1, source_target_pairs={{0,1},{1,2},{2,3},{3,4},{4,5},{5,6},{6,7},{7,0},{8,9},{9,10},{10,1... | collective-permute-start | bytes 884744 | tf_op jit(solution)/shard_map/ppermute | solution.py:103
  11.4 18.4 %collective-permute-start.1 = (bf16[96,1536]{1,0:T(8,128)(2,1)}, bf16[96,1536]{1,0:T(8,128)(2,1)}, u32[]{:S(2)}, u32[]{:S(2)}) collective-permute-start(bf16[96,1536]{1,0:T(8,128)(2,1)} %get-tuple-element.240), channel_id=1, source_target_pairs={{0,7},{1,0},{2,1},{3,2},{4,3},{5,4},{6,5},{7,6},{8,15},{9,8},{10,9... | collective-permute-start | bytes 884744 | tf_op jit(solution)/shard_map/ppermute | solution.py:103
  16.5 150.9 %all-gather.6.cloned.1.call-start = ((), (), s32[]{:S(2)}) async-start(), calls=%async_computation.6 | async-start | bytes 10027008 | tf_op jit(solution)/shard_map/all_gather | solution.py:564
  79.2 27.5 %collective-permute-start.13 = (bf16[8,96,1536]{2,1,0:T(8,128)(2,1)}, bf16[8,96,1536]{2,1,0:T(8,128)(2,1)}, u32[]{:S(2)}, u32[]{:S(2)}) collective-permute-start(bf16[8,96,1536]{2,1,0:T(8,128)(2,1)} %bitcast_dynamic-update-slice_fusion.7), channel_id=1, source_target_pairs={{0,128},{128,0},{1,129},{129,1},{2,130},{130,2},{3,131},{131,3},{4... | collective-permute-start | bytes 7077896 | tf_op jit(solution)/shard_map/ppermute | solution.py:155
  80.1 21.3 %collective-permute-start.11 = (bf16[4,128,1664]{2,1,0:T(8,128)(2,1)}, bf16[4,128,1664]{2,1,0:T(8,128)(2,1)}, u32[]{:S(2)}, u32[]{:S(2)}) collective-permute-start(bf16[4,128,1664]{2,1,0:T(8,128)(2,1)} %pad_maximum_fusion.2.refs_1_), channel_id=1, source_target_pairs={{0,32},{8,40},{16,48},{24,56},{32,64},{40,72},{48,80},{56,88},{64,... | collective-permute-start | bytes 5111816 | tf_op jit(solution)/shard_map/ppermute | solution.py:68
  81.3 21.3 %collective-permute-start.12 = (bf16[4,128,1664]{2,1,0:T(8,128)(2,1)}, bf16[4,128,1664]{2,1,0:T(8,128)(2,1)}, u32[]{:S(2)}, u32[]{:S(2)}) collective-permute-start(bf16[4,128,1664]{2,1,0:T(8,128)(2,1)} %pad_maximum_fusion.2.refs_1_), channel_id=1, source_target_pairs={{0,96},{8,104},{16,112},{24,120},{32,0},{40,8},{48,16},{56,24},{64... | collective-permute-start | bytes 5111816 | tf_op jit(solution)/shard_map/ppermute | solution.py:68
  81.6 48.0 %collective-permute-start.14 = (bf16[4,128,1664]{2,1,0:T(8,128)(2,1)}, bf16[4,128,1664]{2,1,0:T(8,128)(2,1)}, u32[]{:S(2)}, u32[]{:S(2)}) collective-permute-start(bf16[4,128,1664]{2,1,0:T(8,128)(2,1)} %pad_maximum_fusion.2.refs_1_), channel_id=1, source_target_pairs={{0,64},{8,72},{16,80},{24,88},{32,96},{40,104},{48,112},{56,120},{... | collective-permute-start | bytes 5111816 | tf_op jit(solution)/shard_map/ppermute | solution.py:68
  102.6 19.1 %all-to-all-start = ((bf16[8,192,128]{2,1,0:T(8,128)(2,1)}), bf16[8,192,128]{2,1,0:T(8,128)(2,1)}, u32[]{:S(2)}, u32[]{:S(2)}) async-start(bf16[8,192,128]{2,1,0:T(8,128)(2,1)} %copy-done.9), calls=%async_computation | async-start | bytes 786432 | tf_op jit(solution)/shard_map/all_to_all | solution.py:573
  106.7 253.4 %all-gather.8.cloned.1.call-start = ((), (), s32[]{:S(2)}) async-start(), calls=%async_computation.7 | async-start | bytes 3538944 | tf_op jit(solution)/shard_map/all_gather | solution.py:644
  147.2 40.0 %collective-permute-start.18 = (bf16[4,128,1664]{2,1,0:T(8,128)(2,1)}, bf16[4,128,1664]{2,1,0:T(8,128)(2,1)}, u32[]{:S(2)}, u32[]{:S(2)}) collective-permute-start(bf16[4,128,1664]{2,1,0:T(8,128)(2,1)} %pad_maximum_fusion.3.refs_0_), channel_id=1, source_target_pairs={{0,32},{8,40},{16,48},{24,56},{32,64},{40,72},{48,80},{56,88},{64,... | collective-permute-start | bytes 5111816 | tf_op jit(solution)/shard_map/ppermute | solution.py:68
  167.3 23.0 %collective-permute-start.19 = (bf16[4,128,1664]{2,1,0:T(8,128)(2,1)}, bf16[4,128,1664]{2,1,0:T(8,128)(2,1)}, u32[]{:S(2)}, u32[]{:S(2)}) collective-permute-start(bf16[4,128,1664]{2,1,0:T(8,128)(2,1)} %pad_maximum_fusion.3.refs_0_), channel_id=1, source_target_pairs={{0,96},{8,104},{16,112},{24,120},{32,0},{40,8},{48,16},{56,24},{64... | collective-permute-start | bytes 5111816 | tf_op jit(solution)/shard_map/ppermute | solution.py:68
  190.3 27.2 %collective-permute-start.22 = (bf16[4,128,1664]{2,1,0:T(8,128)(2,1)}, bf16[4,128,1664]{2,1,0:T(8,128)(2,1)S(1)}, u32[]{:S(2)}, u32[]{:S(2)}) collective-permute-start(bf16[4,128,1664]{2,1,0:T(8,128)(2,1)} %pad_maximum_fusion.3.refs_0_), channel_id=1, source_target_pairs={{0,64},{8,72},{16,80},{24,88},{32,96},{40,104},{48,112},{56,120},{... | collective-permute-start | bytes 5111816 | tf_op jit(solution)/shard_map/ppermute | solution.py:68
  216.0 35.5 %collective-permute-start.20 = (bf16[4,128,1664]{2,1,0:T(8,128)(2,1)}, bf16[4,128,1664]{2,1,0:T(8,128)(2,1)}, u32[]{:S(2)}, u32[]{:S(2)}) collective-permute-start(bf16[4,128,1664]{2,1,0:T(8,128)(2,1)} %get-tuple-element.133), channel_id=1, source_target_pairs={{0,96},{8,104},{16,112},{24,120},{32,0},{40,8},{48,16},{56,24},{64... | collective-permute-start | bytes 5111816 | tf_op jit(solution)/shard_map/ppermute | solution.py:68
  216.9 34.5 %collective-permute-start.21 = (bf16[4,128,1664]{2,1,0:T(8,128)(2,1)}, bf16[4,128,1664]{2,1,0:T(8,128)(2,1)}, u32[]{:S(2)}, u32[]{:S(2)}) collective-permute-start(bf16[4,128,1664]{2,1,0:T(8,128)(2,1)} %get-tuple-element.134), channel_id=1, source_target_pairs={{0,32},{8,40},{16,48},{24,56},{32,64},{40,72},{48,80},{56,88},{64,... | collective-permute-start | bytes 5111816 | tf_op jit(solution)/shard_map/ppermute | solution.py:68
  232.3 23.3 %collective-permute-start.23 = (bf16[4,128,1664]{2,1,0:T(8,128)(2,1)}, bf16[4,128,1664]{2,1,0:T(8,128)(2,1)S(1)}, u32[]{:S(2)}, u32[]{:S(2)}) collective-permute-start(bf16[4,128,1664]{2,1,0:T(8,128)(2,1)} %get-tuple-element.143), channel_id=1, source_target_pairs={{0,64},{8,72},{16,80},{24,88},{32,96},{40,104},{48,112},{56,120},{... | collective-permute-start | bytes 5111816 | tf_op jit(solution)/shard_map/ppermute | solution.py:68
  258.6 22.3 %collective-permute-start.27 = (bf16[6,768,512]{2,1,0:T(8,128)(2,1)}, bf16[6,768,512]{2,1,0:T(8,128)(2,1)S(1)}, u32[]{:S(2)}, u32[]{:S(2)}) collective-permute-start(bf16[6,768,512]{2,1,0:T(8,128)(2,1)} %get-tuple-element.170), channel_id=1, source_target_pairs={{0,128},{128,0},{1,129},{129,1},{2,130},{130,2},{3,131},{131,3},{4... | collective-permute-start | bytes 14155784 | tf_op jit(solution)/shard_map/ppermute | solution.py:155
  290.0 155.7 %reduce-scatter.2.cloned.1.call-start = ((), (), s32[]{:S(2)}) async-start(), calls=%async_computation.8 | async-start | bytes 5308416 | tf_op jit(solution)/shard_map/reduce_scatter | solution.py:618
  295.1 23.5 %all-to-all-start.1 = ((bf16[8,192,128]{2,1,0:T(8,128)(2,1)}), bf16[8,192,128]{2,1,0:T(8,128)(2,1)}, u32[]{:S(2)}, u32[]{:S(2)}) async-start(bf16[8,192,128]{2,1,0:T(8,128)(2,1)} %bitcast.159), calls=%async_computation.1 | async-start | bytes 786432 | tf_op jit(solution)/shard_map/all_to_all | solution.py:637
  299.3 56.5 %collective-permute-start.28 = (bf16[4,128,1536]{2,1,0:T(8,128)(2,1)}, bf16[4,128,1536]{2,1,0:T(8,128)(2,1)}, u32[]{:S(2)}, u32[]{:S(2)}) collective-permute-start(bf16[4,128,1536]{2,1,0:T(8,128)(2,1)} %get-tuple-element.180), channel_id=1, source_target_pairs={{0,96},{8,104},{16,112},{24,120},{32,0},{40,8},{48,16},{56,24},{64... | collective-permute-start | bytes 4718600 | tf_op jit(solution)/shard_map/ppermute | solution.py:68
  300.0 55.8 %collective-permute-start.29 = (bf16[4,128,1536]{2,1,0:T(8,128)(2,1)}, bf16[4,128,1536]{2,1,0:T(8,128)(2,1)}, u32[]{:S(2)}, u32[]{:S(2)}) collective-permute-start(bf16[4,128,1536]{2,1,0:T(8,128)(2,1)} %get-tuple-element.181), channel_id=1, source_target_pairs={{0,32},{8,40},{16,48},{24,56},{32,64},{40,72},{48,80},{56,88},{64,... | collective-permute-start | bytes 4718600 | tf_op jit(solution)/shard_map/ppermute | solution.py:68
  301.0 54.8 %collective-permute-start.30 = (bf16[4,128,1536]{2,1,0:T(8,128)(2,1)}, bf16[4,128,1536]{2,1,0:T(8,128)(2,1)}, u32[]{:S(2)}, u32[]{:S(2)}) collective-permute-start(bf16[4,128,1536]{2,1,0:T(8,128)(2,1)} %get-tuple-element.182), channel_id=1, source_target_pairs={{0,64},{8,72},{16,80},{24,88},{32,96},{40,104},{48,112},{56,120},{... | collective-permute-start | bytes 4718600 | tf_op jit(solution)/shard_map/ppermute | solution.py:68
  353.1 20.5 %collective-permute-start.35 = (bf16[128,1536]{1,0:T(8,128)(2,1)}, bf16[128,1536]{1,0:T(8,128)(2,1)}, u32[]{:S(2)}, u32[]{:S(2)}) collective-permute-start(bf16[128,1536]{1,0:T(8,128)(2,1)} %get-tuple-element.260), channel_id=1, source_target_pairs={{0,1},{1,2},{2,3},{3,4},{4,5},{5,6},{6,7},{7,0},{8,9},{9,10},{10,1... | collective-permute-start | bytes 1179656 | tf_op jit(solution)/shard_map/ppermute | solution.py:124
  353.1 20.5 %collective-permute-start.37 = (bf16[128,1536]{1,0:T(8,128)(2,1)}, bf16[128,1536]{1,0:T(8,128)(2,1)}, u32[]{:S(2)}, u32[]{:S(2)}) collective-permute-start(bf16[128,1536]{1,0:T(8,128)(2,1)} %get-tuple-element.259), channel_id=1, source_target_pairs={{0,7},{1,0},{2,1},{3,2},{4,3},{5,4},{6,5},{7,6},{8,15},{9,8},{10,9... | collective-permute-start | bytes 1179656 | tf_op jit(solution)/shard_map/ppermute | solution.py:124
  365.3 35.1 %all-to-all-start.2 = ((bf16[32,52,512]{2,1,0:T(8,128)(2,1)}), bf16[32,52,512]{2,1,0:T(8,128)(2,1)S(1)}, u32[]{:S(2)}, u32[]{:S(2)}) async-start(bf16[32,52,512]{2,1,0:T(8,128)(2,1)} %pad_maximum_fusion.1), calls=%async_computation.2 | async-start | bytes 3670016 | tf_op jit(solution)/shard_map/all_to_all | solution.py:662
  375.1 20.2 %collective-permute-start.38 = (bf16[128,1536]{1,0:T(8,128)(2,1)S(1)}, bf16[128,1536]{1,0:T(8,128)(2,1)S(1)}, u32[]{:S(2)}, u32[]{:S(2)}) collective-permute-start(bf16[128,1536]{1,0:T(8,128)(2,1)S(1)} %get-tuple-element.258), channel_id=1, source_target_pairs={{0,1},{1,2},{2,3},{3,4},{4,5},{5,6},{6,7},{7,0},{8,9},{9,10},{10,1... | collective-permute-start | bytes 1179656 | tf_op jit(solution)/shard_map/ppermute | solution.py:124
  375.2 20.1 %collective-permute-start.39 = (bf16[128,1536]{1,0:T(8,128)(2,1)S(1)}, bf16[128,1536]{1,0:T(8,128)(2,1)S(1)}, u32[]{:S(2)}, u32[]{:S(2)}) collective-permute-start(bf16[128,1536]{1,0:T(8,128)(2,1)S(1)} %get-tuple-element.257), channel_id=1, source_target_pairs={{0,7},{1,0},{2,1},{3,2},{4,3},{5,4},{6,5},{7,6},{8,15},{9,8},{10,9... | collective-permute-start | bytes 1179656 | tf_op jit(solution)/shard_map/ppermute | solution.py:124
  397.5 20.0 %collective-permute-start.40 = (bf16[128,1536]{1,0:T(8,128)(2,1)}, bf16[128,1536]{1,0:T(8,128)(2,1)S(1)}, u32[]{:S(2)}, u32[]{:S(2)}) collective-permute-start(bf16[128,1536]{1,0:T(8,128)(2,1)} %get-tuple-element.256), channel_id=1, source_target_pairs={{0,1},{1,2},{2,3},{3,4},{4,5},{5,6},{6,7},{7,0},{8,9},{9,10},{10,1... | collective-permute-start | bytes 1179656 | tf_op jit(solution)/shard_map/ppermute | solution.py:124
  397.5 20.0 %collective-permute-start.41 = (bf16[128,1536]{1,0:T(8,128)(2,1)}, bf16[128,1536]{1,0:T(8,128)(2,1)}, u32[]{:S(2)}, u32[]{:S(2)}) collective-permute-start(bf16[128,1536]{1,0:T(8,128)(2,1)} %get-tuple-element.255), channel_id=1, source_target_pairs={{0,7},{1,0},{2,1},{3,2},{4,3},{5,4},{6,5},{7,6},{8,15},{9,8},{10,9... | collective-permute-start | bytes 1179656 | tf_op jit(solution)/shard_map/ppermute | solution.py:124
  402.1 43.7 %all-to-all-start.3 = ((bf16[32,52,512]{2,1,0:T(8,128)(2,1)}), bf16[32,52,512]{2,1,0:T(8,128)(2,1)S(1)}, u32[]{:S(2)}, u32[]{:S(2)}) async-start(bf16[32,52,512]{2,1,0:T(8,128)(2,1)} %broadcast_in_dim.88), calls=%async_computation.3 | async-start | bytes 3670016 | tf_op jit(solution)/shard_map/all_to_all | solution.py:664
  419.0 20.3 %collective-permute-start.31 = (bf16[128,1536]{1,0:T(8,128)(2,1)}, bf16[128,1536]{1,0:T(8,128)(2,1)S(1)}, u32[]{:S(2)}, u32[]{:S(2)}) collective-permute-start(bf16[128,1536]{1,0:T(8,128)(2,1)} %get-tuple-element.184), channel_id=1, source_target_pairs={{0,24},{8,0},{16,8},{24,16},{32,56},{40,32},{48,40},{56,48},{64,88... | collective-permute-start | bytes 1179656 | tf_op jit(solution)/shard_map/ppermute | solution.py:68
  423.1 21.7 %collective-permute-start.33 = (bf16[128,1536]{1,0:T(8,128)(2,1)}, bf16[128,1536]{1,0:T(8,128)(2,1)S(1)}, u32[]{:S(2)}, u32[]{:S(2)}) collective-permute-start(bf16[128,1536]{1,0:T(8,128)(2,1)} %get-tuple-element.186), channel_id=1, source_target_pairs={{0,16},{8,24},{16,0},{24,8},{32,48},{40,56},{48,32},{56,40},{64,80... | collective-permute-start | bytes 1179656 | tf_op jit(solution)/shard_map/ppermute | solution.py:68
  (71 other events, 796.9 us)
Sparse Core Ops, SparseCore 0:
  16.7 61.1 all-gather.3
  80.3 68.4 all-gather.5
  290.1 47.8 all-gather.7
  340.5 84.4 reduce-scatter.1

commit v5 on v4

--- a/solution.py
+++ b/solution.py
@@ -2,6 +2,7 @@
 
 import jax
 import jax.numpy as jnp
+import numpy as np
 from jax import lax
 from jax.experimental import pallas as pl
 from jax.experimental.layout import Layout, with_layout_constraint
@@ -88,53 +89,10 @@
     ]
 
 
-def scatter_second(line):
-    arrived = [line[0]] + [cross(part, 0, -step) for part, step in zip(line[1:], STEPS[1:])]
-    return by_rows(sum(part.astype(f32) for part in arrived))
-
-
-def ring_gather(block):
-    size = lax.axis_size("tensor")
-    me = lax.axis_index("tensor")
-    half = block.shape[0] // 2
-    held = jnp.zeros((size,) + block.shape, block.dtype)
-
-    def shift(values, step):
-        return lax.ppermute(values, "tensor", [(i, (i + step) % size) for i in range(size)])
-
-    def put(held, values, place, row):
-        return lax.dynamic_update_slice(held, values[None], ((me + place) % size, row, 0))
-
-    held = put(held, block, 0, 0)
-    up = down = block
-    for step in range(1, size // 2):
-        up, down = shift(up, 1), shift(down, -1)
-        held = put(held, up, size - step, 0)
-        held = put(held, down, step, 0)
-    held = put(held, shift(up[:half], 1), size // 2, 0)
-    return put(held, shift(down[half:], -1), size // 2, half)
-
-
-def ring_scatter(parts):
-    size = lax.axis_size("tensor")
-    me = lax.axis_index("tensor")
-    half = parts.shape[1] // 2
-
-    def shift(values, step):
-        return lax.ppermute(values, "tensor", [(i, (i + step) % size) for i in range(size)])
-
-    def part_for(place):
-        return lax.dynamic_index_in_dim(parts, (me + place) % size, 0, keepdims=False)
-
-    far = part_for(size // 2)
-    up, down = shift(far[:half], 1), shift(far[half:], -1)
-    up = jnp.pad(up, ((0, half), (0, 0)))
-    down = jnp.pad(down, ((half, 0), (0, 0)))
-    for place in range(size // 2 - 1, 0, -1):
-        up = (part_for(place).astype(f32) + up.astype(f32)).astype(bf16)
-        down = (part_for(-place).astype(f32) + down.astype(f32)).astype(bf16)
-        up, down = together(shift(by_rows(up), 1), shift(by_rows(down), -1))
-    return part_for(0).astype(f32) + up.astype(f32) + down.astype(f32)
+def scatter_second(line, *beside):
+    arrived = [cross(part, 0, -step) for part, step in zip(line[1:], STEPS[1:])]
+    arrived[0], *beside = together(arrived[0], *beside)
+    return by_rows(sum(part.astype(f32) for part in (line[0], *arrived))), *beside
 
 
 def ring_sum(values):
@@ -185,7 +143,7 @@
 def attention_kernel(
     x_ref, w_ref, col_ref, row_ref, cos_ref, low_ref, high_ref, out_ref, turned_ref, qkv_ref
 ):
-    seq_len = x_ref.shape[0]
+    seq_len = out_ref.shape[0]
     tokens = turned_ref.shape[2]
     heads = out_ref.shape[1] // HEAD_DIM
     last = (heads + 1) * HEAD_DIM
@@ -193,7 +151,9 @@
     for first in range(0, seq_len, step):
         at = slice(first, first + step)
         wide = first + step
-        joined = jnp.dot(x_ref[at, :], w_ref[...], preferred_element_type=f32)
+        blocks = range(first // tokens, wide // tokens)
+        rows = jnp.concatenate([x_ref[block, :tokens, :] for block in blocks], axis=0)
+        joined = jnp.dot(rows, w_ref[...], preferred_element_type=f32)
         turned_part = turn(joined[:, :last], cos_ref[at, :], low_ref[at, :], high_ref[at, :])
         qkv_ref[at, :last] = turned_part.astype(bf16)
         qkv_ref[at, last:] = joined[:, last:].astype(bf16)
@@ -213,7 +173,7 @@
 
 
 def attention_back_kernel(
-    qkv_ref, grad_ref, col_ref, row_ref, cos_ref, low_ref, high_ref, out_ref, key_sum, value_sum
+    qkv_ref, grad_ref, col_ref, row_ref, cos_ref, low_ref, high_ref, out_ref, turned_ref, key_sum, value_sum
 ):
     seq_len = qkv_ref.shape[0]
     heads = grad_ref.shape[1] // HEAD_DIM
@@ -254,10 +214,16 @@
         both = turn(both, cos_ref[at, :], -low_ref[at, :], -high_ref[at, :])
         out_ref[at, :last] = both.astype(bf16)
         out_ref[at, last:] = value_sum[at, :].astype(bf16)
-
-
-def run_attention(normed_all, joined_weights, marks, tables, planes):
-    seq_len = normed_all.shape[0]
+        for block in range(step // tokens):
+            part = slice(block * tokens, (block + 1) * tokens)
+            to = first // tokens + block
+            turned_ref[to, :last, :] = both[part].T.astype(bf16)
+            turned_ref[to, last:, :] = value_sum[first : first + step, :][part].T.astype(bf16)
+
+
+def run_attention(gathered, joined_weights, marks, tables):
+    planes = gathered.shape[0]
+    seq_len = marks[0].shape[0]
     joined_width = joined_weights.shape[1]
     query_width = joined_width - 2 * HEAD_DIM
     vmem = pl.BlockSpec(memory_space=pltpu.VMEM)
@@ -274,17 +240,21 @@
         cost_estimate=pl.CostEstimate(
             flops=4 << 30, bytes_accessed=8 << 20, transcendentals=0
         ),
-    )(normed_all, joined_weights, *marks, *tables)
+    )(gathered, joined_weights, *marks, *tables)
 
 
 def run_attention_back(qkv, context_grad, marks, tables):
     seq_len, joined_width = qkv.shape
+    planes = context_grad.shape[0]
     vmem = pl.BlockSpec(memory_space=pltpu.VMEM)
     return pl.pallas_call(
         attention_back_kernel,
-        out_shape=jax.ShapeDtypeStruct((seq_len, joined_width), bf16),
+        out_shape=(
+            jax.ShapeDtypeStruct((seq_len, joined_width), bf16),
+            jax.ShapeDtypeStruct((planes, joined_width, seq_len // planes), bf16),
+        ),
         in_specs=[vmem] * 7,
-        out_specs=vmem,
+        out_specs=(vmem, vmem),
         scratch_shapes=[pltpu.VMEM((seq_len, HEAD_DIM), f32)] * 2,
         compiler_params=pltpu.CompilerParams(vmem_limit_bytes=48 * 1024 * 1024),
         cost_estimate=pl.CostEstimate(
@@ -294,15 +264,14 @@
 
 
 def rope_tables(seq_len, repeats):
-    frequency = rope_theta ** (-2.0 * jnp.arange(HALF, dtype=f32) / HEAD_DIM)
-    angles = jnp.arange(seq_len, dtype=f32)[:, None] * frequency[None, :]
-    sine = jnp.sin(angles)
-    nothing = jnp.zeros_like(sine)
+    frequency = np.float32(rope_theta) ** (np.arange(HALF, dtype=np.float32) * np.float32(-2.0 / HEAD_DIM))
+    angles = np.arange(seq_len, dtype=np.float32)[:, None] * frequency.astype(np.float32)[None, :]
+    cosine, sine = np.cos(angles), np.sin(angles)
+    nothing = np.zeros_like(sine)
 
     def heads(first, second):
-        return jnp.tile(jnp.concatenate([first, second], axis=1), (1, repeats))
-
-    cosine = jnp.cos(angles)
+        return jnp.asarray(np.tile(np.concatenate([first, second], axis=1), (1, repeats)))
+
     return heads(cosine, cosine), heads(-sine, nothing), heads(nothing, sine)
 
 
@@ -312,15 +281,10 @@
 
 
 def expert_kernel(groups, first_ref, *refs):
-    rows_refs, cots_refs, (w_ref,), back_outs, mix_outs, rest = (
-        refs[:groups],
-        refs[groups : 2 * groups],
-        refs[2 * groups : 2 * groups + 1],
-        refs[2 * groups + 1 : 3 * groups + 1],
-        refs[3 * groups + 1 : 4 * groups + 1],
-        refs[4 * groups + 1 :],
-    )
-    x_ref, c_ref, gate_ref, up_ref, hid_ref, pick_ref, down_ref = rest
+    rows_refs, cots_refs = refs[:groups], refs[groups : 2 * groups]
+    w_ref = refs[2 * groups]
+    back_outs = refs[2 * groups + 1 : 3 * groups + 1]
+    x_ref, c_ref, gate_ref, up_ref, hid_ref, pick_ref, down_ref = refs[3 * groups + 1 :]
     sources, tokens, _ = rows_refs[0].shape
     width = x_ref.shape[2]
     inner = w_ref.shape[2]
@@ -345,16 +309,7 @@
         c_ref[0, order * CAP : (order + 1) * CAP] = cots.astype(bf16)
     gate = jnp.concatenate(gates, axis=0)
 
-    down_rows = inner // HOLDERS
-    chunks = width // inner
-    for holder in range(HOLDERS):
-        for chunk in range(chunks):
-            start = (holder * chunks + chunk) * down_rows
-            down_ref[
-                holder * down_rows : (holder + 1) * down_rows,
-                chunk * inner : (chunk + 1) * inner,
-            ] = w_ref[2, start : start + down_rows, :]
-
+    join_chunks(down_ref, w_ref.at[2], HOLDERS)
     x = x_ref[0]
     gate_pre = jnp.dot(x, w_ref[0], preferred_element_type=f32)
     up_pre = jnp.dot(x, w_ref[1], preferred_element_type=f32)
@@ -378,17 +333,25 @@
         place = slice(order * CAP, (order + 1) * CAP)
         back_outs[group][source, at, :width] = row_grad[place].astype(bf16)
         back_outs[group][source, at, width:] = tail[place].astype(bf16)
-    mixed = gate * jnp.dot(hidden, down_ref[...], preferred_element_type=f32)
-    for order, (group, source) in enumerate(every):
-        place = slice(order * CAP, (order + 1) * CAP)
-        mix_outs[group][source, at] = mixed[place].astype(bf16)
 
     @pl.when(e == 1)
     def _():
         for order, (group, source) in enumerate(every):
-            pick = pick_ref[order]
-            back_outs[group][source] = contract(pick, back_outs[group][source], 0, 0).astype(bf16)
-            mix_outs[group][source] = contract(pick, mix_outs[group][source], 0, 0).astype(bf16)
+            back_outs[group][source] = contract(
+                pick_ref[order], back_outs[group][source], 0, 0
+            ).astype(bf16)
+
+
+def join_chunks(to_ref, from_ref, holders):
+    inner = from_ref.shape[1]
+    rows = inner // HOLDERS
+    chunks = to_ref.shape[1] // inner
+    for holder in range(holders):
+        for chunk in range(chunks):
+            start = (holder * chunks + chunk) * rows
+            to_ref[
+                holder * rows : (holder + 1) * rows, chunk * inner : (chunk + 1) * inner
+            ] = from_ref[start : start + rows, :]
 
 
 def run_experts(first, rows, cots, weights):
@@ -413,35 +376,83 @@
         grid=(2,),
         out_shape=(
             *[jax.ShapeDtypeStruct((sources, tokens, padded), bf16)] * groups,
-            *[jax.ShapeDtypeStruct((sources, tokens, width), bf16)] * groups,
             wide,
             wide,
             acts,
             acts,
             acts,
+            jax.ShapeDtypeStruct((groups * sources, 2 * CAP, tokens), bf16),
         ),
         in_specs=[pl.BlockSpec(memory_space=pltpu.SMEM)]
         + [once(padded)] * (2 * groups)
         + [by_expert(3, width, inner)],
         out_specs=(
             *[once(padded)] * groups,
-            *[once(width)] * groups,
             by_expert(1, slots, width),
             by_expert(1, slots, width),
             by_expert(1, slots, inner),
             by_expert(1, slots, inner),
             by_expert(1, slots, inner),
-        ),
-        scratch_shapes=[
-            pltpu.VMEM((groups * sources, 2 * CAP, tokens), bf16),
-            pltpu.VMEM((inner, width), bf16),
-        ],
+            pl.BlockSpec((groups * sources, 2 * CAP, tokens), lambda e: (0, 0, 0)),
+        ),
+        scratch_shapes=[pltpu.VMEM((inner, width), bf16)],
         compiler_params=pltpu.CompilerParams(vmem_limit_bytes=56 * 1024 * 1024),
         cost_estimate=pl.CostEstimate(
-            flops=2 * 2 * 7 * slots * width * inner, bytes_accessed=24 << 20, transcendentals=0
+            flops=2 * 2 * 6 * slots * width * inner, bytes_accessed=24 << 20, transcendentals=0
         ),
     )(first, *rows, *cots, weights)
-    return outs[:groups], outs[groups : 2 * groups], outs[2 * groups :]
+    return outs[:groups], outs[groups:-1], outs[-1]
+
+
+def mixture_kernel(groups, *refs):
+    pick_refs, hid_refs = refs[:groups], refs[groups : 2 * groups]
+    w_ref = refs[2 * groups]
+    outs, down_ref = refs[2 * groups + 1 : -1], refs[-1]
+    e = pl.program_id(0)
+    at = pl.ds(pl.multiple_of(e * CAP, CAP), CAP)
+    join_chunks(down_ref, w_ref.at[0], HOLDERS)
+    sources = [
+        (pick_ref, hid_ref, source)
+        for pick_ref, hid_ref in zip(pick_refs, hid_refs)
+        for source in range(pick_ref.shape[0])
+    ]
+    to = {}
+    for order, (pick_ref, hid_ref, source) in enumerate(sources):
+        to[order] = (outs[order // SIDE], order % SIDE, pick_ref, source)
+    order = 0
+    for pick_ref, hid_ref in zip(pick_refs, hid_refs):
+        mixed = jnp.dot(hid_ref[0], down_ref[...], preferred_element_type=f32).astype(bf16)
+        for source in range(pick_ref.shape[0]):
+            out, place, _, _ = to[order]
+            out[place, at] = mixed[source * CAP : (source + 1) * CAP]
+            order += 1
+
+    @pl.when(e == 1)
+    def _():
+        for out, place, pick_ref, source in to.values():
+            out[place] = contract(pick_ref[source], out[place], 0, 0).astype(bf16)
+
+
+def run_mixture(picks, hidden, weights):
+    width, inner = weights.shape[1:]
+    groups = len(picks)
+
+    def once(shape):
+        return pl.BlockSpec(shape, lambda e: (0, 0, 0), pipeline_mode=pl.Buffered(1))
+
+    shapes = [(SIDE, picks[0].shape[2], width)] * SIDE
+    return pl.pallas_call(
+        functools.partial(mixture_kernel, groups),
+        grid=(2,),
+        out_shape=[jax.ShapeDtypeStruct(shape, bf16) for shape in shapes],
+        in_specs=[once(pick.shape) for pick in picks]
+        + [pl.BlockSpec((1,) + hid.shape[1:], lambda e: (e, 0, 0)) for hid in hidden]
+        + [pl.BlockSpec((1, width, inner), lambda e: (3 * e + 2, 0, 0))],
+        out_specs=[once(shape) for shape in shapes],
+        scratch_shapes=[pltpu.VMEM((inner, width), bf16)],
+        compiler_params=pltpu.CompilerParams(vmem_limit_bytes=40 * 1024 * 1024),
+        cost_estimate=pl.CostEstimate(flops=1 << 32, bytes_accessed=1 << 20, transcendentals=0),
+    )(*picks, *hidden, weights)
 
 
 def weight_grad_kernel(half_ref, *refs):
@@ -533,9 +544,20 @@
     inverse_one = rms_inverse(token_f32)
     normed_low = (token_f32 * inverse_one * norm1_gain).astype(bf16)
     joined_weights = jnp.concatenate([w_query, w_key, w_value], axis=1)
-    normed_low = by_rows(normed_low)
-    normed_all = lax.all_gather(normed_low, "tensor", axis=0, tiled=True)
     core = lax.axis_index("dp")
+
+    def half_of(rows):
+        count = rows.shape[0] // 2
+        return lax.dynamic_slice_in_dim(rows, core * count, count, 0)
+
+    def both_halves(half):
+        other = swap_cores(half)
+        first, second = jnp.where(core == 0, half, other), jnp.where(core == 0, other, half)
+        return jnp.concatenate([first, second], axis=1).reshape(-1, half.shape[2])
+
+    gathered = lax.all_gather(
+        by_rows(jnp.concatenate([normed_low, half_of(w_out)], axis=0)), "tensor", axis=0
+    )
 
     expert_ids = jnp.arange(experts, dtype=jnp.int32)
     onehot = (routes[:, :, None] == expert_ids[None, None, :]).astype(f32)
@@ -546,8 +568,6 @@
     extra = jnp.pad(rank, ((0, tok_rows - experts), (0, LANES - tok_rows)))
     cot_payload = jnp.concatenate([cotangent, extra], axis=1)
 
-    count = w_out.shape[0] // 2
-    half_out = ring_gather(lax.dynamic_slice_in_dim(w_out, core * count, count, 0))
     chunks = width // hidden_width
     down_rows = w_down.shape[1]
     part_rows = w_gate.shape[1]
@@ -557,25 +577,17 @@
     weights = weights.reshape(3 * local_experts, part_rows, hidden_width)
     tables = rope_tables(seq_len, query_width // HEAD_DIM + 1)
     marks = segment_marks(key_seg)
-    normed_all, half_out, cot_line, weights, joined_weights, *constants = together(
-        normed_all, half_out, gather_first(cot_payload), weights, joined_weights, *tables, *marks
-    )
-    tables, marks = constants[:3], constants[3:]
+    cot_parts = gather_second(gather_first(cot_payload))
+    gathered, weights, joined_weights, col, row, *cot_parts = together(
+        gathered, weights, joined_weights, *marks, *cot_parts
+    )
+    marks = col, row
     weights_all = lax.all_gather(weights, ("dp", "tensor"), axis=1, tiled=True)
-    cot_parts = gather_second(cot_line)
-
-    context, context_blocks, qkv = run_attention(
-        normed_all, joined_weights, marks, tables, planes
-    )
-    context_blocks, cot_parts[1], cot_parts[2] = together(
-        context_blocks, cot_parts[1], cot_parts[2]
-    )
+    context, context_blocks, qkv = run_attention(gathered, joined_weights, marks, tables)
+    context_blocks, joined_half = together(context_blocks, half_of(by_rows(joined_weights.T)))
+    half_joined = lax.all_gather(joined_half, "tensor", axis=0)
     context_home = lax.all_to_all(context_blocks, "tensor", split_axis=0, concat_axis=0)
-    other_out = swap_cores(half_out)
-    w_out_all = jnp.concatenate(
-        [jnp.where(core == 0, half_out, other_out), jnp.where(core == 0, other_out, half_out)],
-        axis=1,
-    ).reshape(planes * query_width, width)
+    w_out_all = both_halves(gathered[:, tok_rows:])
     context_home, w_out_all = together(context_home, w_out_all)
     context_home = context_home.reshape(planes * query_width, tok_rows)
     mid = token_f32 + contract(context_home, w_out_all, 0, 0)
@@ -592,7 +604,6 @@
         [normed_two, gate_high, gate_low, jnp.zeros((tok_rows, LANES - 2 * experts), bf16)],
         axis=1,
     )
-    payload, *cot_parts = together(payload, *cot_parts)
     line = gather_first(payload)
     before, behind = (cross(line, 1, step) for step in STEPS[1:3])
 
@@ -601,23 +612,18 @@
         return run_experts(first_expert, rows, cots, weights_all)
 
     own = compute([line], cot_parts[:1])
-    line, before, behind, *own_saved = together(line, before, behind, *own[2])
+    line, before, behind, *own_saved = together(line, before, behind, *own[1])
     far = cross(line, 1, STEPS[3])
     near = compute([before, behind], cot_parts[1:3])
-    far, *near_saved = together(far, *near[2])
+    far, *near_saved = together(far, *near[1])
     last = compute([far], cot_parts[3:])
-    done = [(*own[:2], own_saved), (*near[:2], near_saved), last]
-    back_line = scatter_first([part for some in done for part in some[0]])
-    *both, given, kept = together(
-        *back_line,
-        *[part for some in done for part in some[1]],
-        *run_weight_grads(core.astype(jnp.int32).reshape(1), [some[2] for some in done]),
-    )
-    back_line, mix_parts = both[:SIDE], both[SIDE:]
+    done = [(*own[0], *near[0], *last[0]), (own_saved, near_saved, last[1])]
+    back_line = scatter_first(done[0])
+    *back_line, given, kept, half_joined = together(
+        *back_line, *run_weight_grads(core.astype(jnp.int32).reshape(1), done[1]), half_joined
+    )
     kept = (kept.astype(f32) + swap_cores(given).astype(f32)).astype(bf16)
-    weight_sum = lax.psum_scatter(kept, "tensor", scatter_dimension=1, tiled=True)
-    back_home = scatter_second(back_line)
-    back_home, kept = together(back_home, kept)
+    back_home, kept = scatter_second(back_line, kept)
 
     cot_f32 = cotangent.astype(f32)
     grad_tail = back_home[:, width:]
@@ -631,43 +637,63 @@
     mid_grad = cot_f32 + mid_part
     attention_low = by_rows(mid_grad.astype(bf16))
     context_grad = by_rows(contract(w_out_all, attention_low, 1, 1).astype(bf16))
-    context_grad, logit_grad, *mix_parts = together(context_grad, logit_grad, *mix_parts)
+    context_grad, logit_grad, kept, half_joined = together(
+        context_grad, logit_grad, kept, half_joined
+    )
+    weight_sum = lax.psum_scatter(kept, "tensor", scatter_dimension=1, tiled=True)
+    mix_parts = run_mixture(
+        [own[2], near[2], last[2]], [own_saved[4], near_saved[4], last[1][4]], weights_all
+    )
     mix_line = scatter_first(mix_parts)
-    router_part = contract(normed_two, logit_grad, 0, 0)
+    sharers = lax.axis_size("dp") * owners
+    columns = joined_width + query_width
+
+    def to_sharers(parts):
+        arrived = lax.all_to_all(parts, ("dp", "expert"), split_axis=0, concat_axis=0)
+        return jnp.sum(arrived.astype(f32), axis=0)
+
+    router_part = contract(logit_grad, normed_two, 0, 0)
+    shared = jnp.concatenate([router_part, norm2_part[None]]).astype(bf16)
+    shared_size = shared.size
+    extra = -(-shared_size // (columns * sharers))
+    shared = jnp.pad(shared.reshape(-1), (0, extra * columns * sharers - shared_size))
     context_grad = lax.all_to_all(
         context_grad.reshape(planes, query_width, tok_rows), "tensor", split_axis=0, concat_axis=0
     )
-    joined_grad = run_attention_back(qkv, context_grad, marks, tables)
-    normed_one_grad = ring_scatter(
-        contract(joined_grad, joined_weights, 1, 1).astype(bf16).reshape(planes, tok_rows, width)
-    )
+    context_grad, shared = together(context_grad, shared)
+    shared = to_sharers(shared.reshape(sharers, extra, columns))
+    joined_grad, joined_blocks = run_attention_back(qkv, context_grad, marks, tables)
+    joined_blocks, shared = together(joined_blocks, shared)
+    joined_home = lax.all_to_all(joined_blocks, "tensor", split_axis=0, concat_axis=0)
+    joined_all = both_halves(half_joined)
     attention_all = lax.all_gather(attention_low, "tensor", axis=0, tiled=True)
+    normed_all = gathered[:, :tok_rows].reshape(seq_len, width)
     joined_part = contract(normed_all, joined_grad, 0, 0)
     out_part = contract(attention_all, context, 0, 0)
     norm1_part = jnp.sum(joined_part * joined_weights.astype(f32), axis=1) / norm1_gain
-
-    sharers = lax.axis_size("dp") * owners
+    ringed = ring_sum(jnp.concatenate([shared, norm1_part.reshape(-1, columns)], axis=0))
+
+    block = width // sharers
     sides = jnp.concatenate([joined_part.astype(bf16), out_part.astype(bf16)], axis=1)
-    columns = sides.shape[1]
-    block = width // sharers
-    shared = jnp.concatenate([router_part.T, norm2_part[None], norm1_part[None]]).astype(bf16)
-    shared_size = shared.size
-    extra = -(-shared_size // (columns * sharers))
-    shared = jnp.pad(shared.reshape(-1), (0, extra * columns * sharers - shared_size))
-    blocks = jnp.concatenate(
-        [sides.reshape(sharers, block, columns), shared.reshape(sharers, extra, columns)], axis=1
-    )
-    blocks, *mix_line = together(blocks, *mix_line)
-    output = (mid + scatter_second(mix_line)).astype(bf16)
-    arrived = lax.all_to_all(blocks, ("dp", "expert"), split_axis=0, concat_axis=0)
-    total = jnp.sum(arrived.astype(f32), axis=0).astype(bf16)
+    sides, joined_home, *mix_line = together(sides, joined_home, *mix_line)
+    output = (mid + scatter_second(mix_line)[0]).astype(bf16)
+    total = to_sharers(sides.reshape(sharers, block, columns))
+    total = jnp.concatenate([total, ringed], axis=0).astype(bf16)
+    total = jnp.pad(total, ((0, -total.shape[0] % 8), (0, 0)))
     spread = lax.all_to_all(
-        jnp.broadcast_to(total[None], arrived.shape), ("dp", "expert"), split_axis=0, concat_axis=0
-    )
+        jnp.broadcast_to(total[None], (sharers,) + total.shape),
+        ("dp", "expert"),
+        split_axis=0,
+        concat_axis=0,
+    )
+    normed_one_grad = contract(joined_home.reshape(-1, tok_rows), joined_all, 0, 0)
     spread, weight_sum = together(spread, weight_sum)
     sides = spread[:, :block].reshape(width, columns).astype(f32)
-    shared = ring_sum(spread[:, block:].reshape(-1, LANES)).astype(f32).reshape(-1)
-    shared = shared[:shared_size].reshape(experts + 2, width)
+    shared = spread[:, block : block + extra].astype(f32).reshape(-1)
+    shared = shared[:shared_size].reshape(experts + 1, width)
+    norm1_rows = width // columns
+    norm1_sum = spread[:, block + extra : block + extra + norm1_rows].astype(f32)
+    norm1_sum = jnp.sum(norm1_sum, axis=0).reshape(width)
     joined_sum = sides[:, :joined_width]
     out_sum = sides[:, joined_width:].T
     weight_sum = weight_sum.reshape(local_experts, 3, part_rows, hidden_width)
@@ -681,7 +707,7 @@
     return (
         output,
         input_grad,
-        shared[experts + 1],
+        norm1_sum,
         joined_sum[:, :query_width],
         joined_sum[:, query_width : query_width + kv_width],
         joined_sum[:, query_width + kv_width :],

time: 495 us -> 453 us (0.915)
  the two profiles are of different devices: /device:TPU:9 before, /device:TPU:1 now
where the time goes in v5:
time: 453 us; the launch traced here: 447 us
  waiting for transfers between devices  155 us (34%)
  Pallas kernels  91 us (20%)
  starting transfers between devices  78.6 us (17%)
  local copies, waits for them, and re-layouts  46.2 us (10%)
  other arithmetic  42.6 us (9%)
  matrix products  18.3 us (4%)
  between operations  15.2 us (3%)
    ppermute x24, waiting for transfers between devices, cross(): return lax.ppermute(values, ('dp', 'expert'), pairs)  60.9 us
    pallas_call x3, Pallas kernels, run_experts(): pl.pallas_call(functools.partial(expert_kernel, groups), grid=(2,), out_s...  43.5 us
    ppermute x24, starting transfers between devices, cross(): return lax.ppermute(values, ('dp', 'expert'), pairs)  36.9 us
    unnamed x134, local copies, waits for them, and re-layouts  19.5 us
    all_to_all x1, waiting for transfers between devices, local(): lax.all_to_all(joined_blocks, 'tensor', split_axis=0, concat_axis=0)  18 us
    dot_general x6, matrix products, contract(): lax.dot_general(left, right, (((left_dim,), (right_dim,)), ((), ())), pre...  17.4 us
    all_to_all x1, waiting for transfers between devices, local(): lax.all_to_all(jnp.broadcast_to(total[None], (sharers,) + total.shape), (...  17.2 us
    pallas_call x1, Pallas kernels, run_weight_grads(): pl.pallas_call(weight_grad_kernel, grid=(2,), out_shape=(out, out), in_sp...  15.8 us
  transfers between devices with their start and end apart: 41, of which 21 were waited for; matrix products, arithmetic and copies ran while one was open for 16% of the time, Pallas kernels for 20%

profile of v5, /device:TPU:1, one launch (start us, length us, event | category | flops | bytes accessed | tf_op | source)
XLA Modules:
  0.0 446.7 jit_solution(1545598600123957428)
XLA Ops:
  17.2 4.3 collective-permute-done.2
  21.6 4.9 %collective-permute-done.1 = bf16[128,1664]{1,0:T(8,128)(2,1)S(1)} collective-permute-done((bf16[128,1664]{1,0:T(8,128)(2,1)S(1)}, bf16[128,1664]{1,0:T(8,128)(2,1)S(1)}, u32[]{:S(2)}, u32[]{:S(2)}) %collective-permute-start.1) | collective-permute-done | bytes 426016 | tf_op jit(solution)/shard_map/ppermute | solution.py:69
  35.9 13.3 %collective-permute-done.3.refs_2_ = bf16[4,128,1664]{2,1,0:T(8,128)(2,1)} collective-permute-done((bf16[4,128,1664]{2,1,0:T(8,128)(2,1)S(1)}, bf16[4,128,1664]{2,1,0:T(8,128)(2,1)}, u32[]{:S(2)}, u32[]{:S(2)}) %collective-permute-start.3) | collective-permute-done | bytes 1703968 | tf_op jit(solution)/shard_map/ppermute | solution.py:69
  49.2 17.5 %collective-permute-done.4.refs_3_ = bf16[4,128,1664]{2,1,0:T(8,128)(2,1)} collective-permute-done((bf16[4,128,1664]{2,1,0:T(8,128)(2,1)S(1)}, bf16[4,128,1664]{2,1,0:T(8,128)(2,1)}, u32[]{:S(2)}, u32[]{:S(2)}) %collective-permute-start.4) | collective-permute-done | bytes 1703968 | tf_op jit(solution)/shard_map/ppermute | solution.py:69
  68.6 13.5 %all-gather.11.cloned.1.call-done = bf16[1792,1536]{1,0:T(8,128)(2,1)} async-done(((bf16[224,1536]{1,0:T(8,128)(2,1)}), bf16[1792,1536]{1,0:T(8,128)(2,1)}) %all-gather.11.cloned.1.call-update) | async-done | bytes 5505040 | tf_op jit(solution)/shard_map/all_gather | solution.py:558
  91.7 9.8 %shard_map.256 = (bf16[1024,192]{1,0:T(8,128)(2,1)S(1)}, bf16[8,192,128]{2,1,0:T(8,128)(2,1)}, bf16[1024,320]{1,0:T(8,128)(2,1)S(1)}) custom-call(bf16[8,224,1536]{2,1,0:T(8,128)(2,1)} %bitcast.97, bf16[1536,320]{1,0:T(8,128)(2,1)} %copy.136.w_ref, s32[1024,1]{1,0:T(8,128)S(1)} %compare_select_fusion.col_ref, s32[1,1024]{1,0:T(1,128)S(1)} %compare_select_fusion.1.row_ref, ...), custom_call_target="tpu_custom_call" | custom-call | flops 4294967296 | bytes 8388608 | tf_op jit(solution)/shard_map/pallas_call | solution.py:230
  112.5 13.1 %all-to-all-done = bf16[8,192,128]{2,1,0:T(8,128)(2,1)S(1)} async-done(((bf16[8,192,128]{2,1,0:T(8,128)(2,1)}), bf16[8,192,128]{2,1,0:T(8,128)(2,1)S(1)}, u32[]{:S(2)}, u32[]{:S(2)}) %all-to-all-start) | async-done | bytes 393248 | tf_op jit(solution)/shard_map/all_to_all | solution.py:589
  134.2 4.6 %collective-permute-done.9 = bf16[128,1664]{1,0:T(8,128)(2,1)S(1)} collective-permute-done((bf16[128,1664]{1,0:T(8,128)(2,1)S(1)}, bf16[128,1664]{1,0:T(8,128)(2,1)S(1)}, u32[]{:S(2)}, u32[]{:S(2)}) %collective-permute-start.9) | collective-permute-done | bytes 426016 | tf_op jit(solution)/shard_map/ppermute | solution.py:69
  138.8 4.7 %collective-permute-done.8 = bf16[128,1664]{1,0:T(8,128)(2,1)S(1)} collective-permute-done((bf16[128,1664]{1,0:T(8,128)(2,1)S(1)}, bf16[128,1664]{1,0:T(8,128)(2,1)S(1)}, u32[]{:S(2)}, u32[]{:S(2)}) %collective-permute-start.8) | collective-permute-done | bytes 426016 | tf_op jit(solution)/shard_map/ppermute | solution.py:69
  146.8 6.1 %all-gather.7.cloned.1.call-done.refs_2_.refs_4_.refs_6_ = bf16[6,1536,512]{2,1,0:T(8,128)(2,1)} async-done(((bf16[6,96,512]{2,1,0:T(8,128)(2,1)}), bf16[6,1536,512]{2,1,0:T(8,128)(2,1)}) %all-gather.7.cloned.1.call-update) | async-done | bytes 9437200 | tf_op jit(solution)/shard_map/all_gather | solution.py:585
  152.9 11.8 %shard_map.257 = (bf16[4,128,1664]{2,1,0:T(8,128)(2,1)}, bf16[2,256,1536]{2,1,0:T(8,128)(2,1)}, bf16[2,256,1536]{2,1,0:T(8,128)(2,1)}, bf16[2,256,512]{2,1,0:T(8...) custom-call(s32[1]{0:T(128)} %bitcast.16.first_ref, ...), custom_call_target="tpu_custom_call" | custom-call | flops 4831838208 | bytes 25165824 | tf_op jit(solution)/shard_map/pallas_call | solution.py:374
  168.8 19.8 %shard_map.258 = (bf16[4,128,1664]{2,1,0:T(8,128)(2,1)}, bf16[4,128,1664]{2,1,0:T(8,128)(2,1)}, bf16[2,512,1536]{2,1,0:T(8,128)(2,1)}, bf16[2,512,1536]{2,1,0:T(...) custom-call(s32[1]{0:T(128)} %bitcast.16.first_ref, ...), custom_call_target="tpu_custom_call" | custom-call | flops 9663676416 | bytes 25165824 | tf_op jit(solution)/shard_map/pallas_call | solution.py:374
  193.0 11.9 %shard_map.259 = (bf16[4,128,1664]{2,1,0:T(8,128)(2,1)}, bf16[2,256,1536]{2,1,0:T(8,128)(2,1)}, bf16[2,256,1536]{2,1,0:T(8,128)(2,1)}, bf16[2,256,512]{2,1,0:T(8...) custom-call(s32[1]{0:T(128)} %bitcast.16.first_ref, ...), custom_call_target="tpu_custom_call" | custom-call | flops 4831838208 | bytes 25165824 | tf_op jit(solution)/shard_map/pallas_call | solution.py:374
  206.1 15.8 %shard_map.260 = (bf16[6,768,512]{2,1,0:T(8,128)(2,1)}, bf16[6,768,512]{2,1,0:T(8,128)(2,1)}) custom-call(s32[1]{0:T(128)} %bitcast.25.half_ref, bf16[2,256,1536]{2,1,0:T(8,128)(2,1)} %get-tuple-element.129.refs_0_, bf16[2,512,1536]{2,1,0:T(8,128)(2,1)} %get-tuple-element.130.refs_1_, bf16[2,256,1536]{2,1,0:T(8,128)(2,1)} %get-tuple-element.131.refs_2_, ...), custom_call_target="tpu_custom_call" | custom-call | flops 268435456 | bytes 1048576 | tf_op jit(solution)/shard_map/pallas_call | solution.py:499
  221.9 7.5 %collective-permute-done.13 = bf16[4,128,1664]{2,1,0:T(8,128)(2,1)S(1)} collective-permute-done((bf16[4,128,1664]{2,1,0:T(8,128)(2,1)}, bf16[4,128,1664]{2,1,0:T(8,128)(2,1)S(1)}, u32[]{:S(2)}, u32[]{:S(2)}) %collective-permute-start.13) | collective-permute-done | bytes 1703968 | tf_op jit(solution)/shard_map/ppermute | solution.py:69
  231.2 4.2 collective-permute-start.17
  243.1 6.0 %add_convert_fusion = bf16[6,768,512]{2,1,0:T(8,128)(2,1)} fusion(bf16[6,768,512]{2,1,0:T(8,128)(2,1)S(1)} %collective-permute-done.17, bf16[6,768,512]{2,1,0:T(8,128)(2,1)} %get-tuple-element.149), kind=kLoop, calls=%fused_computation | loop fusion | flops 9437184 | bytes 14155776 | tf_op jit(solution)/shard_map/convert_element_type | solution.py:625
  253.9 4.5 %convolution_convert_fusion.1 = bf16[1536,128]{1,0:T(8,128)(2,1)} fusion(bf16[1536,1536]{1,0:T(8,128)(2,1)} %bitcast.95, bf16[128,1536]{1,0:T(8,128)(2,1)} %get-tuple-element.256), kind=kOutput, calls=%fused_computation.12 | convolution fusion | flops 604176384 | bytes 5505024 | tf_op jit(solution)/shard_map/dot_general | solution.py:117
  266.1 9.0 %shard_map.262 = (bf16[4,128,1536]{2,1,0:T(8,128)(2,1)S(1)}, bf16[4,128,1536]{2,1,0:T(8,128)(2,1)}, bf16[4,128,1536]{2,1,0:T(8,128)(2,1)}, bf16[4,128,1536]{2,1,0:T(8,128)(2,1)}) custom-call(bf16[4,128,128]{2,1,0:T(8,128)(2,1)S(1)} %copy-done.22, bf16[8,128,128]{2,1,0:T(8,128)(2,1)S(1)} %copy-done.21, bf16[4,128,128]{2,1,0:T(8,128)(2,1)S(1)} %copy-done.23, ...), custom_call_target="tpu_custom_call" | custom-call | flops 4294967296 | bytes 1048576 | tf_op jit(solution)/shard_map/pallas_call | solution.py:444
  289.9 5.5 %all-to-all-start.2 = ((bf16[32,4,512]{2,1,0:T(4,128)(2,1)}), bf16[32,4,512]{2,1,0:T(4,128)(2,1)}, u32[]{:S(2)}, u32[]{:S(2)}) async-start(bf16[32,4,512]{2,1,0:T(4,128)(2,1)} %reshape.239), calls=%async_computation.2 | async-start | bytes 262144 | tf_op jit(solution)/shard_map/all_to_all | solution.py:652
  297.8 12.8 %shard_map.261 = (bf16[1024,320]{1,0:T(8,128)(2,1)S(1)}, bf16[8,320,128]{2,1,0:T(8,128)(2,1)}) custom-call(bf16[1024,320]{1,0:T(8,128)(2,1)S(1)} %copy-done.20, bf16[8,192,128]{2,1,0:T(8,128)(2,1)S(1)} %all-to-all-done.1.grad_ref, s32[1024,1]{1,0:T(8,128)S(1)} %copy-done.9, s32[1,1024]{1,0:T(1,128)S(1)} %compare_select_fusion.1.row_ref, ...), custom_call_target="tpu_custom_call" | custom-call | flops 8589934592 | bytes 4194304 | tf_op jit(solution)/shard_map/pallas_call | solution.py:250
  311.4 6.5 %all-to-all-done.2 = bf16[32,4,512]{2,1,0:T(4,128)(2,1)} async-done(((bf16[32,4,512]{2,1,0:T(4,128)(2,1)}), bf16[32,4,512]{2,1,0:T(4,128)(2,1)}, u32[]{:S(2)}, u32[]{:S(2)}) %all-to-all-start.2) | async-done | bytes 131104 | tf_op jit(solution)/shard_map/all_to_all | solution.py:652
  318.9 6.9 %all-to-all-start.3 = ((bf16[8,320,128]{2,1,0:T(8,128)(2,1)}), bf16[8,320,128]{2,1,0:T(8,128)(2,1)S(1)}, u32[]{:S(2)}, u32[]{:S(2)}) async-start(bf16[8,320,128]{2,1,0:T(8,128)(2,1)} %get-tuple-element.163), calls=%async_computation.3 | async-start | bytes 1310720 | tf_op jit(solution)/shard_map/all_to_all | solution.py:667
  325.9 4.2 fusion.28
  335.3 18.0 %all-to-all-done.3 = bf16[8,320,128]{2,1,0:T(8,128)(2,1)S(1)} async-done(((bf16[8,320,128]{2,1,0:T(8,128)(2,1)}), bf16[8,320,128]{2,1,0:T(8,128)(2,1)S(1)}, u32[]{:S(2)}, u32[]{:S(2)}) %all-to-all-start.3) | async-done | bytes 655392 | tf_op jit(solution)/shard_map/all_to_all | solution.py:667
  354.8 6.7 %all-to-all-start.4 = ((bf16[32,48,512]{2,1,0:T(8,128)(2,1)}), bf16[32,48,512]{2,1,0:T(8,128)(2,1)S(1)}, u32[]{:S(2)}, u32[]{:S(2)}) async-start(bf16[32,48,512]{2,1,0:T(8,128)(2,1)} %bitcast.33), calls=%async_computation.4 | async-start | bytes 3145728 | tf_op jit(solution)/shard_map/all_to_all | solution.py:652
  365.3 4.6 %collective-permute-done.28 = f32[7,512]{1,0:T(8,128)S(1)} collective-permute-done((f32[7,512]{1,0:T(8,128)S(1)}, f32[7,512]{1,0:T(8,128)S(1)}, u32[]{:S(2)}, u32[]{:S(2)}) %collective-permute-start.28) | collective-permute-done | bytes 14368 | tf_op jit(solution)/shard_map/ppermute | solution.py:103
  369.9 7.4 %collective-permute-done.29 = f32[7,512]{1,0:T(8,128)S(1)} collective-permute-done((f32[7,512]{1,0:T(8,128)S(1)}, f32[7,512]{1,0:T(8,128)S(1)}, u32[]{:S(2)}, u32[]{:S(2)}) %collective-permute-start.29) | collective-permute-done | bytes 14368 | tf_op jit(solution)/shard_map/ppermute | solution.py:103
  377.2 5.6 %broadcast_select_fusion.1 = (bf16[8,160,1536]{2,1,0:T(8,128)(2,1)}, bf16[8,160,1536]{2,1,0:T(8,128)(2,1)}) fusion(bf16[8,160,1536]{2,1,0:T(8,128)(2,1)} %bitcast.102, bf16[8,160,1536]{2,1,0:T(8,128)(2,1)} %collective-permute-done.26, pred[]{:T(512)S(6)} %eq.44), kind=kLoop, calls=%fused_computation.7 | loop fusion | flops 3932160 | bytes 15728641 | tf_op jit(solution)/shard_map/jit(_where)/select_n | solution.py:555
  389.7 8.8 %all-to-all-start.5 = ((bf16[32,56,512]{2,1,0:T(8,128)(2,1)}), bf16[32,56,512]{2,1,0:T(8,128)(2,1)S(1)}, u32[]{:S(2)}, u32[]{:S(2)}) async-start(bf16[32,56,512]{2,1,0:T(8,128)(2,1)} %broadcast_in_dim.17), calls=%async_computation.5 | async-start | bytes 3670016 | tf_op jit(solution)/shard_map/all_to_all | solution.py:683
  398.5 4.3 fusion.19
  406.3 17.2 %all-to-all-done.5 = bf16[32,56,512]{2,1,0:T(8,128)(2,1)S(1)} async-done(((bf16[32,56,512]{2,1,0:T(8,128)(2,1)}), bf16[32,56,512]{2,1,0:T(8,128)(2,1)S(1)}, u32[]{:S(2)}, u32[]{:S(2)}) %all-to-all-start.5) | async-done | bytes 1835040 | tf_op jit(solution)/shard_map/all_to_all | solution.py:683
  (278 shorter events, 140.7 us)
Async XLA Ops:
  7.2 75.0 %all-gather.11.cloned.1.call-start = ((), (), s32[]{:S(2)}) async-start(), calls=%async_computation.10 | async-start | bytes 6193152 | tf_op jit(solution)/shard_map/all_gather | solution.py:558
  11.1 141.8 %all-gather.7.cloned.1.call-start = ((), (), s32[]{:S(2)}) async-start(), calls=%async_computation.7 | async-start | bytes 10027008 | tf_op jit(solution)/shard_map/all_gather | solution.py:585
  26.8 22.4 %collective-permute-start.3 = (bf16[4,128,1664]{2,1,0:T(8,128)(2,1)S(1)}, bf16[4,128,1664]{2,1,0:T(8,128)(2,1)}, u32[]{:S(2)}, u32[]{:S(2)}) collective-permute-start(bf16[4,128,1664]{2,1,0:T(8,128)(2,1)S(1)} %pad_maximum_fusion.1.refs_1_), channel_id=1, source_target_pairs={{0,32},{8,40},{16,48},{24,56},{32,64},{40,72},{48,80},{56,88},{64,... | collective-permute-start | bytes 5111816 | tf_op jit(solution)/shard_map/ppermute | solution.py:69
  28.2 38.6 %collective-permute-start.4 = (bf16[4,128,1664]{2,1,0:T(8,128)(2,1)S(1)}, bf16[4,128,1664]{2,1,0:T(8,128)(2,1)}, u32[]{:S(2)}, u32[]{:S(2)}) collective-permute-start(bf16[4,128,1664]{2,1,0:T(8,128)(2,1)S(1)} %pad_maximum_fusion.1.refs_1_), channel_id=1, source_target_pairs={{0,96},{8,104},{16,112},{24,120},{32,0},{40,8},{48,16},{56,24},{64... | collective-permute-start | bytes 5111816 | tf_op jit(solution)/shard_map/ppermute | solution.py:69
  29.7 39.0 %collective-permute-start.5 = (bf16[4,128,1664]{2,1,0:T(8,128)(2,1)S(1)}, bf16[4,128,1664]{2,1,0:T(8,128)(2,1)}, u32[]{:S(2)}, u32[]{:S(2)}) collective-permute-start(bf16[4,128,1664]{2,1,0:T(8,128)(2,1)S(1)} %pad_maximum_fusion.1.refs_1_), channel_id=1, source_target_pairs={{0,64},{8,72},{16,80},{24,88},{32,96},{40,104},{48,112},{56,120},{... | collective-permute-start | bytes 5111816 | tf_op jit(solution)/shard_map/ppermute | solution.py:69
  85.4 21.8 %collective-permute-start.6 = (bf16[8,96,1536]{2,1,0:T(8,128)(2,1)}, bf16[8,96,1536]{2,1,0:T(8,128)(2,1)}, u32[]{:S(2)}, u32[]{:S(2)}) collective-permute-start(bf16[8,96,1536]{2,1,0:T(8,128)(2,1)} %slice.164), channel_id=1, source_target_pairs={{0,128},{128,0},{1,129},{129,1},{2,130},{130,2},{3,131},{131,3},{4... | collective-permute-start | bytes 7077896 | tf_op jit(solution)/shard_map/ppermute | solution.py:113
  102.4 23.2 %all-to-all-start = ((bf16[8,192,128]{2,1,0:T(8,128)(2,1)}), bf16[8,192,128]{2,1,0:T(8,128)(2,1)S(1)}, u32[]{:S(2)}, u32[]{:S(2)}) async-start(bf16[8,192,128]{2,1,0:T(8,128)(2,1)} %get-tuple-element.102), calls=%async_computation | async-start | bytes 786432 | tf_op jit(solution)/shard_map/all_to_all | solution.py:589
  106.5 124.7 %all-gather.13.cloned.1.call-start = ((), (), s32[]{:S(2)}) async-start(), calls=%async_computation.11 | async-start | bytes 4423680 | tf_op jit(solution)/shard_map/all_gather | solution.py:588
  107.2 225.1 %all-gather.9.cloned.1.call-start = ((), (), s32[]{:S(2)}) async-start(), calls=%async_computation.8 | async-start | bytes 3538944 | tf_op jit(solution)/shard_map/all_gather | solution.py:669
  132.8 10.8 %collective-permute-start.8 = (bf16[128,1664]{1,0:T(8,128)(2,1)S(1)}, bf16[128,1664]{1,0:T(8,128)(2,1)S(1)}, u32[]{:S(2)}, u32[]{:S(2)}) collective-permute-start(bf16[128,1664]{1,0:T(8,128)(2,1)S(1)} %concatenate.36), channel_id=1, source_target_pairs={{0,24},{8,0},{16,8},{24,16},{32,56},{40,32},{48,40},{56,48},{64,88... | collective-permute-start | bytes 1277960 | tf_op jit(solution)/shard_map/ppermute | solution.py:69
  143.8 22.4 %collective-permute-start.10 = (bf16[4,128,1664]{2,1,0:T(8,128)(2,1)S(1)}, bf16[4,128,1664]{2,1,0:T(8,128)(2,1)}, u32[]{:S(2)}, u32[]{:S(2)}) collective-permute-start(bf16[4,128,1664]{2,1,0:T(8,128)(2,1)S(1)} %pad_maximum_fusion.2.refs_0_), channel_id=1, source_target_pairs={{0,32},{8,40},{16,48},{24,56},{32,64},{40,72},{48,80},{56,88},{64,... | collective-permute-start | bytes 5111816 | tf_op jit(solution)/shard_map/ppermute | solution.py:69
  145.1 21.3 %collective-permute-start.11 = (bf16[4,128,1664]{2,1,0:T(8,128)(2,1)S(1)}, bf16[4,128,1664]{2,1,0:T(8,128)(2,1)}, u32[]{:S(2)}, u32[]{:S(2)}) collective-permute-start(bf16[4,128,1664]{2,1,0:T(8,128)(2,1)S(1)} %pad_maximum_fusion.2.refs_0_), channel_id=1, source_target_pairs={{0,96},{8,104},{16,112},{24,120},{32,0},{40,8},{48,16},{56,24},{64... | collective-permute-start | bytes 5111816 | tf_op jit(solution)/shard_map/ppermute | solution.py:69
  166.4 25.4 %collective-permute-start.14 = (bf16[4,128,1664]{2,1,0:T(8,128)(2,1)}, bf16[4,128,1664]{2,1,0:T(8,128)(2,1)S(1)}, u32[]{:S(2)}, u32[]{:S(2)}) collective-permute-start(bf16[4,128,1664]{2,1,0:T(8,128)(2,1)} %copy-done.37), channel_id=1, source_target_pairs={{0,64},{8,72},{16,80},{24,88},{32,96},{40,104},{48,112},{56,120},{... | collective-permute-start | bytes 5111816 | tf_op jit(solution)/shard_map/ppermute | solution.py:69
  188.7 40.7 %collective-permute-start.13 = (bf16[4,128,1664]{2,1,0:T(8,128)(2,1)}, bf16[4,128,1664]{2,1,0:T(8,128)(2,1)S(1)}, u32[]{:S(2)}, u32[]{:S(2)}) collective-permute-start(bf16[4,128,1664]{2,1,0:T(8,128)(2,1)} %get-tuple-element.119), channel_id=1, source_target_pairs={{0,32},{8,40},{16,48},{24,56},{32,64},{40,72},{48,80},{56,88},{64,... | collective-permute-start | bytes 5111816 | tf_op jit(solution)/shard_map/ppermute | solution.py:69
  189.5 39.8 %collective-permute-start.12 = (bf16[4,128,1664]{2,1,0:T(8,128)(2,1)}, bf16[4,128,1664]{2,1,0:T(8,128)(2,1)S(1)}, u32[]{:S(2)}, u32[]{:S(2)}) collective-permute-start(bf16[4,128,1664]{2,1,0:T(8,128)(2,1)} %get-tuple-element.118), channel_id=1, source_target_pairs={{0,96},{8,104},{16,112},{24,120},{32,0},{40,8},{48,16},{56,24},{64... | collective-permute-start | bytes 5111816 | tf_op jit(solution)/shard_map/ppermute | solution.py:69
  204.9 24.5 %collective-permute-start.15 = (bf16[4,128,1664]{2,1,0:T(8,128)(2,1)}, bf16[4,128,1664]{2,1,0:T(8,128)(2,1)S(1)}, u32[]{:S(2)}, u32[]{:S(2)}) collective-permute-start(bf16[4,128,1664]{2,1,0:T(8,128)(2,1)} %get-tuple-element.128), channel_id=1, source_target_pairs={{0,64},{8,72},{16,80},{24,88},{32,96},{40,104},{48,112},{56,120},{... | collective-permute-start | bytes 5111816 | tf_op jit(solution)/shard_map/ppermute | solution.py:69
  231.2 11.9 %collective-permute-start.17 = (bf16[6,768,512]{2,1,0:T(8,128)(2,1)}, bf16[6,768,512]{2,1,0:T(8,128)(2,1)S(1)}, u32[]{:S(2)}, u32[]{:S(2)}) collective-permute-start(bf16[6,768,512]{2,1,0:T(8,128)(2,1)} %get-tuple-element.150), channel_id=1, source_target_pairs={{0,128},{128,0},{1,129},{129,1},{2,130},{130,2},{3,131},{131,3},{4... | collective-permute-start | bytes 14155784 | tf_op jit(solution)/shard_map/ppermute | solution.py:113
  235.3 14.2 %collective-permute-start.19 = (bf16[128,1664]{1,0:T(8,128)(2,1)}, bf16[128,1664]{1,0:T(8,128)(2,1)S(1)}, u32[]{:S(2)}, u32[]{:S(2)}) collective-permute-start(bf16[128,1664]{1,0:T(8,128)(2,1)} %get-tuple-element.153), channel_id=1, source_target_pairs={{0,16},{8,24},{16,0},{24,8},{32,48},{40,56},{48,32},{56,40},{64,80... | collective-permute-start | bytes 1277960 | tf_op jit(solution)/shard_map/ppermute | solution.py:69
  236.4 13.8 %collective-permute-start.18 = (bf16[128,1664]{1,0:T(8,128)(2,1)}, bf16[128,1664]{1,0:T(8,128)(2,1)S(1)}, u32[]{:S(2)}, u32[]{:S(2)}) collective-permute-start(bf16[128,1664]{1,0:T(8,128)(2,1)} %get-tuple-element.152), channel_id=1, source_target_pairs={{0,8},{8,16},{16,24},{24,0},{32,40},{40,48},{48,56},{56,32},{64,72... | collective-permute-start | bytes 1277960 | tf_op jit(solution)/shard_map/ppermute | solution.py:69
  253.8 169.7 %reduce-scatter.2.cloned.1.call-start = ((), (), s32[]{:S(2)}) async-start(), calls=%async_computation.9 | async-start | bytes 5308416 | tf_op jit(solution)/shard_map/reduce_scatter | solution.py:643
  258.4 29.9 %all-to-all-start.1 = ((bf16[8,192,128]{2,1,0:T(8,128)(2,1)}), bf16[8,192,128]{2,1,0:T(8,128)(2,1)S(1)}, u32[]{:S(2)}, u32[]{:S(2)}) async-start(bf16[8,192,128]{2,1,0:T(8,128)(2,1)} %bitcast.27), calls=%async_computation.1 | async-start | bytes 786432 | tf_op jit(solution)/shard_map/all_to_all | solution.py:660
  262.0 115.2 %collective-permute-start.26 = (bf16[8,160,1536]{2,1,0:T(8,128)(2,1)}, bf16[8,160,1536]{2,1,0:T(8,128)(2,1)}, u32[]{:S(2)}, u32[]{:S(2)}) collective-permute-start(bf16[8,160,1536]{2,1,0:T(8,128)(2,1)} %bitcast.101), channel_id=1, source_target_pairs={{0,128},{128,0},{1,129},{129,1},{2,130},{130,2},{3,131},{131,3},{4... | collective-permute-start | bytes 11796488 | tf_op jit(solution)/shard_map/ppermute | solution.py:113
  275.2 50.7 %collective-permute-start.22 = (bf16[4,128,1536]{2,1,0:T(8,128)(2,1)}, bf16[4,128,1536]{2,1,0:T(8,128)(2,1)}, u32[]{:S(2)}, u32[]{:S(2)}) collective-permute-start(bf16[4,128,1536]{2,1,0:T(8,128)(2,1)} %get-tuple-element.170), channel_id=1, source_target_pairs={{0,64},{8,72},{16,80},{24,88},{32,96},{40,104},{48,112},{56,120},{... | collective-permute-start | bytes 4718600 | tf_op jit(solution)/shard_map/ppermute | solution.py:69
  277.6 48.3 %collective-permute-start.21 = (bf16[4,128,1536]{2,1,0:T(8,128)(2,1)}, bf16[4,128,1536]{2,1,0:T(8,128)(2,1)}, u32[]{:S(2)}, u32[]{:S(2)}) collective-permute-start(bf16[4,128,1536]{2,1,0:T(8,128)(2,1)} %get-tuple-element.169), channel_id=1, source_target_pairs={{0,32},{8,40},{16,48},{24,56},{32,64},{40,72},{48,80},{56,88},{64,... | collective-permute-start | bytes 4718600 | tf_op jit(solution)/shard_map/ppermute | solution.py:69
  278.1 47.7 %collective-permute-start.20 = (bf16[4,128,1536]{2,1,0:T(8,128)(2,1)}, bf16[4,128,1536]{2,1,0:T(8,128)(2,1)}, u32[]{:S(2)}, u32[]{:S(2)}) collective-permute-start(bf16[4,128,1536]{2,1,0:T(8,128)(2,1)} %get-tuple-element.168), channel_id=1, source_target_pairs={{0,96},{8,104},{16,112},{24,120},{32,0},{40,8},{48,16},{56,24},{64... | collective-permute-start | bytes 4718600 | tf_op jit(solution)/shard_map/ppermute | solution.py:69
  289.9 28.0 %all-to-all-start.2 = ((bf16[32,4,512]{2,1,0:T(4,128)(2,1)}), bf16[32,4,512]{2,1,0:T(4,128)(2,1)}, u32[]{:S(2)}, u32[]{:S(2)}) async-start(bf16[32,4,512]{2,1,0:T(4,128)(2,1)} %reshape.239), calls=%async_computation.2 | async-start | bytes 262144 | tf_op jit(solution)/shard_map/all_to_all | solution.py:652
  318.9 34.4 %all-to-all-start.3 = ((bf16[8,320,128]{2,1,0:T(8,128)(2,1)}), bf16[8,320,128]{2,1,0:T(8,128)(2,1)S(1)}, u32[]{:S(2)}, u32[]{:S(2)}) async-start(bf16[8,320,128]{2,1,0:T(8,128)(2,1)} %get-tuple-element.163), calls=%async_computation.3 | async-start | bytes 1310720 | tf_op jit(solution)/shard_map/all_to_all | solution.py:667
  354.8 33.2 %all-to-all-start.4 = ((bf16[32,48,512]{2,1,0:T(8,128)(2,1)}), bf16[32,48,512]{2,1,0:T(8,128)(2,1)S(1)}, u32[]{:S(2)}, u32[]{:S(2)}) async-start(bf16[32,48,512]{2,1,0:T(8,128)(2,1)} %bitcast.33), calls=%async_computation.4 | async-start | bytes 3145728 | tf_op jit(solution)/shard_map/all_to_all | solution.py:652
  382.8 21.3 %collective-permute-start.25 = (bf16[128,1536]{1,0:T(8,128)(2,1)}, bf16[128,1536]{1,0:T(8,128)(2,1)}, u32[]{:S(2)}, u32[]{:S(2)}) collective-permute-start(bf16[128,1536]{1,0:T(8,128)(2,1)} %get-tuple-element.174), channel_id=1, source_target_pairs={{0,16},{8,24},{16,0},{24,8},{32,48},{40,56},{48,32},{56,40},{64,80... | collective-permute-start | bytes 1179656 | tf_op jit(solution)/shard_map/ppermute | solution.py:69
  385.4 18.7 %collective-permute-start.24 = (bf16[128,1536]{1,0:T(8,128)(2,1)}, bf16[128,1536]{1,0:T(8,128)(2,1)}, u32[]{:S(2)}, u32[]{:S(2)}) collective-permute-start(bf16[128,1536]{1,0:T(8,128)(2,1)} %get-tuple-element.173), channel_id=1, source_target_pairs={{0,8},{8,16},{16,24},{24,0},{32,40},{40,48},{48,56},{56,32},{64,72... | collective-permute-start | bytes 1179656 | tf_op jit(solution)/shard_map/ppermute | solution.py:69
  385.7 18.4 %collective-permute-start.23 = (bf16[128,1536]{1,0:T(8,128)(2,1)}, bf16[128,1536]{1,0:T(8,128)(2,1)}, u32[]{:S(2)}, u32[]{:S(2)}) collective-permute-start(bf16[128,1536]{1,0:T(8,128)(2,1)} %get-tuple-element.172), channel_id=1, source_target_pairs={{0,24},{8,0},{16,8},{24,16},{32,56},{40,32},{48,40},{56,48},{64,88... | collective-permute-start | bytes 1179656 | tf_op jit(solution)/shard_map/ppermute | solution.py:69
  389.7 33.8 %all-to-all-start.5 = ((bf16[32,56,512]{2,1,0:T(8,128)(2,1)}), bf16[32,56,512]{2,1,0:T(8,128)(2,1)S(1)}, u32[]{:S(2)}, u32[]{:S(2)}) async-start(bf16[32,56,512]{2,1,0:T(8,128)(2,1)} %broadcast_in_dim.17), calls=%async_computation.5 | async-start | bytes 3670016 | tf_op jit(solution)/shard_map/all_to_all | solution.py:683
  (73 other events, 576.0 us)
Sparse Core Ops, SparseCore 0:
  11.2 70.8 all-gather.10
  84.6 68.2 all-gather.6
  154.7 50.4 all-gather.12
  253.9 49.2 all-gather.8
  305.6 73.4 reduce-scatter.1
